TPU v7x, 256 devices: a whole 4x4x8 slice. The times are simulated.
256 devices in a mesh: leaf: 64 (over z, y, core), sub: 4 (over x).
Axes of the slice: x: 4, y: 4, z: 8, core: 2. Of those that a mesh axis runs over, the one named last changes fastest.
Arguments:
- points: float32 [3, 1048576], P(None, ('leaf', 'sub')), may hold values from 0 to 2048, as said below
- vectors: float32 [32, 1048576], P(None, ('leaf', 'sub')), may hold values from -6 to 6
- counts: int32 [2048, 8], P(('leaf', 'sub')), may hold values from 1 to 64, 384 in all within a row
Outputs:
- product: float32 [32, 1048576], P(None, ('leaf', 'sub'))
Inputs may be any that keep to these rules, and one draw needn't show every extreme that they name: `points`: rows 0, 1, 2 are x, y, z. The slots of leaf l = 8 s + 4 cz + 2 cy + cx lie in its cell: x in [cx / 2, (cx + 1) / 2], y in [cy / 2, (cy + 1) / 2], z in [s + cz / 2, s + (cz + 1) / 2]. Leaf 8 s + c holds its points in its first counts[s, c] slots; later slots are empty. Each row sums to 384 and holds 64 at least once.
All inputs are finite; a program needn't handle non-finite values.
Results may differ from a plain program's by a relative error of at most 0.0003.
Values sent between devices are 32-bit elements; how exact they have to be, the bound alone decides.
No kernel may reach another device: no remote copies, remote signals or barrier semaphores. Data moves between devices by JAX's collectives and lax.ppermute only.
A program may use at most 128 MiB of HBM per device.

v0:
```python
import math

import jax
import jax.numpy as jnp
import numpy as np
from jax import lax
from jax.sharding import PartitionSpec as P

ORDER = 4


TERM_SCALE = 1.0 / 32.0
ROOT_THREE = math.sqrt(3.0)
far_offsets = (-3, -2, 2, 3)
far_sources = ((0, (0, 4, 5)), (1, (0, 1, 5)))


def padded_2(block, sides, width):
    for axis, dim in sides:
        count = lax.axis_size(axis)
        forward = [(i, i + 1) for i in range(count - 1)]
        backward = [(target, source) for source, target in forward]
        low = lax.ppermute(
            lax.slice_in_dim(block, block.shape[dim] - width, None, axis=dim), axis, forward
        )
        high = lax.ppermute(lax.slice_in_dim(block, 0, width, axis=dim), axis, backward)
        block = jnp.concatenate([low, block, high], axis=dim)
    return block


def from_behind(shard, axis, by):
    size = lax.axis_size(axis)
    pairs = [(i, i + by) for i in range(size) if 0 <= i + by < size]
    return lax.ppermute(shard, axis, pairs)


def swapped(value, axis, bit):
    mask = 2**bit
    pairs = [(source, source ^ mask) for source in range(lax.axis_size(axis))]
    return lax.ppermute(value, axis, pairs)


def term_lengths(slab_count):
    term_count = (slab_count.bit_length() - 1) // 3 + 1
    return [slab_count / 4.0 / 8.0**term_index for term_index in range(term_count)]


def chebyshev(order):
    return np.cos((2.0 * np.arange(order) + 1.0) * np.pi / (2.0 * order))


def lagrange_table(values, node_values):
    columns = []
    for anchor in range(len(node_values)):
        product = values * 0.0 + 1.0
        for against in range(len(node_values)):
            if against != anchor:
                product = (
                    product
                    * (values - node_values[against])
                    / (node_values[anchor] - node_values[against])
                )
        columns.append(product)
    return np.stack(columns, -1)


def lagrange_values(values, node_values):
    columns = []
    for anchor in range(len(node_values)):
        product = jnp.ones_like(values)
        for against in range(len(node_values)):
            if against != anchor:
                factor = 1.0 / float(node_values[anchor] - node_values[against])
                product = product * ((values - float(node_values[against])) * factor)
        columns.append(product)
    return jnp.stack(columns, -1)


def grid_nodes(node_values):
    number = len(node_values)
    along_z, along_y, along_x = np.meshgrid(
        np.arange(number), np.arange(number), np.arange(number), indexing="ij"
    )
    return np.stack(
        [node_values[along_x.ravel()], node_values[along_y.ravel()], node_values[along_z.ravel()]],
        -1,
    )


def kernel_table(targets, sources, lengths):
    offsets_xyz = targets[:, None, :] - sources[None, :, :]
    distance = np.sqrt(np.sum(offsets_xyz * offsets_xyz, -1))
    summed_terms = distance * 0.0
    for length in lengths:
        scaled = distance * (ROOT_THREE / length)
        summed_terms = summed_terms + TERM_SCALE / math.sqrt(length) * (1.0 + scaled) * np.exp(
            -scaled
        )
    return summed_terms


def kernel_values(squared, lengths):
    distance = jnp.sqrt(squared)
    summed_terms = jnp.zeros_like(distance)
    for length in lengths:
        scaled = distance * (ROOT_THREE / length)
        summed_terms = summed_terms + TERM_SCALE / math.sqrt(length) * (1.0 + scaled) * jnp.exp(
            -scaled
        )
    return summed_terms


def child_tables(node_values):
    halves = [
        lagrange_table(side_offset + 0.5 * node_values, node_values) for side_offset in (-0.5, 0.5)
    ]
    identity = np.eye(len(node_values))
    octant_rows = []
    for depth_index in range(2):
        for row_index in range(2):
            for column_index in range(2):
                octant_rows.append(
                    np.kron(np.kron(halves[depth_index], halves[row_index]), halves[column_index])
                )
    octant_array = np.stack(octant_rows).reshape((2, 2, 2) + octant_rows[0].shape)
    half_array = np.stack(
        [np.kron(np.kron(halves[half_index], identity), identity) for half_index in range(2)]
    )
    return (octant_array, half_array)


def leaf_coupling(node_values, depth_index, layer_index, lengths):
    scaled = grid_nodes(node_values) * 0.25
    targets = []
    sources = []
    for row_index in range(2):
        for column_index in range(2):
            targets.append(
                scaled
                + np.array(
                    [(column_index + 0.5) * 0.5, (row_index + 0.5) * 0.5, (depth_index + 0.5) * 0.5]
                )
            )
            sources.append(
                scaled
                + np.array(
                    [(column_index + 0.5) * 0.5, (row_index + 0.5) * 0.5, (layer_index - 1.5) * 0.5]
                )
            )
    return kernel_table(np.concatenate(targets), np.concatenate(sources), lengths)


def coarse_couplings(node_values, height, lengths):
    span = float(1 << height)
    targets = grid_nodes(node_values) * np.array([0.5, 0.5, 0.5 * span])
    return np.stack(
        [
            kernel_table(targets, targets + np.array([0.0, 0.0, offset * span]), lengths)
            for offset in far_offsets
        ]
    )


def basis_of(coords, first_slab, node_values):
    layer_ids = jnp.arange(coords.shape[1])
    slab_of = (first_slab + layer_ids // 2).astype(coords.dtype)
    depth_centre = ((layer_ids % 2).astype(coords.dtype) + 0.5) * 0.5
    centre = (jnp.arange(2).astype(coords.dtype) + 0.5) * 0.5
    along_width = (coords[0] - centre[None, None, :, None]) * 4.0
    along_height = (coords[1] - centre[None, :, None, None]) * 4.0
    along_depth = (
        coords[2] - slab_of[:, None, None, None] - depth_centre[:, None, None, None]
    ) * 4.0
    poly_width = lagrange_values(along_width, node_values)
    poly_height = lagrange_values(along_height, node_values)
    poly_depth = lagrange_values(along_depth, node_values)
    combined = (
        poly_depth[..., :, None, None]
        * poly_height[..., None, :, None]
        * poly_width[..., None, None, :]
    )
    return combined.reshape(combined.shape[:4] + (-1,))


def near_field(window, targets, lengths):
    layer_count = targets.shape[1]
    padded = jnp.pad(window, ((0, 0), (0, 0), (1, 1), (1, 1), (0, 0)))
    summed = jnp.zeros((window.shape[0] - 3,) + targets.shape[1:], window.dtype)
    for step_depth in (-1, 0, 1):
        for step_height in (-1, 0, 1):
            for step_width in (-1, 0, 1):
                source = padded[
                    :,
                    1 + step_depth : 1 + step_depth + layer_count,
                    1 + step_height : 3 + step_height,
                    1 + step_width : 3 + step_width,
                ]
                squared = (
                    (targets[0][..., :, None] - source[0][..., None, :]) ** 2
                    + (targets[1][..., :, None] - source[1][..., None, :]) ** 2
                    + (targets[2][..., :, None] - source[2][..., None, :]) ** 2
                )
                weights = kernel_values(squared, lengths)
                summed = summed + jnp.einsum(
                    "zyxij,vzyxj->vzyxi", weights, source[3:], precision=lax.Precision.HIGHEST
                )
    return summed


def leaf_far(window, node_values, lengths):
    pair_count = (window.shape[0] - 4) // 2
    rank_count = window.shape[3]
    vector_count = window.shape[4]
    stacked = []
    for depth_index, layer_list in far_sources:
        summed = jnp.zeros((pair_count, 4 * rank_count, vector_count), window.dtype)
        for layer_index in layer_list:
            coupling = jnp.asarray(
                leaf_coupling(node_values, depth_index, layer_index, lengths), jnp.float32
            )
            source = window[layer_index : layer_index + 2 * pair_count : 2].reshape(
                pair_count, 4 * rank_count, vector_count
            )
            summed = summed + jnp.einsum(
                "mn,jnv->jmv", coupling, source, precision=lax.Precision.HIGHEST
            )
        stacked.append(summed.reshape(pair_count, 2, 2, rank_count, vector_count))
    return jnp.stack(stacked, 1).reshape(2 * pair_count, 2, 2, rank_count, vector_count)


def upward(leaf_bases, masked):
    return jnp.einsum("zyxpr,vzyxp->zyxrv", leaf_bases, masked, precision=lax.Precision.HIGHEST)


def lift_pair(coeffs, partner, is_even, half_tables):
    lower_half = jnp.where(is_even, coeffs, partner)
    upper_half = jnp.where(is_even, partner, coeffs)
    lower_term = jnp.dot(half_tables[0].T, lower_half, precision=lax.Precision.HIGHEST)
    return lower_term + jnp.dot(half_tables[1].T, upper_half, precision=lax.Precision.HIGHEST)


def local(points, vectors, counts):
    cube_count = counts.shape[0]
    leaf_points = points.shape[1] // (8 * cube_count)
    layer_count = 2 * cube_count
    vector_count = vectors.shape[0]
    own_index = lax.axis_index(("leaf", "sub"))
    slab_count = cube_count * lax.axis_size(("leaf", "sub"))
    level_count = slab_count.bit_length() - 2
    cube_levels = cube_count.bit_length() - 1
    lengths = term_lengths(slab_count)
    first_slab = own_index * cube_count
    node_values = chebyshev(ORDER)
    octant_array, half_array = child_tables(node_values)
    octants = jnp.asarray(octant_array, jnp.float32)
    half_tables = jnp.asarray(half_array, jnp.float32)
    coords = points.reshape(3, layer_count, 2, 2, leaf_points)
    occupied = (
        (jnp.arange(leaf_points)[None, :] < counts.reshape(-1, 1))
        .astype(jnp.float32)
        .reshape(layer_count, 2, 2, leaf_points)
    )
    masked = vectors.reshape(vector_count, layer_count, 2, 2, leaf_points) * occupied
    record = jnp.concatenate([coords, masked], 0)
    near_window = padded_2(record, ((("leaf", "sub"), 1),), 1)
    leaf_bases = basis_of(coords, first_slab, node_values)
    leaf_coeffs = upward(leaf_bases, masked)
    coeff_window = padded_2(leaf_coeffs, ((("leaf", "sub"), 0),), 2)
    near_term = near_field(near_window, coords, lengths)
    rank_count = leaf_coeffs.shape[3]
    coeffs = jnp.einsum(
        "abcmn,sabcmv->snv",
        octants,
        leaf_coeffs.reshape(cube_count, 2, 2, 2, rank_count, vector_count),
        precision=lax.Precision.HIGHEST,
    )
    far_terms = []
    for height in range(cube_levels):
        box_count = coeffs.shape[0]
        couplings = jnp.asarray(coarse_couplings(node_values, height, lengths), jnp.float32)
        rimmed = padded_2(coeffs, ((("leaf", "sub"), 0),), 2)
        padded = jnp.pad(rimmed, ((1, 1), (0, 0), (0, 0)))
        parity = (jnp.arange(box_count) % 2 == 0)[:, None, None]
        summed = jnp.zeros_like(coeffs)
        for position, offset in enumerate(far_offsets):
            source = padded[3 + offset : 3 + offset + box_count]
            contribution = jnp.einsum(
                "mn,inv->imv", couplings[position], source, precision=lax.Precision.HIGHEST
            )
            if offset == 3:
                contribution = jnp.where(parity, contribution, 0.0)
            if offset == -3:
                contribution = jnp.where(parity, 0.0, contribution)
            summed = summed + contribution
        far_terms.append(summed)
        paired = coeffs.reshape(box_count // 2, 2, rank_count, vector_count)
        coeffs = jnp.einsum("cmn,icmv->inv", half_tables, paired, precision=lax.Precision.HIGHEST)
    coeffs = coeffs[0]
    for height in range(cube_levels, level_count):
        bit_number = height - cube_levels
        stride = 1 << bit_number
        box_index = own_index // stride
        is_even = box_index % 2 == 0
        couplings = jnp.asarray(coarse_couplings(node_values, height, lengths), jnp.float32)
        summed = jnp.zeros_like(coeffs)
        for position, offset in enumerate(far_offsets):
            source = from_behind(coeffs, ("leaf", "sub"), -offset * stride)
            contribution = jnp.dot(couplings[position], source, precision=lax.Precision.HIGHEST)
            if offset == 3:
                contribution = jnp.where(is_even, contribution, 0.0)
            if offset == -3:
                contribution = jnp.where(is_even, 0.0, contribution)
            summed = summed + contribution
        if height + 1 < level_count:
            partner = swapped(coeffs, ("leaf", "sub"), bit_number)
            coeffs = lift_pair(coeffs, partner, is_even, half_tables)
        far_terms.append(summed)
    local_exp = far_terms[level_count - 1]
    for height in range(level_count - 2, cube_levels - 1, -1):
        is_even = own_index // (1 << height - cube_levels) % 2 == 0
        transfer = jnp.where(is_even, half_tables[0], half_tables[1])
        local_exp = far_terms[height] + jnp.dot(
            transfer, local_exp, precision=lax.Precision.HIGHEST
        )
    local_exp = local_exp[None]
    for height in range(cube_levels - 1, -1, -1):
        children = jnp.einsum(
            "cmn,inv->icmv", half_tables, local_exp, precision=lax.Precision.HIGHEST
        )
        local_exp = far_terms[height] + children.reshape(-1, rank_count, vector_count)
    inherited = jnp.einsum(
        "abcmn,snv->sabcmv", octants, local_exp, precision=lax.Precision.HIGHEST
    ).reshape(layer_count, 2, 2, rank_count, vector_count)
    leaf_local = inherited + leaf_far(coeff_window, node_values, lengths)
    result = (
        jnp.einsum("zyxpr,zyxrv->vzyxp", leaf_bases, leaf_local, precision=lax.Precision.HIGHEST)
        + near_term
    )
    return (result * occupied).reshape(vector_count, -1)


def solution(mesh):
    in_specs = (P(None, ("leaf", "sub")), P(None, ("leaf", "sub")), P(("leaf", "sub"), None))
    out_specs = P(None, ("leaf", "sub"))
    return jax.shard_map(local, mesh=mesh, in_specs=in_specs, out_specs=out_specs, check_vma=False)
```

profile of v0, /device:TPU:192, one launch (start us, length us, event | category | flops | bytes accessed | tf_op | source)
XLA Modules:
  0.0 584.4 jit_solution(17893752591429235091)
XLA Ops:
  0.9 2.8 reshape.544
  16.3 3.4 collective-permute-start.4
  19.7 6.4 %collective-permute-start.5 = (f32[2,64,32]{1,2,0:T(8,128)S(1)}, f32[2,64,32]{1,2,0:T(8,128)S(1)}, u32[]{:S(2)}, u32[]{:S(2)}) collective-permute-start(f32[2,64,32]{1,2,0:T(8,128)S(1)} %convolution_bitcast_fusion.3), channel_id=1, source_target_pairs={{1,0},{2,1},{3,2},{4,3},{5,4},{6,5},{7,6},{8,7},{9,8},{10,9},{11,1... | collective-permute-start | bytes 49160 | tf_op jit(solution)/shard_map/ppermute | solution.py:26
  26.9 3.1 collective-permute-start.9
  30.0 3.3 collective-permute-start.7
  35.8 7.7 %fusion.484 = f32[16,2,2,32,64]{4,3,2,1,0:T(8,128)} fusion(f32[32,16,2,2,64]{4,0,3,2,1:T(8,128)S(1)} %copy_multiply_fusion, f32[16,2,2,64]{3,2,1,0:T(2,128)S(1)} %sub.1294, f32[16,2,2,64]{3,2,1,0:T(2,128)S(1)} %sub.1289, f32[16,2,2,64]{3,2,1,0:T(2,128)S(1)} %sub.1284), kind=kOutput, calls=%fused_computation.491 | convolution fusion | flops 108789760 | bytes 1097728 | tf_op jit(solution)/shard_map/zyxij,vzyxj->vzyxi/dot_general | solution.py:204
  43.8 6.7 %collective-permute-start.8 = (f32[64,32]{0,1:T(8,128)}, f32[64,32]{0,1:T(8,128)S(1)}, u32[]{:S(2)}, u32[]{:S(2)}) collective-permute-start(f32[64,32]{0,1:T(8,128)} %convolution_bitcast_fusion.4), channel_id=1, source_target_pairs={{2,0},{3,1},{4,2},{5,3},{6,4},{7,5},{8,6},{9,7},{10,8},{11,9},{12,... | collective-permute-start | bytes 24584 | tf_op jit(solution)/shard_map/ppermute | solution.py:34
  61.2 6.7 %collective-permute-done = f32[2,64,32]{1,2,0:T(8,128)S(1)} collective-permute-done((f32[2,64,32]{1,2,0:T(8,128)S(1)}, f32[2,64,32]{1,2,0:T(8,128)S(1)}, u32[]{:S(2)}, u32[]{:S(2)}) %collective-permute-start) | collective-permute-done | bytes 16416 | tf_op jit(solution)/shard_map/ppermute | solution.py:23
  77.5 5.7 collective-permute-done.2
  90.7 3.8 collective-permute-done.15
  94.5 4.8 collective-permute-start.43
  106.8 3.1 collective-permute-done.14
  112.5 4.7 collective-permute-done.12
  120.7 21.8 %collective-permute-start.20 = (f32[64,32]{0,1:T(8,128)S(1)}, f32[64,32]{0,1:T(8,128)S(1)}, u32[]{:S(2)}, u32[]{:S(2)}) collective-permute-start(f32[64,32]{0,1:T(8,128)S(1)} %fusion.1167), channel_id=1, source_target_pairs={{0,4},{1,5},{2,6},{3,7},{4,0},{5,1},{6,2},{7,3},{8,12},{9,13},{10,... | collective-permute-start | bytes 24584 | tf_op jit(solution)/shard_map/ppermute | solution.py:40
  143.4 5.6 collective-permute-start.19
  153.7 4.4 collective-permute-done.17
  158.1 3.4 collective-permute-start.18
  163.7 11.8 %collective-permute-start.25 = (f32[64,32]{0,1:T(8,128)S(1)}, f32[64,32]{0,1:T(8,128)S(1)}, u32[]{:S(2)}, u32[]{:S(2)}) collective-permute-start(f32[64,32]{0,1:T(8,128)S(1)} %fusion.1161), channel_id=1, source_target_pairs={{0,8},{1,9},{2,10},{3,11},{4,12},{5,13},{6,14},{7,15},{8,0},{9,1},... | collective-permute-start | bytes 24584 | tf_op jit(solution)/shard_map/ppermute | solution.py:40
  178.8 3.0 collective-permute-start.24
  182.1 3.5 collective-permute-done.24
  185.6 4.4 collective-permute-start.22
  190.8 2.8 collective-permute-done.22
  193.6 4.1 collective-permute-start.23
  205.4 15.3 %collective-permute-start.30 = (f32[64,32]{0,1:T(8,128)S(1)}, f32[64,32]{0,1:T(8,128)S(1)}, u32[]{:S(2)}, u32[]{:S(2)}) collective-permute-start(f32[64,32]{0,1:T(8,128)S(1)} %fusion.1155), channel_id=1, source_target_pairs={{0,16},{1,17},{2,18},{3,19},{4,20},{5,21},{6,22},{7,23},{8,24},{9,... | collective-permute-start | bytes 24584 | tf_op jit(solution)/shard_map/ppermute | solution.py:40
  226.2 7.9 %fusion.743 = f32[16,2,2,32,64]{4,3,2,1,0:T(8,128)S(1)} fusion(f32[35,18,4,4,64]{4,0,3,2,1:T(8,128)S(1)} %select_maximum_fusion, f32[16,2,2,64]{3,2,1,0:T(2,128)S(1)} %bitcast.482, f32[16,2,2,64]{3,2,1,0:T(2,128)S(1)} %bitcast.483, f32[16,2,2,64]{3,2,1,0:T(2,128)S(1)} %bitcast.484, f32[16,2,2,64]{3,2,1,0:T(2,128)S(1)} %sub.1294, ...), kind=kOutput, calls=%fused_computation.750 | convolution fusion | flops 108789760 | bytes 1769472 | tf_op jit(solution)/shard_map/zyxij,vzyxj->vzyxi/dot_general | solution.py:204
  234.1 7.9 %fusion.706 = f32[16,2,2,32,64]{4,3,2,1,0:T(8,128)S(1)} fusion(f32[35,18,4,4,64]{4,0,3,2,1:T(8,128)S(1)} %select_maximum_fusion, f32[16,2,2,64]{3,2,1,0:T(2,128)S(1)} %bitcast.479, f32[16,2,2,64]{3,2,1,0:T(2,128)S(1)} %bitcast.480, f32[16,2,2,64]{3,2,1,0:T(2,128)S(1)} %bitcast.481, f32[16,2,2,64]{3,2,1,0:T(2,128)S(1)} %sub.1294, ...), kind=kOutput, calls=%fused_computation.713 | convolution fusion | flops 108789760 | bytes 1769472 | tf_op jit(solution)/shard_map/zyxij,vzyxj->vzyxi/dot_general | solution.py:204
  242.0 7.9 %fusion.669 = f32[16,2,2,32,64]{4,3,2,1,0:T(8,128)S(1)} fusion(f32[35,18,4,4,64]{4,0,3,2,1:T(8,128)S(1)} %select_maximum_fusion, f32[16,2,2,64]{3,2,1,0:T(2,128)S(1)} %bitcast.476, f32[16,2,2,64]{3,2,1,0:T(2,128)S(1)} %bitcast.477, f32[16,2,2,64]{3,2,1,0:T(2,128)S(1)} %bitcast.478, f32[16,2,2,64]{3,2,1,0:T(2,128)S(1)} %sub.1294, ...), kind=kOutput, calls=%fused_computation.676 | convolution fusion | flops 108789760 | bytes 1769472 | tf_op jit(solution)/shard_map/zyxij,vzyxj->vzyxi/dot_general | solution.py:204
  249.9 7.9 %fusion.632 = f32[16,2,2,32,64]{4,3,2,1,0:T(8,128)S(1)} fusion(f32[35,18,4,4,64]{4,0,3,2,1:T(8,128)S(1)} %select_maximum_fusion, f32[16,2,2,64]{3,2,1,0:T(2,128)S(1)} %bitcast.473, f32[16,2,2,64]{3,2,1,0:T(2,128)S(1)} %bitcast.474, f32[16,2,2,64]{3,2,1,0:T(2,128)S(1)} %bitcast.475, f32[16,2,2,64]{3,2,1,0:T(2,128)S(1)} %sub.1294, ...), kind=kOutput, calls=%fused_computation.639 | convolution fusion | flops 108789760 | bytes 1769472 | tf_op jit(solution)/shard_map/zyxij,vzyxj->vzyxi/dot_general | solution.py:204
  257.8 7.9 %fusion.595 = f32[16,2,2,32,64]{4,3,2,1,0:T(8,128)S(1)} fusion(f32[35,18,4,4,64]{4,0,3,2,1:T(8,128)S(1)} %select_maximum_fusion, f32[16,2,2,64]{3,2,1,0:T(2,128)S(1)} %bitcast.467, f32[16,2,2,64]{3,2,1,0:T(2,128)S(1)} %bitcast.468, f32[16,2,2,64]{3,2,1,0:T(2,128)S(1)} %bitcast.469, f32[16,2,2,64]{3,2,1,0:T(2,128)S(1)} %sub.1294, ...), kind=kOutput, calls=%fused_computation.602 | convolution fusion | flops 108789760 | bytes 1769472 | tf_op jit(solution)/shard_map/zyxij,vzyxj->vzyxi/dot_general | solution.py:204
  265.7 7.9 %fusion.558 = f32[16,2,2,32,64]{4,3,2,1,0:T(8,128)S(1)} fusion(f32[35,18,4,4,64]{4,0,3,2,1:T(8,128)S(1)} %select_maximum_fusion, f32[16,2,2,64]{3,2,1,0:T(2,128)S(1)} %bitcast.464, f32[16,2,2,64]{3,2,1,0:T(2,128)S(1)} %bitcast.465, f32[16,2,2,64]{3,2,1,0:T(2,128)S(1)} %bitcast.466, f32[16,2,2,64]{3,2,1,0:T(2,128)S(1)} %sub.1294, ...), kind=kOutput, calls=%fused_computation.565 | convolution fusion | flops 108789760 | bytes 1769472 | tf_op jit(solution)/shard_map/zyxij,vzyxj->vzyxi/dot_general | solution.py:204
  273.6 7.9 %fusion.521 = f32[16,2,2,32,64]{4,3,2,1,0:T(8,128)S(1)} fusion(f32[35,18,4,4,64]{4,0,3,2,1:T(8,128)S(1)} %select_maximum_fusion, f32[16,2,2,64]{3,2,1,0:T(2,128)S(1)} %bitcast.470, f32[16,2,2,64]{3,2,1,0:T(2,128)S(1)} %bitcast.471, f32[16,2,2,64]{3,2,1,0:T(2,128)S(1)} %bitcast.472, f32[16,2,2,64]{3,2,1,0:T(2,128)S(1)} %sub.1294, ...), kind=kOutput, calls=%fused_computation.528 | convolution fusion | flops 108789760 | bytes 1769472 | tf_op jit(solution)/shard_map/zyxij,vzyxj->vzyxi/dot_general | solution.py:204
  281.4 7.9 %fusion.780 = f32[16,2,2,32,64]{4,3,2,1,0:T(8,128)S(1)} fusion(f32[35,18,4,4,64]{4,0,3,2,1:T(8,128)S(1)} %select_maximum_fusion, f32[16,2,2,64]{3,2,1,0:T(2,128)S(1)} %bitcast.494, f32[16,2,2,64]{3,2,1,0:T(2,128)S(1)} %bitcast.495, f32[16,2,2,64]{3,2,1,0:T(2,128)S(1)} %bitcast.496, f32[16,2,2,64]{3,2,1,0:T(2,128)S(1)} %sub.1294, ...), kind=kOutput, calls=%fused_computation.787 | convolution fusion | flops 108789760 | bytes 1769472 | tf_op jit(solution)/shard_map/zyxij,vzyxj->vzyxi/dot_general | solution.py:204
  289.3 7.9 %fusion.854 = f32[16,2,2,32,64]{4,3,2,1,0:T(8,128)S(1)} fusion(f32[35,18,4,4,64]{4,0,3,2,1:T(8,128)S(1)} %select_maximum_fusion, f32[16,2,2,64]{3,2,1,0:T(2,128)S(1)} %bitcast.491, f32[16,2,2,64]{3,2,1,0:T(2,128)S(1)} %bitcast.492, f32[16,2,2,64]{3,2,1,0:T(2,128)S(1)} %bitcast.493, f32[16,2,2,64]{3,2,1,0:T(2,128)S(1)} %sub.1294, ...), kind=kOutput, calls=%fused_computation.861 | convolution fusion | flops 108789760 | bytes 1769472 | tf_op jit(solution)/shard_map/zyxij,vzyxj->vzyxi/dot_general | solution.py:204
  297.2 7.9 %fusion.891 = f32[16,2,2,32,64]{4,3,2,1,0:T(8,128)S(1)} fusion(f32[35,18,4,4,64]{4,0,3,2,1:T(8,128)S(1)} %select_maximum_fusion, f32[16,2,2,64]{3,2,1,0:T(2,128)S(1)} %bitcast.488, f32[16,2,2,64]{3,2,1,0:T(2,128)S(1)} %bitcast.489, f32[16,2,2,64]{3,2,1,0:T(2,128)S(1)} %bitcast.490, f32[16,2,2,64]{3,2,1,0:T(2,128)S(1)} %sub.1294, ...), kind=kOutput, calls=%fused_computation.898 | convolution fusion | flops 108789760 | bytes 1769472 | tf_op jit(solution)/shard_map/zyxij,vzyxj->vzyxi/dot_general | solution.py:204
  305.1 7.9 %fusion.928 = f32[16,2,2,32,64]{4,3,2,1,0:T(8,128)S(1)} fusion(f32[35,18,4,4,64]{4,0,3,2,1:T(8,128)S(1)} %select_maximum_fusion, f32[16,2,2,64]{3,2,1,0:T(2,128)S(1)} %bitcast.485, f32[16,2,2,64]{3,2,1,0:T(2,128)S(1)} %bitcast.486, f32[16,2,2,64]{3,2,1,0:T(2,128)S(1)} %bitcast.487, f32[16,2,2,64]{3,2,1,0:T(2,128)S(1)} %sub.1294, ...), kind=kOutput, calls=%fused_computation.935 | convolution fusion | flops 108789760 | bytes 1769472 | tf_op jit(solution)/shard_map/zyxij,vzyxj->vzyxi/dot_general | solution.py:204
  313.0 8.0 %fusion.410 = f32[16,2,2,32,64]{4,3,2,1,0:T(8,128)} fusion(f32[35,18,4,4,64]{4,0,3,2,1:T(8,128)S(1)} %select_maximum_fusion, f32[16,2,2,64]{3,2,1,0:T(2,128)S(1)} %bitcast.443, f32[16,2,2,64]{3,2,1,0:T(2,128)S(1)} %bitcast.444, f32[16,2,2,64]{3,2,1,0:T(2,128)S(1)} %bitcast.445, f32[16,2,2,64]{3,2,1,0:T(2,128)S(1)} %sub.1294, ...), kind=kOutput, calls=%fused_computation.417 | convolution fusion | flops 108789760 | bytes 1769472 | tf_op jit(solution)/shard_map/zyxij,vzyxj->vzyxi/dot_general | solution.py:204
  321.0 7.8 %fusion.373 = f32[16,2,2,32,64]{4,3,2,1,0:T(8,128)} fusion(f32[35,18,4,4,64]{4,0,3,2,1:T(8,128)S(1)} %select_maximum_fusion, f32[16,2,2,64]{3,2,1,0:T(2,128)S(1)} %bitcast.440, f32[16,2,2,64]{3,2,1,0:T(2,128)S(1)} %bitcast.441, f32[16,2,2,64]{3,2,1,0:T(2,128)S(1)} %bitcast.442, f32[16,2,2,64]{3,2,1,0:T(2,128)S(1)} %sub.1294, ...), kind=kOutput, calls=%fused_computation.380 | convolution fusion | flops 108789760 | bytes 1769472 | tf_op jit(solution)/shard_map/zyxij,vzyxj->vzyxi/dot_general | solution.py:204
  328.8 7.8 %fusion.1003 = f32[32,16,2,2,64]{4,0,3,2,1:T(8,128)} fusion(f32[35,18,4,4,64]{4,0,3,2,1:T(8,128)S(1)} %select_maximum_fusion, f32[16,2,2,64]{3,2,1,0:T(2,128)S(1)} %bitcast.437, f32[16,2,2,64]{3,2,1,0:T(2,128)S(1)} %bitcast.438, f32[16,2,2,64]{3,2,1,0:T(2,128)S(1)} %bitcast.439, f32[16,2,2,64]{3,2,1,0:T(2,128)S(1)} %sub.1294, ...), kind=kOutput, calls=%fused_computation.1014 | convolution fusion | flops 108789760 | bytes 1769472 | tf_op jit(solution)/shard_map/zyxij,vzyxj->vzyxi/dot_general | solution.py:204
  336.5 7.8 %fusion.1006 = f32[32,16,2,2,64]{4,0,3,2,1:T(8,128)} fusion(f32[35,18,4,4,64]{4,0,3,2,1:T(8,128)S(1)} %select_maximum_fusion, f32[16,2,2,64]{3,2,1,0:T(2,128)S(1)} %bitcast.434, f32[16,2,2,64]{3,2,1,0:T(2,128)S(1)} %bitcast.435, f32[16,2,2,64]{3,2,1,0:T(2,128)S(1)} %bitcast.436, f32[16,2,2,64]{3,2,1,0:T(2,128)S(1)} %sub.1294, ...), kind=kOutput, calls=%fused_computation.1015 | convolution fusion | flops 108789760 | bytes 1769472 | tf_op jit(solution)/shard_map/zyxij,vzyxj->vzyxi/dot_general | solution.py:204
  344.3 8.6 %fusion.1009 = f32[32,16,2,2,64]{4,0,3,2,1:T(8,128)} fusion(f32[35,18,4,4,64]{4,0,3,2,1:T(8,128)} %copy-done.2, f32[16,2,2,64]{3,2,1,0:T(2,128)S(1)} %bitcast.463, f32[16,2,2,64]{3,2,1,0:T(2,128)S(1)} %bitcast.432, f32[16,2,2,64]{3,2,1,0:T(2,128)S(1)} %bitcast.433, f32[16,2,2,64]{3,2,1,0:T(2,128)S(1)} %sub.1294, f32[16,2,2,64]{3,2,1,0:T(2,128)S(1)} %sub.1289, ...), kind=kOutput, calls=%fused_computation.1016 | convolution fusion | flops 108789760 | bytes 1671168 | tf_op jit(solution)/shard_map/zyxij,vzyxj->vzyxi/dot_general | solution.py:204
  353.0 9.0 %fusion.1012 = f32[32,16,2,2,64]{4,0,3,2,1:T(8,128)} fusion(f32[35,18,4,4,64]{4,0,3,2,1:T(8,128)} %copy-done.2, f32[16,2,2,64]{3,2,1,0:T(2,128)S(1)} %bitcast.460, f32[16,2,2,64]{3,2,1,0:T(2,128)S(1)} %bitcast.461, f32[16,2,2,64]{3,2,1,0:T(2,128)S(1)} %bitcast.462, f32[16,2,2,64]{3,2,1,0:T(2,128)S(1)} %sub.1294, f32[16,2,2,64]{3,2,1,0:T(2,128)S(1)} %sub.1289, ...), kind=kOutput, calls=%fused_computation.1017 | convolution fusion | flops 108789760 | bytes 1671168 | tf_op jit(solution)/shard_map/zyxij,vzyxj->vzyxi/dot_general | solution.py:204
  362.0 8.6 %fusion.1015 = f32[32,16,2,2,64]{4,0,3,2,1:T(8,128)} fusion(f32[35,18,4,4,64]{4,0,3,2,1:T(8,128)} %copy-done.2, f32[16,2,2,64]{3,2,1,0:T(2,128)S(1)} %bitcast.457, f32[16,2,2,64]{3,2,1,0:T(2,128)S(1)} %bitcast.458, f32[16,2,2,64]{3,2,1,0:T(2,128)S(1)} %bitcast.459, f32[16,2,2,64]{3,2,1,0:T(2,128)S(1)} %sub.1294, f32[16,2,2,64]{3,2,1,0:T(2,128)S(1)} %sub.1289, ...), kind=kOutput, calls=%fused_computation.1018 | convolution fusion | flops 108789760 | bytes 1671168 | tf_op jit(solution)/shard_map/zyxij,vzyxj->vzyxi/dot_general | solution.py:204
  370.7 8.6 %fusion.1021 = f32[32,16,2,2,64]{4,0,3,2,1:T(8,128)} fusion(f32[35,18,4,4,64]{4,0,3,2,1:T(8,128)} %copy-done.2, f32[16,2,2,64]{3,2,1,0:T(2,128)S(1)} %bitcast.454, f32[16,2,2,64]{3,2,1,0:T(2,128)S(1)} %bitcast.455, f32[16,2,2,64]{3,2,1,0:T(2,128)S(1)} %bitcast.456, f32[16,2,2,64]{3,2,1,0:T(2,128)S(1)} %sub.1294, f32[16,2,2,64]{3,2,1,0:T(2,128)S(1)} %sub.1289, ...), kind=kOutput, calls=%fused_computation.1020 | convolution fusion | flops 108789760 | bytes 1671168 | tf_op jit(solution)/shard_map/zyxij,vzyxj->vzyxi/dot_general | solution.py:204
  379.3 8.8 %fusion.1024 = f32[32,16,2,2,64]{4,0,3,2,1:T(8,128)} fusion(f32[35,18,4,4,64]{4,0,3,2,1:T(8,128)} %copy-done.2, f32[16,2,2,64]{3,2,1,0:T(2,128)S(1)} %bitcast.451, f32[16,2,2,64]{3,2,1,0:T(2,128)S(1)} %bitcast.452, f32[16,2,2,64]{3,2,1,0:T(2,128)S(1)} %bitcast.453, f32[16,2,2,64]{3,2,1,0:T(2,128)S(1)} %sub.1294, f32[16,2,2,64]{3,2,1,0:T(2,128)S(1)} %sub.1289, ...), kind=kOutput, calls=%fused_computation.1021 | convolution fusion | flops 108789760 | bytes 1671168 | tf_op jit(solution)/shard_map/zyxij,vzyxj->vzyxi/dot_general | solution.py:204
  388.1 8.6 %fusion.1027 = f32[32,16,2,2,64]{4,0,3,2,1:T(8,128)} fusion(f32[35,18,4,4,64]{4,0,3,2,1:T(8,128)} %copy-done.2, f32[16,2,2,64]{3,2,1,0:T(2,128)S(1)} %bitcast.448, f32[16,2,2,64]{3,2,1,0:T(2,128)S(1)} %bitcast.449, f32[16,2,2,64]{3,2,1,0:T(2,128)S(1)} %bitcast.450, f32[16,2,2,64]{3,2,1,0:T(2,128)S(1)} %sub.1294, f32[16,2,2,64]{3,2,1,0:T(2,128)S(1)} %sub.1289, ...), kind=kOutput, calls=%fused_computation.1022 | convolution fusion | flops 108789760 | bytes 1671168 | tf_op jit(solution)/shard_map/zyxij,vzyxj->vzyxi/dot_general | solution.py:204
  396.7 8.6 %fusion.1030 = f32[32,16,2,2,64]{4,0,3,2,1:T(8,128)} fusion(f32[35,18,4,4,64]{4,0,3,2,1:T(8,128)} %copy-done.2, f32[16,2,2,64]{3,2,1,0:T(2,128)S(1)} %bitcast.431, f32[16,2,2,64]{3,2,1,0:T(2,128)S(1)} %bitcast.446, f32[16,2,2,64]{3,2,1,0:T(2,128)S(1)} %bitcast.447, f32[16,2,2,64]{3,2,1,0:T(2,128)S(1)} %sub.1294, f32[16,2,2,64]{3,2,1,0:T(2,128)S(1)} %sub.1289, ...), kind=kOutput, calls=%fused_computation.1023 | convolution fusion | flops 108789760 | bytes 1671168 | tf_op jit(solution)/shard_map/zyxij,vzyxj->vzyxi/dot_general | solution.py:204
  405.8 7.9 %fusion.817 = f32[16,2,2,32,64]{4,3,2,1,0:T(8,128)S(1)} fusion(f32[35,17,2,2,64]{4,0,3,2,1:T(8,128)S(1)} %get-tuple-element.93, f32[16,2,2,64]{3,2,1,0:T(2,128)S(1)} %bitcast.502, f32[16,2,2,64]{3,2,1,0:T(2,128)S(1)} %bitcast.501, f32[16,2,2,64]{3,2,1,0:T(2,128)S(1)} %bitcast.500, f32[16,2,2,64]{3,2,1,0:T(2,128)S(1)} %sub.1294, ...), kind=kOutput, calls=%fused_computation.824 | convolution fusion | flops 108789760 | bytes 1769472 | tf_op jit(solution)/shard_map/zyxij,vzyxj->vzyxi/dot_general | solution.py:204
  413.7 9.4 %fusion.1108 = f32[16,2,2,32,64]{4,3,2,1,0:T(8,128)} fusion(f32[16,2,2,32,64]{4,3,2,1,0:T(8,128)S(1)} %copy-done.109, f32[16,2,2,32,64]{4,3,2,1,0:T(8,128)S(1)} %fusion.521, f32[16,2,2,32,64]{4,3,2,1,0:T(8,128)S(1)} %fusion.558, f32[16,2,2,32,64]{4,3,2,1,0:T(8,128)S(1)} %fusion.595, f32[16,2,2,32,64]{4,3,2,1,0:T(8,128)S(1)} %fusion.632, ...), kind=kOutput, calls=%fused_computation.1049 | convolution fusion | flops 110493696 | bytes 8486912 | tf_op jit(solution)/shard_map/zyxij,vzyxj->vzyxi/dot_general | solution.py:204
  423.2 7.8 %fusion.1018 = f32[32,16,2,2,64]{4,0,3,2,1:T(8,128)} fusion(f32[35,17,2,2,64]{4,0,3,2,1:T(8,128)S(1)} %get-tuple-element.94, f32[16,2,2,64]{3,2,1,0:T(2,128)S(1)} %bitcast.497, f32[16,2,2,64]{3,2,1,0:T(2,128)S(1)} %bitcast.498, f32[16,2,2,64]{3,2,1,0:T(2,128)S(1)} %bitcast.499, f32[16,2,2,64]{3,2,1,0:T(2,128)S(1)} %sub.1294, ...), kind=kOutput, calls=%fused_computation.1019 | convolution fusion | flops 108789760 | bytes 1769472 | tf_op jit(solution)/shard_map/zyxij,vzyxj->vzyxi/dot_general | solution.py:204
  431.3 6.4 %collective-permute-start.29 = (f32[64,32]{0,1:T(8,128)S(1)}, f32[64,32]{0,1:T(8,128)S(1)}, u32[]{:S(2)}, u32[]{:S(2)}) collective-permute-start(f32[64,32]{0,1:T(8,128)S(1)} %fusion.1155), channel_id=1, source_target_pairs={{48,0},{49,1},{50,2},{51,3},{52,4},{53,5},{54,6},{55,7},{56,8},{57... | collective-permute-start | bytes 24584 | tf_op jit(solution)/shard_map/ppermute | solution.py:34
  445.2 3.1 collective-permute-start.28
  450.8 13.9 %collective-permute-start.35 = (f32[64,32]{0,1:T(8,128)S(1)}, f32[64,32]{0,1:T(8,128)S(1)}, u32[]{:S(2)}, u32[]{:S(2)}) collective-permute-start(f32[64,32]{0,1:T(8,128)S(1)} %fusion.1149), channel_id=1, source_target_pairs={{0,32},{1,33},{2,34},{3,35},{4,36},{5,37},{6,38},{7,39},{8,40},{9,... | collective-permute-start | bytes 24584 | tf_op jit(solution)/shard_map/ppermute | solution.py:40
  467.3 3.0 collective-permute-start.34
  474.0 6.3 %collective-permute-done.32 = f32[64,32]{0,1:T(8,128)S(1)} collective-permute-done((f32[64,32]{0,1:T(8,128)S(1)}, f32[64,32]{0,1:T(8,128)S(1)}, u32[]{:S(2)}, u32[]{:S(2)}) %collective-permute-start.32) | collective-permute-done | bytes 8224 | tf_op jit(solution)/shard_map/ppermute | solution.py:34
  480.3 6.0 %collective-permute-start.33 = (f32[64,32]{0,1:T(8,128)S(1)}, f32[64,32]{0,1:T(8,128)S(1)}, u32[]{:S(2)}, u32[]{:S(2)}) collective-permute-start(f32[64,32]{0,1:T(8,128)S(1)} %fusion.1149), channel_id=1, source_target_pairs={{64,0},{65,1},{66,2},{67,3},{68,4},{69,5},{70,6},{71,7},{72,8},{73... | collective-permute-start | bytes 24584 | tf_op jit(solution)/shard_map/ppermute | solution.py:34
  490.0 7.3 %collective-permute-done.37 = f32[64,32]{0,1:T(8,128)S(1)} collective-permute-done((f32[64,32]{0,1:T(8,128)S(1)}, f32[64,32]{0,1:T(8,128)S(1)}, u32[]{:S(2)}, u32[]{:S(2)}) %collective-permute-start.37) | collective-permute-done | bytes 8224 | tf_op jit(solution)/shard_map/ppermute | solution.py:34
  500.3 8.9 %collective-permute-start.39 = (f32[64,32]{0,1:T(8,128)S(1)}, f32[64,32]{0,1:T(8,128)S(1)}, u32[]{:S(2)}, u32[]{:S(2)}) collective-permute-start(f32[64,32]{0,1:T(8,128)S(1)} %fusion.1143), channel_id=1, source_target_pairs={{192,0},{193,1},{194,2},{195,3},{196,4},{197,5},{198,6},{199,7},{2... | collective-permute-start | bytes 24584 | tf_op jit(solution)/shard_map/ppermute | solution.py:34
  512.9 5.5 collective-permute-done.36
  520.8 6.2 %collective-permute-done.31 = f32[64,32]{0,1:T(8,128)S(1)} collective-permute-done((f32[64,32]{0,1:T(8,128)S(1)}, f32[64,32]{0,1:T(8,128)S(1)}, u32[]{:S(2)}, u32[]{:S(2)}) %collective-permute-start.31) | collective-permute-done | bytes 8224 | tf_op jit(solution)/shard_map/ppermute | solution.py:34
  530.1 5.9 %collective-permute-done.26 = f32[64,32]{0,1:T(8,128)S(1)} collective-permute-done((f32[64,32]{0,1:T(8,128)S(1)}, f32[64,32]{0,1:T(8,128)S(1)}, u32[]{:S(2)}, u32[]{:S(2)}) %collective-permute-start.26) | collective-permute-done | bytes 8224 | tf_op jit(solution)/shard_map/ppermute | solution.py:34
  536.0 3.9 collective-permute-start.21
  545.6 4.4 collective-permute-done.16
  567.9 3.4 convolution_bitcast_fusion.1
  571.3 10.0 %fusion.1117 = f32[32,16,2,2,64]{4,0,3,2,1:T(8,128)S(1)} fusion(f32[32,16,2,2,64]{4,0,3,2,1:T(8,128)S(1)} %convolution_bitcast_fusion.1, f32[32,16,2,2,64]{4,0,3,2,1:T(8,128)} %fusion.1030, f32[32,16,2,2,64]{4,0,3,2,1:T(8,128)} %fusion.1027, f32[32,16,2,2,64]{4,0,3,2,1:T(8,128)} %fusion.1024, f32[32,16,2,2,64]{4,0,3,2,1:T(8,128)} %fusion.1021, ...), kind=kOutput, calls=%fused_computation.1053 | convolution fusion | flops 110755840 | bytes 13221888 | tf_op jit(solution)/shard_map/zyxij,vzyxj->vzyxi/dot_general | solution.py:204
  (398 shorter events, 140.4 us)
Async XLA Ops:
  16.3 84.1 %collective-permute-start.4 = (f32[2,64,32]{1,2,0:T(8,128)S(1)}, f32[2,64,32]{1,2,0:T(8,128)S(1)}, u32[]{:S(2)}, u32[]{:S(2)}) collective-permute-start(f32[2,64,32]{1,2,0:T(8,128)S(1)} %convolution_bitcast_fusion.3), channel_id=1, source_target_pairs={{0,1},{1,2},{2,3},{3,4},{4,5},{5,6},{6,7},{7,8},{8,9},{9,10},{10,1... | collective-permute-start | bytes 49160 | tf_op jit(solution)/shard_map/ppermute | solution.py:23
  19.7 83.4 %collective-permute-start.5 = (f32[2,64,32]{1,2,0:T(8,128)S(1)}, f32[2,64,32]{1,2,0:T(8,128)S(1)}, u32[]{:S(2)}, u32[]{:S(2)}) collective-permute-start(f32[2,64,32]{1,2,0:T(8,128)S(1)} %convolution_bitcast_fusion.3), channel_id=1, source_target_pairs={{1,0},{2,1},{3,2},{4,3},{5,4},{6,5},{7,6},{8,7},{9,8},{10,9},{11,1... | collective-permute-start | bytes 49160 | tf_op jit(solution)/shard_map/ppermute | solution.py:26
  26.9 16.9 %collective-permute-start.10 = (f32[64,32]{0,1:T(8,128)}, f32[64,32]{0,1:T(8,128)S(1)}, u32[]{:S(2)}, u32[]{:S(2)}) collective-permute-start(f32[64,32]{0,1:T(8,128)} %convolution_bitcast_fusion.4), channel_id=1, source_target_pairs={{0,1},{1,0},{2,3},{3,2},{4,5},{5,4},{6,7},{7,6},{8,9},{9,8},{10,11... | collective-permute-start | bytes 24584 | tf_op jit(solution)/shard_map/ppermute | solution.py:40
  26.9 25.3 %collective-permute-start.9 = (f32[64,32]{0,1:T(8,128)}, f32[64,32]{0,1:T(8,128)S(1)}, u32[]{:S(2)}, u32[]{:S(2)}) collective-permute-start(f32[64,32]{0,1:T(8,128)} %convolution_bitcast_fusion.4), channel_id=1, source_target_pairs={{3,0},{4,1},{5,2},{6,3},{7,4},{8,5},{9,6},{10,7},{11,8},{12,9},{13... | collective-permute-start | bytes 24584 | tf_op jit(solution)/shard_map/ppermute | solution.py:34
  30.0 25.0 %collective-permute-start.7 = (f32[64,32]{0,1:T(8,128)}, f32[64,32]{0,1:T(8,128)S(1)}, u32[]{:S(2)}, u32[]{:S(2)}) collective-permute-start(f32[64,32]{0,1:T(8,128)} %convolution_bitcast_fusion.4), channel_id=1, source_target_pairs={{0,2},{1,3},{2,4},{3,5},{4,6},{5,7},{6,8},{7,9},{8,10},{9,11},{10,... | collective-permute-start | bytes 24584 | tf_op jit(solution)/shard_map/ppermute | solution.py:34
  35.4 387.7 %copy-start.77 = (f32[16,2,2,64]{3,2,1,0:T(2,128)}, f32[16,2,2,64]{3,2,1,0:T(2,128)S(1)}, u32[]{:S(2)}) copy-start(f32[16,2,2,64]{3,2,1,0:T(2,128)S(1)} %sub.1284) | copy-start | bytes 49156
  35.5 387.6 %copy-start.79 = (f32[16,2,2,64]{3,2,1,0:T(2,128)}, f32[16,2,2,64]{3,2,1,0:T(2,128)S(1)}, u32[]{:S(2)}) copy-start(f32[16,2,2,64]{3,2,1,0:T(2,128)S(1)} %sub.1289) | copy-start | bytes 49156
  35.6 387.5 %copy-start.81 = (f32[16,2,2,64]{3,2,1,0:T(2,128)}, f32[16,2,2,64]{3,2,1,0:T(2,128)S(1)}, u32[]{:S(2)}) copy-start(f32[16,2,2,64]{3,2,1,0:T(2,128)S(1)} %sub.1294) | copy-start | bytes 49156
  43.6 131.9 %copy-start.87 = (f32[64,64]{1,0:T(8,128)S(1)}, f32[64,64]{1,0:T(8,128)}, u32[]{:S(2)}) copy-start(f32[64,64]{1,0:T(8,128)} %constant.363) | copy-start | bytes 49156
  43.6 146.4 %copy-start.86 = (f32[64,64]{1,0:T(8,128)S(1)}, f32[64,64]{1,0:T(8,128)}, u32[]{:S(2)}) copy-start(f32[64,64]{1,0:T(8,128)} %constant.373) | copy-start | bytes 49156
  43.6 154.1 %copy-start.85 = (f32[64,64]{1,0:T(8,128)S(1)}, f32[64,64]{1,0:T(8,128)}, u32[]{:S(2)}) copy-start(f32[64,64]{1,0:T(8,128)} %constant.369) | copy-start | bytes 49156
  43.6 159.1 %copy-start.84 = (f32[64,64]{1,0:T(8,128)S(1)}, f32[64,64]{1,0:T(8,128)}, u32[]{:S(2)}) copy-start(f32[64,64]{1,0:T(8,128)} %constant.371) | copy-start | bytes 49156
  43.6 179.0 %copy-start.103 = (pred[2]{0:T(512)(128)(4,1)}, pred[2]{0:T(512)(128)(4,1)S(1)}, u32[]{:S(2)}) copy-start(pred[2]{0:T(512)(128)(4,1)S(1)} %fusion.1688) | copy-start | bytes 10
  43.8 14.7 %collective-permute-start.8 = (f32[64,32]{0,1:T(8,128)}, f32[64,32]{0,1:T(8,128)S(1)}, u32[]{:S(2)}, u32[]{:S(2)}) collective-permute-start(f32[64,32]{0,1:T(8,128)} %convolution_bitcast_fusion.4), channel_id=1, source_target_pairs={{2,0},{3,1},{4,2},{5,3},{6,4},{7,5},{8,6},{9,7},{10,8},{11,9},{12,... | collective-permute-start | bytes 24584 | tf_op jit(solution)/shard_map/ppermute | solution.py:34
  52.2 500.1 %collective-permute-start.6 = (f32[64,32]{0,1:T(8,128)}, f32[64,32]{0,1:T(8,128)}, u32[]{:S(2)}, u32[]{:S(2)}) collective-permute-start(f32[64,32]{0,1:T(8,128)} %convolution_bitcast_fusion.4), channel_id=1, source_target_pairs={{0,3},{1,4},{2,5},{3,6},{4,7},{5,8},{6,9},{7,10},{8,11},{9,12},{10... | collective-permute-start | bytes 24584 | tf_op jit(solution)/shard_map/ppermute | solution.py:34
  54.9 148.6 %collective-permute-start.42 = (f32[35,1,2,2,64]{4,0,3,2,1:T(8,128)S(1)}, f32[35,1,2,2,64]{4,0,3,2,1:T(8,128)S(1)}, u32[]{:S(2)}, u32[]{:S(2)}) collective-permute-start(f32[35,1,2,2,64]{4,0,3,2,1:T(8,128)S(1)} %get-tuple-element.95), channel_id=1, source_target_pairs={{0,1},{1,2},{2,3},{3,4},{4,5},{5,6},{6,7},{7,8},{8,9},{9,10},{10,1... | collective-permute-start | bytes 107528 | tf_op jit(solution)/shard_map/ppermute | solution.py:23
  58.5 9.4 %collective-permute-start = (f32[2,64,32]{1,2,0:T(8,128)S(1)}, f32[2,64,32]{1,2,0:T(8,128)S(1)}, u32[]{:S(2)}, u32[]{:S(2)}) collective-permute-start(f32[2,64,32]{1,2,0:T(8,128)S(1)} %get-tuple-element.99), channel_id=1, source_target_pairs={{0,1},{1,2},{2,3},{3,4},{4,5},{5,6},{6,7},{7,8},{8,9},{9,10},{10,1... | collective-permute-start | bytes 49160 | tf_op jit(solution)/shard_map/ppermute | solution.py:23
  68.0 5.8 collective-permute-start.1
  73.8 148.9 %copy-start.32 = (f32[2,64,32]{1,2,0:T(8,128)}, f32[2,64,32]{1,2,0:T(8,128)S(1)}, u32[]{:S(2)}) copy-start(f32[2,64,32]{1,2,0:T(8,128)S(1)} %collective-permute-done.1) | copy-start | bytes 49156
  73.8 9.4 %collective-permute-start.2 = (f32[2,64,32]{1,2,0:T(8,128)S(1)}, f32[2,64,32]{1,2,0:T(8,128)S(1)}, u32[]{:S(2)}, u32[]{:S(2)}) collective-permute-start(f32[2,64,32]{1,2,0:T(8,128)S(1)} %get-tuple-element.104), channel_id=1, source_target_pairs={{0,1},{1,2},{2,3},{3,4},{4,5},{5,6},{6,7},{7,8},{8,9},{9,10},{10,1... | collective-permute-start | bytes 49160 | tf_op jit(solution)/shard_map/ppermute | solution.py:23
  83.2 139.5 %copy-start.26 = (f32[2,64,32]{1,2,0:T(8,128)}, f32[2,64,32]{1,2,0:T(8,128)S(1)}, u32[]{:S(2)}) copy-start(f32[2,64,32]{1,2,0:T(8,128)S(1)} %collective-permute-done.2) | copy-start | bytes 49156
  83.2 5.8 collective-permute-start.3
  89.0 133.7 %copy-start.28 = (f32[2,64,32]{1,2,0:T(8,128)}, f32[2,64,32]{1,2,0:T(8,128)S(1)}, u32[]{:S(2)}) copy-start(f32[2,64,32]{1,2,0:T(8,128)S(1)} %collective-permute-done.3) | copy-start | bytes 49156
  89.0 5.5 collective-permute-start.15
  94.5 110.9 %collective-permute-start.43 = (f32[35,1,2,2,64]{4,0,3,2,1:T(8,128)S(1)}, f32[35,1,2,2,64]{4,0,3,2,1:T(8,128)S(1)}, u32[]{:S(2)}, u32[]{:S(2)}) collective-permute-start(f32[35,1,2,2,64]{4,0,3,2,1:T(8,128)S(1)} %get-tuple-element.96), channel_id=1, source_target_pairs={{1,0},{2,1},{3,2},{4,3},{5,4},{6,5},{7,6},{8,7},{9,8},{10,9},{11,1... | collective-permute-start | bytes 107528 | tf_op jit(solution)/shard_map/ppermute | solution.py:26
  100.3 456.0 %collective-permute-start.40 = (f32[2,2,2,64,32]{3,4,2,1,0:T(8,128)}, f32[2,2,2,64,32]{3,4,2,1,0:T(8,128)}, u32[]{:S(2)}, u32[]{:S(2)}) collective-permute-start(f32[2,2,2,64,32]{3,4,2,1,0:T(8,128)} %get-tuple-element.97), channel_id=1, source_target_pairs={{0,1},{1,2},{2,3},{3,4},{4,5},{5,6},{6,7},{7,8},{8,9},{9,10},{10,1... | collective-permute-start | bytes 196616 | tf_op jit(solution)/shard_map/ppermute | solution.py:23
  103.1 6.8 %collective-permute-start.14 = (f32[64,32]{0,1:T(8,128)}, f32[64,32]{0,1:T(8,128)S(1)}, u32[]{:S(2)}, u32[]{:S(2)}) collective-permute-start(f32[64,32]{0,1:T(8,128)} %fusion.1173), channel_id=1, source_target_pairs={{6,0},{7,1},{8,2},{9,3},{10,4},{11,5},{12,6},{13,7},{14,8},{15,9},... | collective-permute-start | bytes 24584 | tf_op jit(solution)/shard_map/ppermute | solution.py:34
  109.8 7.4 %collective-permute-start.12 = (f32[64,32]{0,1:T(8,128)}, f32[64,32]{0,1:T(8,128)S(1)}, u32[]{:S(2)}, u32[]{:S(2)}) collective-permute-start(f32[64,32]{0,1:T(8,128)} %fusion.1173), channel_id=1, source_target_pairs={{0,4},{1,5},{2,6},{3,7},{4,8},{5,9},{6,10},{7,11},{8,12},{9,13},{1... | collective-permute-start | bytes 24584 | tf_op jit(solution)/shard_map/ppermute | solution.py:34
  117.2 3.5 collective-permute-start.13
  120.7 22.6 %collective-permute-start.20 = (f32[64,32]{0,1:T(8,128)S(1)}, f32[64,32]{0,1:T(8,128)S(1)}, u32[]{:S(2)}, u32[]{:S(2)}) collective-permute-start(f32[64,32]{0,1:T(8,128)S(1)} %fusion.1167), channel_id=1, source_target_pairs={{0,4},{1,5},{2,6},{3,7},{4,0},{5,1},{6,2},{7,3},{8,12},{9,13},{10,... | collective-permute-start | bytes 24584 | tf_op jit(solution)/shard_map/ppermute | solution.py:40
  143.4 7.0 %collective-permute-start.19 = (f32[64,32]{0,1:T(8,128)S(1)}, f32[64,32]{0,1:T(8,128)S(1)}, u32[]{:S(2)}, u32[]{:S(2)}) collective-permute-start(f32[64,32]{0,1:T(8,128)S(1)} %fusion.1167), channel_id=1, source_target_pairs={{12,0},{13,1},{14,2},{15,3},{16,4},{17,5},{18,6},{19,7},{20,8},{21... | collective-permute-start | bytes 24584 | tf_op jit(solution)/shard_map/ppermute | solution.py:34
  150.4 7.7 %collective-permute-start.17 = (f32[64,32]{0,1:T(8,128)S(1)}, f32[64,32]{0,1:T(8,128)S(1)}, u32[]{:S(2)}, u32[]{:S(2)}) collective-permute-start(f32[64,32]{0,1:T(8,128)S(1)} %fusion.1167), channel_id=1, source_target_pairs={{0,8},{1,9},{2,10},{3,11},{4,12},{5,13},{6,14},{7,15},{8,16},{9,17... | collective-permute-start | bytes 24584 | tf_op jit(solution)/shard_map/ppermute | solution.py:34
  158.1 5.6 collective-permute-start.18
  163.7 15.0 %collective-permute-start.25 = (f32[64,32]{0,1:T(8,128)S(1)}, f32[64,32]{0,1:T(8,128)S(1)}, u32[]{:S(2)}, u32[]{:S(2)}) collective-permute-start(f32[64,32]{0,1:T(8,128)S(1)} %fusion.1161), channel_id=1, source_target_pairs={{0,8},{1,9},{2,10},{3,11},{4,12},{5,13},{6,14},{7,15},{8,0},{9,1},... | collective-permute-start | bytes 24584 | tf_op jit(solution)/shard_map/ppermute | solution.py:40
  178.8 6.8 %collective-permute-start.24 = (f32[64,32]{0,1:T(8,128)S(1)}, f32[64,32]{0,1:T(8,128)S(1)}, u32[]{:S(2)}, u32[]{:S(2)}) collective-permute-start(f32[64,32]{0,1:T(8,128)S(1)} %fusion.1161), channel_id=1, source_target_pairs={{24,0},{25,1},{26,2},{27,3},{28,4},{29,5},{30,6},{31,7},{32,8},{33... | collective-permute-start | bytes 24584 | tf_op jit(solution)/shard_map/ppermute | solution.py:34
  185.6 8.0 %collective-permute-start.22 = (f32[64,32]{0,1:T(8,128)S(1)}, f32[64,32]{0,1:T(8,128)S(1)}, u32[]{:S(2)}, u32[]{:S(2)}) collective-permute-start(f32[64,32]{0,1:T(8,128)S(1)} %fusion.1161), channel_id=1, source_target_pairs={{0,16},{1,17},{2,18},{3,19},{4,20},{5,21},{6,22},{7,23},{8,24},{9,... | collective-permute-start | bytes 24584 | tf_op jit(solution)/shard_map/ppermute | solution.py:34
  193.6 7.1 %collective-permute-start.23 = (f32[64,32]{0,1:T(8,128)S(1)}, f32[64,32]{0,1:T(8,128)S(1)}, u32[]{:S(2)}, u32[]{:S(2)}) collective-permute-start(f32[64,32]{0,1:T(8,128)S(1)} %fusion.1161), channel_id=1, source_target_pairs={{16,0},{17,1},{18,2},{19,3},{20,4},{21,5},{22,6},{23,7},{24,8},{25... | collective-permute-start | bytes 24584 | tf_op jit(solution)/shard_map/ppermute | solution.py:34
  200.7 355.6 %collective-permute-start.41 = (f32[2,2,2,64,32]{3,4,2,1,0:T(8,128)}, f32[2,2,2,64,32]{3,4,2,1,0:T(8,128)}, u32[]{:S(2)}, u32[]{:S(2)}) collective-permute-start(f32[2,2,2,64,32]{3,4,2,1,0:T(8,128)} %get-tuple-element.98), channel_id=1, source_target_pairs={{1,0},{2,1},{3,2},{4,3},{5,4},{6,5},{7,6},{8,7},{9,8},{10,9},{11,1... | collective-permute-start | bytes 196616 | tf_op jit(solution)/shard_map/ppermute | solution.py:26
  203.5 347.6 %collective-permute-start.11 = (f32[64,32]{0,1:T(8,128)}, f32[64,32]{0,1:T(8,128)}, u32[]{:S(2)}, u32[]{:S(2)}) collective-permute-start(f32[64,32]{0,1:T(8,128)} %fusion.1173), channel_id=1, source_target_pairs={{0,6},{1,7},{2,8},{3,9},{4,10},{5,11},{6,12},{7,13},{8,14},{9,15},... | collective-permute-start | bytes 24584 | tf_op jit(solution)/shard_map/ppermute | solution.py:34
  205.4 225.9 %collective-permute-start.30 = (f32[64,32]{0,1:T(8,128)S(1)}, f32[64,32]{0,1:T(8,128)S(1)}, u32[]{:S(2)}, u32[]{:S(2)}) collective-permute-start(f32[64,32]{0,1:T(8,128)S(1)} %fusion.1155), channel_id=1, source_target_pairs={{0,16},{1,17},{2,18},{3,19},{4,20},{5,21},{6,22},{7,23},{8,24},{9,... | collective-permute-start | bytes 24584 | tf_op jit(solution)/shard_map/ppermute | solution.py:40
  423.2 126.8 %copy-start.59 = (f32[32,64]{1,0:T(8,128)S(1)}, f32[32,64]{1,0:T(8,128)}, u32[]{:S(2)}) copy-start(f32[32,64]{1,0:T(8,128)} %convolution_select_fusion.14) | copy-start | bytes 24580
  423.2 126.8 %copy-start.60 = (f32[32,64]{1,0:T(8,128)S(1)}, f32[32,64]{1,0:T(8,128)}, u32[]{:S(2)}) copy-start(f32[32,64]{1,0:T(8,128)} %fusion.1958) | copy-start | bytes 24580
  423.2 126.8 %copy-start.61 = (f32[32,64]{1,0:T(8,128)S(1)}, f32[32,64]{1,0:T(8,128)}, u32[]{:S(2)}) copy-start(f32[32,64]{1,0:T(8,128)} %fusion.1959) | copy-start | bytes 24580
  431.2 124.8 %copy-start.6 = (f32[8,32,64,1,1,1]{2,1,5,4,3,0:T(8,128)S(1)}, f32[8,32,64,1,1,1]{2,1,5,4,3,0:T(8,128)}, u32[]{:S(2)}) copy-start(f32[8,32,64,1,1,1]{2,1,5,4,3,0:T(8,128)} %copy-done.5) | copy-start | bytes 196612
  431.2 124.8 %copy-start.19 = (f32[8,32,64]{2,1,0:T(8,128)S(1)}, f32[8,32,64]{2,1,0:T(8,128)}, u32[]{:S(2)}) copy-start(f32[8,32,64]{2,1,0:T(8,128)} %fusion.1613) | copy-start | bytes 196612
  431.2 124.8 %copy-start.20 = (f32[8,32,64]{2,1,0:T(8,128)S(1)}, f32[8,32,64]{2,1,0:T(8,128)}, u32[]{:S(2)}) copy-start(f32[8,32,64]{2,1,0:T(8,128)} %convolution_select_fusion) | copy-start | bytes 196612
  431.2 124.8 %copy-start.21 = (f32[8,32,64]{2,1,0:T(8,128)S(1)}, f32[8,32,64]{2,1,0:T(8,128)}, u32[]{:S(2)}) copy-start(f32[8,32,64]{2,1,0:T(8,128)} %fusion.1617) | copy-start | bytes 196612
  431.2 124.8 %copy-start.31 = (f32[2,64,32]{1,2,0:T(8,128)S(1)}, f32[2,64,32]{1,2,0:T(8,128)}, u32[]{:S(2)}) copy-start(f32[2,64,32]{1,2,0:T(8,128)} %copy-done.30) | copy-start | bytes 49156
  431.2 124.8 %copy-start.33 = (f32[2,64,32]{1,2,0:T(8,128)S(1)}, f32[2,64,32]{1,2,0:T(8,128)}, u32[]{:S(2)}) copy-start(f32[2,64,32]{1,2,0:T(8,128)} %copy-done.32) | copy-start | bytes 49156
  431.3 8.2 %collective-permute-start.29 = (f32[64,32]{0,1:T(8,128)S(1)}, f32[64,32]{0,1:T(8,128)S(1)}, u32[]{:S(2)}, u32[]{:S(2)}) collective-permute-start(f32[64,32]{0,1:T(8,128)S(1)} %fusion.1155), channel_id=1, source_target_pairs={{48,0},{49,1},{50,2},{51,3},{52,4},{53,5},{54,6},{55,7},{56,8},{57... | collective-permute-start | bytes 24584 | tf_op jit(solution)/shard_map/ppermute | solution.py:34
  439.5 5.8 collective-permute-start.27
  445.2 5.6 collective-permute-start.28
  450.8 16.5 %collective-permute-start.35 = (f32[64,32]{0,1:T(8,128)S(1)}, f32[64,32]{0,1:T(8,128)S(1)}, u32[]{:S(2)}, u32[]{:S(2)}) collective-permute-start(f32[64,32]{0,1:T(8,128)S(1)} %fusion.1149), channel_id=1, source_target_pairs={{0,32},{1,33},{2,34},{3,35},{4,36},{5,37},{6,38},{7,39},{8,40},{9,... | collective-permute-start | bytes 24584 | tf_op jit(solution)/shard_map/ppermute | solution.py:40
  467.3 4.5 collective-permute-start.34
  471.8 8.5 %collective-permute-start.32 = (f32[64,32]{0,1:T(8,128)S(1)}, f32[64,32]{0,1:T(8,128)S(1)}, u32[]{:S(2)}, u32[]{:S(2)}) collective-permute-start(f32[64,32]{0,1:T(8,128)S(1)} %fusion.1149), channel_id=1, source_target_pairs={{0,64},{1,65},{2,66},{3,67},{4,68},{5,69},{6,70},{7,71},{8,72},{9,... | collective-permute-start | bytes 24584 | tf_op jit(solution)/shard_map/ppermute | solution.py:34
  480.3 7.4 %collective-permute-start.33 = (f32[64,32]{0,1:T(8,128)S(1)}, f32[64,32]{0,1:T(8,128)S(1)}, u32[]{:S(2)}, u32[]{:S(2)}) collective-permute-start(f32[64,32]{0,1:T(8,128)S(1)} %fusion.1149), channel_id=1, source_target_pairs={{64,0},{65,1},{66,2},{67,3},{68,4},{69,5},{70,6},{71,7},{72,8},{73... | collective-permute-start | bytes 24584 | tf_op jit(solution)/shard_map/ppermute | solution.py:34
  487.8 9.5 %collective-permute-start.37 = (f32[64,32]{0,1:T(8,128)S(1)}, f32[64,32]{0,1:T(8,128)S(1)}, u32[]{:S(2)}, u32[]{:S(2)}) collective-permute-start(f32[64,32]{0,1:T(8,128)S(1)} %fusion.1143), channel_id=1, source_target_pairs={{0,128},{1,129},{2,130},{3,131},{4,132},{5,133},{6,134},{7,135},{8... | collective-permute-start | bytes 24584 | tf_op jit(solution)/shard_map/ppermute | solution.py:34
  497.3 3.1 collective-permute-start.38
  500.3 10.4 %collective-permute-start.39 = (f32[64,32]{0,1:T(8,128)S(1)}, f32[64,32]{0,1:T(8,128)S(1)}, u32[]{:S(2)}, u32[]{:S(2)}) collective-permute-start(f32[64,32]{0,1:T(8,128)S(1)} %fusion.1143), channel_id=1, source_target_pairs={{192,0},{193,1},{194,2},{195,3},{196,4},{197,5},{198,6},{199,7},{2... | collective-permute-start | bytes 24584 | tf_op jit(solution)/shard_map/ppermute | solution.py:34
  510.7 7.7 %collective-permute-start.36 = (f32[64,32]{0,1:T(8,128)S(1)}, f32[64,32]{0,1:T(8,128)S(1)}, u32[]{:S(2)}, u32[]{:S(2)}) collective-permute-start(f32[64,32]{0,1:T(8,128)S(1)} %fusion.1143), channel_id=1, source_target_pairs={{0,192},{1,193},{2,194},{3,195},{4,196},{5,197},{6,198},{7,199},{8... | collective-permute-start | bytes 24584 | tf_op jit(solution)/shard_map/ppermute | solution.py:34
  518.4 8.6 %collective-permute-start.31 = (f32[64,32]{0,1:T(8,128)S(1)}, f32[64,32]{0,1:T(8,128)S(1)}, u32[]{:S(2)}, u32[]{:S(2)}) collective-permute-start(f32[64,32]{0,1:T(8,128)S(1)} %fusion.1149), channel_id=1, source_target_pairs={{0,96},{1,97},{2,98},{3,99},{4,100},{5,101},{6,102},{7,103},{8,104... | collective-permute-start | bytes 24584 | tf_op jit(solution)/shard_map/ppermute | solution.py:34
  527.1 8.9 %collective-permute-start.26 = (f32[64,32]{0,1:T(8,128)S(1)}, f32[64,32]{0,1:T(8,128)S(1)}, u32[]{:S(2)}, u32[]{:S(2)}) collective-permute-start(f32[64,32]{0,1:T(8,128)S(1)} %fusion.1155), channel_id=1, source_target_pairs={{0,48},{1,49},{2,50},{3,51},{4,52},{5,53},{6,54},{7,55},{8,56},{9,... | collective-permute-start | bytes 24584 | tf_op jit(solution)/shard_map/ppermute | solution.py:34
  536.0 6.5 %collective-permute-start.21 = (f32[64,32]{0,1:T(8,128)S(1)}, f32[64,32]{0,1:T(8,128)S(1)}, u32[]{:S(2)}, u32[]{:S(2)}) collective-permute-start(f32[64,32]{0,1:T(8,128)S(1)} %copy-done.47), channel_id=1, source_target_pairs={{0,24},{1,25},{2,26},{3,27},{4,28},{5,29},{6,30},{7,31},{8,32},{9,... | collective-permute-start | bytes 24584 | tf_op jit(solution)/shard_map/ppermute | solution.py:34
  542.5 7.5 %collective-permute-start.16 = (f32[64,32]{0,1:T(8,128)S(1)}, f32[64,32]{0,1:T(8,128)S(1)}, u32[]{:S(2)}, u32[]{:S(2)}) collective-permute-start(f32[64,32]{0,1:T(8,128)S(1)} %copy-done.45), channel_id=1, source_target_pairs={{0,12},{1,13},{2,14},{3,15},{4,16},{5,17},{6,18},{7,19},{8,20},{9,... | collective-permute-start | bytes 24584 | tf_op jit(solution)/shard_map/ppermute | solution.py:34
  (90 other events, 5794.5 us)
where the time goes:
time: 596 us; the launch traced here: 584 us
  matrix products  273 us (46%)
  starting transfers between devices  183 us (31%)
  waiting for transfers between devices  95.6 us (16%)
  local copies, waits for them, and re-layouts  21.9 us (4%)
  other arithmetic  8.05 us (1%)
    dot_general x27, matrix products, near_field(): jnp.einsum('zyxij,vzyxj->vzyxi', weights, source[3:], precision=lax.Preci...  222 us
    ppermute x28, starting transfers between devices, from_behind(): return lax.ppermute(shard, axis, pairs)  90.4 us
    ppermute x28, waiting for transfers between devices, from_behind(): return lax.ppermute(shard, axis, pairs)  69.1 us
    ppermute x6, starting transfers between devices, swapped(): return lax.ppermute(value, axis, pairs)  62.9 us
    dot_general x28, matrix products, local(): jnp.dot(couplings[position], source, precision=lax.Precision.HIGHEST)  23.4 us
    ppermute x5, starting transfers between devices, padded_2(): lax.ppermute(lax.slice_in_dim(block, 0, width, axis=dim), axis, backward)  17.5 us
    ppermute x5, waiting for transfers between devices, padded_2(): lax.ppermute(lax.slice_in_dim(block, block.shape[dim] - width, None, axis...  12.4 us
    ppermute x5, starting transfers between devices, padded_2(): lax.ppermute(lax.slice_in_dim(block, block.shape[dim] - width, None, axis...  11.9 us
  transfers between devices with their start and end apart: 44, of which 31 were waited for; matrix products, arithmetic and copies ran while one was open for 44% of the time, Pallas kernels for 0%

commit v1 on v0

v1 whole, which is shorter than its diff:
```python
import functools
import math

import jax
import jax.numpy as jnp
import ml_dtypes
import numpy as np
from jax import lax
from jax.experimental import pallas as pl
from jax.experimental.pallas import tpu as pltpu
from jax.sharding import PartitionSpec as P

ORDER = 4
VECS = 32
CUBES = 8
LAYERS = 16
SLOTS = 4096
TOP = 10
ROOT_THREE = math.sqrt(3.0)
AXES = ("leaf", "sub")
F32 = jnp.float32
BF16 = jnp.bfloat16
NN = (((1,), (0,)), ((), ()))
NT = (((1,), (1,)), ((), ()))
NODES = np.cos((2.0 * np.arange(ORDER) + 1.0) * np.pi / (2.0 * ORDER))
LENGTHS = [512.0, 64.0, 8.0, 1.0]
STRETCH = ROOT_THREE / math.log(2.0)
VMEM_LIMIT = 48 * 1024 * 1024


def lagrange_table(values):
    columns = []
    for anchor in range(ORDER):
        product = values * 0.0 + 1.0
        for against in range(ORDER):
            if against != anchor:
                product = product * (values - NODES[against]) / (NODES[anchor] - NODES[against])
        columns.append(product)
    return np.stack(columns, -1)


def grid_nodes():
    z, y, x = np.meshgrid(np.arange(ORDER), np.arange(ORDER), np.arange(ORDER), indexing="ij")
    return np.stack([NODES[x.ravel()], NODES[y.ravel()], NODES[z.ravel()]], -1)


def kernel_table(targets, sources):
    gaps = targets[:, None, :] - sources[None, :, :]
    distance = np.sqrt(np.sum(gaps * gaps, -1))
    total = distance * 0.0
    for length in LENGTHS:
        scaled = distance * (ROOT_THREE / length)
        total = total + (1.0 + scaled) * np.exp(-scaled) / (32.0 * math.sqrt(length))
    return total


def layer_nodes(layer):
    scaled = grid_nodes() * 0.25
    leaves = []
    for row in range(2):
        for column in range(2):
            centre = [(column + 0.5) * 0.5, (row + 0.5) * 0.5, (layer + 0.5) * 0.5]
            leaves.append(scaled + np.array(centre))
    return np.concatenate(leaves)


def pair_coupling(level):
    span = float(1 << level)
    nodes = grid_nodes() * np.array([0.5, 0.5, 0.5 * span])

    def block(offset):
        return kernel_table(nodes, nodes + np.array([0.0, 0.0, offset * span])).T

    zero = np.zeros((64, 64))
    before = np.block([[block(-2), block(-3)], [zero, block(-2)]])
    after = np.block([[block(2), zero], [block(3), block(2)]])
    return np.concatenate([before, after], 0)


def transfer_tables():
    halves = [lagrange_table(side + 0.5 * NODES) for side in (-0.5, 0.5)]
    eye = np.eye(ORDER)
    octants = [
        np.kron(np.kron(halves[z], halves[y]), halves[x])
        for z in range(2)
        for y in range(2)
        for x in range(2)
    ]
    along = [np.kron(np.kron(half, eye), eye) for half in halves]
    return np.concatenate(octants, 0), np.concatenate(along, 0)


def hi_lo(table):
    high = table.astype(ml_dtypes.bfloat16)
    low = (table - high.astype(np.float64)).astype(ml_dtypes.bfloat16)
    return jnp.asarray(high), jnp.asarray(low)


def split(x):
    high = x.astype(BF16)
    return high, (x - high.astype(F32)).astype(BF16)


def mxu(a, b, dims=NN):
    return lax.dot_general(a, b, dims, preferred_element_type=F32)


def dot3(x, high, low, dims=NN):
    rows = x.shape[0]
    x_high, x_low = split(x)
    both = mxu(jnp.concatenate([x_high, x_low], 0), high, dims)
    return both[:rows] + both[rows:] + mxu(x_high, low, dims)


def poly4(u):
    gaps = [u - float(node) for node in NODES]
    polys = []
    for anchor in range(ORDER):
        scale = 1.0
        product = None
        for against in range(ORDER):
            if against != anchor:
                scale = scale / float(NODES[anchor] - NODES[against])
                product = gaps[against] if product is None else product * gaps[against]
        polys.append(product * scale)
    return polys


def basis64(u):
    count = u.shape[1]
    polys = poly4(u)
    row = lax.broadcasted_iota(jnp.int32, (16, count), 0)

    def picked(dim, key):
        rows = [jnp.broadcast_to(poly[dim : dim + 1], (16, count)) for poly in polys]
        low = jnp.where(key == 0, rows[0], rows[1])
        high = jnp.where(key == 2, rows[2], rows[3])
        return jnp.where(key < 2, low, high)

    plane = picked(0, row % 4) * picked(1, row // 4)
    return jnp.concatenate([plane * poly[2:3] for poly in polys], 0)


def stack_rows(x, width):
    return jnp.concatenate(
        [x[:, i * width : (i + 1) * width] for i in range(x.shape[1] // width)], 0
    )


def pair_rows(boxes):
    count = boxes.shape[0] // VECS
    parts = [boxes[i * VECS : (i + 1) * VECS] for i in range(count)]
    return jnp.concatenate(
        [jnp.concatenate(parts[i : i + 2], 1) for i in range(0, count, 2)], 0
    )


def unpair_rows(pairs):
    count = pairs.shape[0] // VECS
    parts = []
    for i in range(count):
        block = pairs[i * VECS : (i + 1) * VECS]
        parts += [block[:, :64], block[:, 64:]]
    return jnp.concatenate(parts, 0)


def pack_box(box):
    return jnp.concatenate([box[:16], box[16:]], 1)


def unpack_box(packed):
    return jnp.concatenate([packed[:, :64], packed[:, 64:]], 0)


def features(coords, origin):
    row = lax.broadcasted_iota(jnp.int32, coords.shape, 0)
    q = (coords - jnp.where(row == 2, origin, 0.0)) * STRETCH
    norm = jnp.sum(q * q, axis=0, keepdims=True)
    left = jnp.where(row == 3, norm, jnp.where(row == 4, 1.0, q))
    right = jnp.where(row == 3, 1.0, jnp.where(row == 4, norm, -2.0 * q))
    return left, right


def three_parts(x):
    first = x.astype(BF16).astype(F32)
    rest = x - first
    second = rest.astype(BF16).astype(F32)
    return first, second, rest - second


def left_side(left):
    f1, f2, f3 = three_parts(left)
    return jnp.concatenate([f1, f1, f2, f2, f1, f3], 0)


def right_side(right):
    g1, g2, g3 = three_parts(right)
    return jnp.concatenate([g1, g2, g1, g2, g3, g1], 0).astype(BF16)


def matern(squared):
    squared = jnp.maximum(squared, 1e-20)
    w = squared * lax.rsqrt(squared)
    total = None
    for length in LENGTHS:
        weight = 1.0 / (32.0 * math.sqrt(length))
        slope = weight * math.log(2.0) / length
        term = (weight + slope * w) * jnp.exp2(w * (-1.0 / length))
        total = term if total is None else total + term
    return total


def fill_weights(left, right, high_ref, low_ref):
    turned = jnp.transpose(left_side(left)).astype(BF16)
    sources = right_side(right)
    rows, columns = left.shape[1], right.shape[1]
    step = 32
    for top in range(0, rows, step):
        for start in range(0, columns, 256):
            squared = mxu(turned[top : top + step], sources[:, start : start + 256])
            high, low = split(matern(squared))
            high_ref[top : top + step, start : start + 256] = high
            low_ref[top : top + step, start : start + 256] = low


def weigh(x, high, low, dims):
    return dot3(x, high, low, dims)


def head_kernel(slab_ref, counts_ref, points_ref, vectors_ref, coords_ref, masked_ref, occ_ref,
                box_ref, high_ref, low_ref):
    first = slab_ref[0].astype(F32)
    lane = lax.broadcasted_iota(jnp.int32, (1, 512), 1)
    row = lax.broadcasted_iota(jnp.int32, (8, 512), 0)

    def cube(s, total):
        at = pl.ds(pl.multiple_of(s * 512, 512), 512)
        filled = jnp.zeros((1, 512), jnp.int32)
        for c in range(8):
            filled = jnp.where(lane // 64 == c, counts_ref[s, c], filled)
        occupied = (lane % 64 < filled).astype(F32)
        occ_ref[:, at] = occupied
        masked = vectors_ref[:, at] * occupied
        masked_ref[:, at] = masked
        points = points_ref[:, at]
        points = jnp.concatenate([points, jnp.zeros((5, 512), F32)], 0)
        shift = jnp.where(row == 2, first, jnp.where(row < 2, 0.5, 0.0))
        coords = points - shift
        coords_ref[:, at] = coords
        u = (coords - jnp.where(row == 2, 4.0, 0.0)) * jnp.where(row == 2, 0.25, 2.0)
        high, low = split(basis64(u))
        high_ref[:, at] = high
        low_ref[:, at] = low
        return total + dot3(masked, high, low, NT)

    total = lax.fori_loop(0, CUBES, cube, jnp.zeros((VECS, 64), F32))
    box_ref[...] = pack_box(total)


def spread_basis(high, low):
    lane = lax.broadcasted_iota(jnp.int32, (1, 256), 1)
    highs, lows = [], []
    for leaf in range(4):
        mask = (lane // 64 == leaf).astype(F32).astype(BF16)
        highs.append(high * mask)
        lows.append(low * mask)
    return jnp.concatenate(highs, 0), jnp.concatenate(lows, 0)


def leaf_kernel(coords_ref, masked_ref, octh_ref, octl_ref, lifth_ref, liftl_ref, coef_ref,
                high_ref, low_ref, p0_ref, p1_ref, p2_ref, ahead_ref, behind_ref):
    lane = lax.broadcasted_iota(jnp.int32, (8, 256), 1)
    row = lax.broadcasted_iota(jnp.int32, (8, 256), 0)
    centre_x = jnp.where(lane // 64 % 2 == 0, -0.25, 0.25)
    centre_y = jnp.where(lane // 128 == 0, -0.25, 0.25)

    def layer(z, carry):
        at = pl.ds(pl.multiple_of(z * 256, 256), 256)
        centre_z = z.astype(F32) * 0.5 + 0.25
        centre = jnp.where(row == 0, centre_x, jnp.where(row == 1, centre_y, centre_z))
        u = (coords_ref[:, at] - centre) * 4.0
        high, low = split(basis64(u))
        high_ref[:, at] = high
        low_ref[:, at] = low
        wide_high, wide_low = spread_basis(high, low)
        coef_ref[:, at] = dot3(masked_ref[:, at], wide_high, wide_low, NT)
        return carry

    lax.fori_loop(0, LAYERS, layer, 0)
    boxes = dot3(stack_rows(coef_ref[...], 512), octh_ref[...], octl_ref[...])
    p0 = pair_rows(boxes)
    p1 = pair_rows(dot3(p0, lifth_ref[...], liftl_ref[...]))
    p2 = pair_rows(dot3(p1, lifth_ref[...], liftl_ref[...]))
    p0_ref[...] = p0
    p1_ref[...] = p1
    p2_ref[...] = p2
    for ref, near, far, low_pair, mid_pair in (
        (ahead_ref, SLOTS - 256, SLOTS - 512, p0[96:], p1[32:]),
        (behind_ref, 0, 0, p0[:32], p1[:32]),
    ):
        ref[:, 0:256] = masked_ref[:, near : near + 256]
        ref[:, 256:768] = coef_ref[:, far : far + 512]
        ref[:, 768:896] = low_pair
        ref[:, 896:1024] = mid_pair
        ref[:, 1024:1152] = p2
        ref[:, 1152:1280] = jnp.zeros((VECS, 128), F32)
        ref[0:8, 1152:1280] = coords_ref[:, near : near + 128]
        ref[8:16, 1152:1280] = coords_ref[:, near + 128 : near + 256]


def near_kernel(begin, end, coords_ref, masked_ref, before_ref, hold_ref, near_ref, high_ref,
                low_ref):
    del hold_ref
    near_ref[...] = before_ref[...] if begin else jnp.zeros_like(near_ref)

    def layer(z, carry):
        own = pl.ds(pl.multiple_of(z * 256, 256), 256)
        both = pl.ds(pl.multiple_of(z * 256, 256), 512)
        after = pl.ds(pl.multiple_of(z * 256 + 256, 256), 256)
        left, right = features(coords_ref[:, both], z.astype(F32) * 0.5 + 0.5)
        fill_weights(left[:, :256], right, high_ref, low_ref)
        x = masked_ref[:, own]
        summed = weigh(x, high_ref[...], low_ref[...], NN)
        back = weigh(masked_ref[:, after], high_ref[:, 256:], low_ref[:, 256:], NT)
        near_ref[:, own] += summed[:, :256] + back
        near_ref[:, after] += summed[:, 256:]
        return carry

    lax.fori_loop(begin, min(end, LAYERS - 1), layer, 0)
    if end == LAYERS:
        left, right = features(coords_ref[:, SLOTS - 256 :], LAYERS / 2.0)
        fill_weights(left, right, high_ref, low_ref)
        near_ref[:, SLOTS - 256 :] += weigh(
            masked_ref[:, SLOTS - 256 :], high_ref[:, :256], low_ref[:, :256], NN
        )


def gather_kernel(member_ref, a_ref, b_ref, c_ref, d_ref, lifth_ref, liftl_ref, hold_ref,
                  quad_ref, pair_ref, box_ref, ahead_ref, behind_ref, slots):
    del hold_ref
    member = member_ref[0]
    for step, ref in enumerate((a_ref, b_ref, c_ref, d_ref)):
        slots[pl.ds(member ^ step, 1)] = unpack_box(ref[...])[None]
    left = jnp.concatenate([slots[0], slots[1]], 1)
    right = jnp.concatenate([slots[2], slots[3]], 1)
    quad_ref[...] = jnp.concatenate([left, right], 1)
    lifted = dot3(jnp.concatenate([left, right], 0), lifth_ref[...], liftl_ref[...])
    pair = pair_rows(lifted)
    pair_ref[...] = pair
    box_ref[...] = pack_box(dot3(pair, lifth_ref[...], liftl_ref[...]))
    ahead_ref[...] = jnp.concatenate([right, pair], 1)
    behind_ref[...] = jnp.concatenate([left, pair], 1)


def rim_kernel(coords_ref, masked_ref, near_ref, coef_ref, basish_ref, basisl_ref, p0_ref, p1_ref,
               p2_ref, left_ref, right_ref, k2h_ref, k2l_ref, k3h_ref, k3l_ref, m0h_ref, m0l_ref,
               m1h_ref, m1l_ref, m2h_ref, m2l_ref, sinkh_ref, sinkl_ref, octh_ref, octl_ref,
               hold_ref, base_ref, high_ref, low_ref):
    del hold_ref
    base_ref[...] = near_ref[...]
    row = lax.broadcasted_iota(jnp.int32, (8, 256), 0)

    def rim_coords(ref, shift):
        coords = jnp.concatenate([ref[0:8, 1152:1280], ref[8:16, 1152:1280]], 1)
        return coords + jnp.where(row == 2, shift, 0.0)

    low_rim = rim_coords(left_ref, -float(CUBES))
    left, _ = features(low_rim, 0.0)
    _, right = features(coords_ref[:, :256], 0.0)
    fill_weights(left, right, high_ref, low_ref)
    base_ref[:, :256] += weigh(left_ref[:, :256], high_ref[...], low_ref[...], NN)
    high_rim = rim_coords(right_ref, float(CUBES))
    left, _ = features(coords_ref[:, SLOTS - 256 :], float(CUBES))
    _, right = features(high_rim, float(CUBES))
    fill_weights(left, right, high_ref, low_ref)
    base_ref[:, SLOTS - 256 :] += weigh(right_ref[:, :256], high_ref[...], low_ref[...], NT)

    coefs = [coef_ref[:, 512 * s : 512 * s + 512] for s in range(CUBES)]
    before = jnp.concatenate([left_ref[:, 256:768]] + coefs[:-1], 0)
    after = jnp.concatenate(coefs[1:] + [right_ref[:, 256:768]], 0)
    k2 = (k2h_ref[...], k2l_ref[...])
    k3 = (k3h_ref[...], k3l_ref[...])
    even = dot3(before[:, :256], *k2) + dot3(after[:, :256], *k2, NT) + dot3(after[:, 256:], *k3, NT)
    odd = dot3(before[:, :256], *k3) + dot3(before[:, 256:], *k2) + dot3(after[:, 256:], *k2, NT)

    def coupled(pairs, lower, upper, high, low):
        sides = jnp.concatenate(
            [
                jnp.concatenate([lower, pairs[:-VECS]], 0) if pairs.shape[0] > VECS else lower,
                jnp.concatenate([pairs[VECS:], upper], 0) if pairs.shape[0] > VECS else upper,
            ],
            1,
        )
        return dot3(sides, high, low)

    sink = (sinkh_ref[...], sinkl_ref[...])
    local = coupled(p2_ref[...], left_ref[:, 1024:1152], right_ref[:, 1024:1152], m2h_ref[...], m2l_ref[...])
    local = coupled(
        p1_ref[...], left_ref[:, 896:1024], right_ref[:, 896:1024], m1h_ref[...], m1l_ref[...]
    ) + dot3(unpair_rows(local), *sink)
    local = coupled(
        p0_ref[...], left_ref[:, 768:896], right_ref[:, 768:896], m0h_ref[...], m0l_ref[...]
    ) + dot3(unpair_rows(local), *sink)
    inherited = dot3(unpair_rows(local), octh_ref[...], octl_ref[...], NT)
    even = even + inherited[:, :256]
    odd = odd + inherited[:, 256:]
    for s in range(CUBES):
        for part, values in ((0, even), (1, odd)):
            at = slice(512 * s + 256 * part, 512 * s + 256 * part + 256)
            high, low = spread_basis(basish_ref[:, at], basisl_ref[:, at])
            base_ref[:, at] += dot3(values[VECS * s : VECS * s + VECS], high, low)


def tail_kernel(index_ref, base_ref, occ_ref, high_ref, low_ref, boxes_ref, quad3_ref, quad5_ref,
                left3_ref, right3_ref, left5_ref, right5_ref, mh_ref, ml_ref, sinkh_ref, sinkl_ref,
                out_ref):
    index = index_ref[0]
    top = index // 16

    def box7(number):
        inside = ((number >= 0) & (number < 16)).astype(F32)
        safe = jnp.clip(number, 0, 15)
        return unpack_box(boxes_ref[pl.ds(safe ^ top, 1)][0]) * inside

    sink = (sinkh_ref[...], sinkl_ref[...])

    def lift(pairs):
        return pair_rows(dot3(pairs, *sink, NT))

    def level7(pair):
        return jnp.concatenate([box7(2 * pair), box7(2 * pair + 1)], 1)

    sides = {}
    for level, quad_ref, left_ref, right_ref in (
        (3, quad3_ref, left3_ref, right3_ref),
        (5, quad5_ref, left5_ref, right5_ref),
    ):
        is_low = index // (1 << (level - 2)) % 2 == 0
        left, right = left_ref[...], right_ref[...]
        sides[level] = jnp.concatenate(
            [
                jnp.where(is_low, left[:, :128], quad_ref[:, :128]),
                jnp.where(is_low, quad_ref[:, 128:], right[:, :128]),
            ],
            1,
        )
        sides[level + 1] = jnp.concatenate([left[:, 128:], right[:, 128:]], 1)
    pair7 = top // 2
    sides[7] = jnp.concatenate([level7(pair7 - 1), level7(pair7 + 1)], 1)
    pair8 = top // 4
    pairs = [level7(2 * (pair8 + side) + half) for side in (-1, 1) for half in (0, 1)]
    pair9 = 1 - top // 8
    pairs += [level7(4 * pair9 + quarter) for quarter in range(4)]
    lifted = lift(jnp.concatenate(pairs, 0))
    sides[8] = jnp.concatenate([lifted[:VECS], lifted[VECS : 2 * VECS]], 1)
    other = lift(lifted[2 * VECS :])
    is_upper = (pair9 == 0).astype(F32)
    sides[9] = jnp.concatenate([other * is_upper, other * (1.0 - is_upper)], 1)
    local = None
    for level in range(TOP - 1, 2, -1):
        far = dot3(sides[level], mh_ref[level - 3], ml_ref[level - 3])
        if local is not None:
            far = far + dot3(local, *sink)
        is_low = index // (1 << (level - 3)) % 2 == 0
        local = jnp.where(is_low, far[:, :64], far[:, 64:])
    out_ref[...] = (base_ref[...] + dot3(local, high_ref[...], low_ref[...])) * occ_ref[...]


VMEM = pl.BlockSpec(memory_space=pltpu.VMEM)
SMEM = pl.BlockSpec(memory_space=pltpu.SMEM)
ANY = pl.BlockSpec(memory_space=pl.ANY)


def call(body, in_specs, outs, scratch=(), aliases=None, name=None):
    return pl.pallas_call(
        body,
        out_shape=[jax.ShapeDtypeStruct(shape, dtype) for shape, dtype in outs],
        in_specs=in_specs,
        out_specs=[VMEM] * len(outs),
        scratch_shapes=list(scratch),
        input_output_aliases=aliases or {},
        compiler_params=pltpu.CompilerParams(vmem_limit_bytes=VMEM_LIMIT),
        name=name,
    )


def local(points, vectors, counts):
    devices = lax.axis_size(AXES)
    index = lax.axis_index(AXES).astype(jnp.int32)

    def crossed(value, mask):
        return lax.ppermute(value, AXES, [(i, i ^ mask) for i in range(devices)])

    def shifted(value, by):
        pairs = [(i, i + by) for i in range(devices) if 0 <= i + by < devices]
        return lax.ppermute(value, AXES, pairs)

    octants, along = transfer_tables()
    octants = hi_lo(octants)
    lift = hi_lo(along)
    sink = hi_lo(along.T)
    k2 = hi_lo(kernel_table(layer_nodes(0), layer_nodes(2)))
    k3 = hi_lo(kernel_table(layer_nodes(0), layer_nodes(3)))
    low_tables = [table for level in range(3) for table in hi_lo(pair_coupling(level))]
    high_tables = hi_lo(np.stack([pair_coupling(level) for level in range(3, TOP)]))

    coords, masked, occupied, box3, far_high, far_low = call(
        head_kernel,
        [SMEM, SMEM, VMEM, VMEM],
        [
            ((8, SLOTS), F32),
            ((VECS, SLOTS), F32),
            ((1, SLOTS), F32),
            ((16, 128), F32),
            ((64, SLOTS), BF16),
            ((64, SLOTS), BF16),
        ],
        name="head",
    )((index * CUBES)[None], counts, points, vectors)

    def gathered(box, bit, hold):
        others = [crossed(box, step << bit) for step in (1, 2, 3)]
        return call(
            gather_kernel,
            [SMEM] + [VMEM] * 6 + [ANY],
            [
                ((VECS, 256), F32),
                ((VECS, 128), F32),
                ((16, 128), F32),
                ((VECS, 256), F32),
                ((VECS, 256), F32),
            ],
            [pltpu.VMEM((4, VECS, 64), F32)],
            name="gather",
        )((index >> bit & 3)[None], box, *others, *lift, hold)

    def near_part(before, begin, end, hold):
        return call(
            functools.partial(near_kernel, begin, end),
            [VMEM] * 3 + [ANY],
            [((VECS, SLOTS), F32)],
            [pltpu.VMEM((256, 512), BF16), pltpu.VMEM((256, 512), BF16)],
            aliases={2: 0},
            name="near",
        )(coords, masked, before, hold)[0]

    coef, leaf_high, leaf_low, p0, p1, p2, ahead, behind = call(
        leaf_kernel,
        [VMEM] * 6,
        [
            ((VECS, SLOTS), F32),
            ((64, SLOTS), BF16),
            ((64, SLOTS), BF16),
            ((4 * VECS, 128), F32),
            ((2 * VECS, 128), F32),
            ((VECS, 128), F32),
            ((VECS, 1280), F32),
            ((VECS, 1280), F32),
        ],
        name="leaf",
    )(coords, masked, *octants, *lift)
    from_left = shifted(ahead, 1)
    from_right = shifted(behind, -1)
    quad3, _, box5, ahead3, behind3 = gathered(box3, 0, p2)
    left3 = shifted(ahead3, 4)
    right3 = shifted(behind3, -4)
    near = near_part(masked, 0, 5, quad3)
    quad5, _, box7, ahead5, behind5 = gathered(box5, 2, near)
    left5 = shifted(ahead5, 16)
    right5 = shifted(behind5, -16)
    near = near_part(near, 5, 9, quad5)
    boxes = jnp.stack([box7, crossed(box7, 16)])
    near = near_part(near, 9, 13, boxes)
    boxes = jnp.concatenate([boxes, crossed(boxes, 32)], 0)
    near = near_part(near, 13, 16, boxes)
    boxes = jnp.concatenate([boxes, crossed(boxes, 64)], 0)
    base = call(
        rim_kernel,
        [VMEM] * 25 + [ANY],
        [((VECS, SLOTS), F32)],
        [pltpu.VMEM((256, 256), BF16), pltpu.VMEM((256, 256), BF16)],
        aliases={2: 0},
        name="rim",
    )(
        coords, masked, near, coef, leaf_high, leaf_low, p0, p1, p2, from_left, from_right,
        *k2, *k3, *low_tables, *sink, *octants, boxes,
    )[0]
    boxes = jnp.concatenate([boxes, crossed(boxes, 128)], 0)
    return call(
        tail_kernel,
        [SMEM] + [VMEM] * 15,
        [((VECS, SLOTS), F32)],
        aliases={1: 0},
        name="tail",
    )(
        index[None], base, occupied, far_high, far_low, boxes, quad3, quad5, left3, right3, left5,
        right5, *high_tables, *sink,
    )[0]


def solution(mesh):
    in_specs = (P(None, AXES), P(None, AXES), P(AXES, None))
    return jax.shard_map(
        local, mesh=mesh, in_specs=in_specs, out_specs=P(None, AXES), check_vma=False
    )
```

time: 596 us -> 101 us (0.17)
  the two profiles are of different devices: /device:TPU:192 before, /device:TPU:224 now
where the time goes in v1:
time: 101 us; the launch traced here: 100 us
  Pallas kernels  43.3 us (43%)
  starting transfers between devices  37.5 us (37%)
  local copies, waits for them, and re-layouts  10.4 us (10%)
  waiting for transfers between devices  8.19 us (8%)
    ppermute x6, starting transfers between devices, shifted(): return lax.ppermute(value, AXES, pairs)  26 us
    pallas_call x4, Pallas kernels, near_part(): call(functools.partial(near_kernel, begin, end), [VMEM] * 3 + [ANY], [((V...  22.5 us
    ppermute x10, starting transfers between devices, crossed(): return lax.ppermute(value, AXES, [(i, i ^ mask) for i in range(devices)])  11.5 us
    unnamed x81, local copies, waits for them, and re-layouts  10.4 us
    ppermute x10, waiting for transfers between devices, crossed(): return lax.ppermute(value, AXES, [(i, i ^ mask) for i in range(devices)])  8.17 us
    pallas_call x1, Pallas kernels, local(): call(leaf_kernel, [VMEM] * 6, [((VECS, SLOTS), F32), ((64, SLOTS), BF16),...  5.18 us
    pallas_call x1, Pallas kernels, local(): call(rim_kernel, [VMEM] * 25 + [ANY], [((VECS, SLOTS), F32)], [pltpu.VMEM...  4.9 us
    pallas_call x1, Pallas kernels, local(): call(tail_kernel, [SMEM] + [VMEM] * 15, [((VECS, SLOTS), F32)], aliases={...  4.25 us
  transfers between devices with their start and end apart: 16, of which 1 were waited for; matrix products, arithmetic and copies ran while one was open for 1% of the time, Pallas kernels for 34%

profile of v1, /device:TPU:224, one launch (start us, length us, event | category | flops | bytes accessed | tf_op | source)
XLA Modules:
  0.0 100.0 jit_solution(6688696703432177491)
XLA Ops:
  0.0 0.7 copy-done.33
  0.7 1.0 %copy-done.3 = f32[32,4096]{1,0:T(8,128)S(1)} copy-done((f32[32,4096]{1,0:T(8,128)S(1)}, f32[32,4096]{1,0:T(8,128)}, u32[]{:S(2)}) %copy-start.3) | copy-done | bytes 524312
  1.7 0.8 copy-done.28
  2.6 3.0 %head.1 = (f32[8,4096]{1,0:T(8,128)S(1)}, f32[32,4096]{1,0:T(8,128)S(1)}, f32[1,4096]{1,0:T(1,128)S(1)}, f32[16,128]{1,0:T(8,128)}, bf16[64,4096]{1,0:T(8,128)(2,1)S(1)}, /*index=5*/bf16[64,4096]{1,0:T(8,128)(2,1)S(1)}) custom-call(s32[1]{0:T(128)} %bitcast.1.slab_ref, s32[8,8]{1,0:T(8,128)S(1)} %copy-done.33, f32[3,4096]{1,0:T(4,128)S(1)} %copy-done.28, ...), custom_call_target="tpu_custom_call" | custom-call | tf_op jit(solution)/shard_map/head/pallas_call | solution.py:507
  5.5 0.6 copy-done.31
  6.1 1.5 %collective-permute-start = (f32[16,128]{1,0:T(8,128)}, f32[16,128]{1,0:T(8,128)}, u32[]{:S(2)}, u32[]{:S(2)}) collective-permute-start(f32[16,128]{1,0:T(8,128)} %get-tuple-element.29.a_ref), channel_id=1, source_target_pairs={{0,1},{1,0},{2,3},{3,2},{4,5},{5,4},{6,7},{7,6},{8,9},{9,8},{10,11... | collective-permute-start | bytes 24584 | tf_op jit(solution)/shard_map/ppermute | solution.py:492
  7.6 2.7 %collective-permute-start.1 = (f32[16,128]{1,0:T(8,128)}, f32[16,128]{1,0:T(8,128)}, u32[]{:S(2)}, u32[]{:S(2)}) collective-permute-start(f32[16,128]{1,0:T(8,128)} %get-tuple-element.29.a_ref), channel_id=1, source_target_pairs={{0,2},{1,3},{2,0},{3,1},{4,6},{5,7},{6,4},{7,5},{8,10},{9,11},{10,... | collective-permute-start | bytes 24584 | tf_op jit(solution)/shard_map/ppermute | solution.py:492
  10.4 0.5 collective-permute-start.2
  10.8 0.8 copy-done.6
  11.6 0.8 copy-done.9
  12.4 5.2 %leaf.1 = (f32[32,4096]{1,0:T(8,128)S(1)}, bf16[64,4096]{1,0:T(8,128)(2,1)S(1)}, bf16[64,4096]{1,0:T(8,128)(2,1)S(1)}, f32[128,128]{1,0:T(8,128)S(1)}, f32[64,12...) custom-call(f32[8,4096]{1,0:T(8,128)S(1)} %get-tuple-element.27.coords_ref, ...), custom_call_target="tpu_custom_call" | custom-call | tf_op jit(solution)/shard_map/leaf/pallas_call | solution.py:547
  17.5 0.6 copy-done.24
  18.2 0.6 copy-done.29
  18.8 0.0 collective-permute-done.b_ref
  18.8 0.0 collective-permute-done.1.c_ref
  18.8 0.0 collective-permute-done.2.d_ref
  18.8 1.9 %gather.2 = (f32[32,256]{1,0:T(8,128)S(1)}, f32[32,128]{1,0:T(8,128)}, f32[16,128]{1,0:T(8,128)}, f32[32,256]{1,0:T(8,128)S(1)}, f32[32,256]{1,0:T(8,128)S(1)}) custom-call(s32[1]{0:T(128)} %bitcast.2.member_ref, f32[16,128]{1,0:T(8,128)} %get-tuple-element.29.a_ref, f32[16,128]{1,0:T(8,128)} %collective-permute-done.b_ref, ...), custom_call_target="tpu_custom_call" | custom-call | tf_op jit(solution)/shard_map/gather/pallas_call | solution.py:523
  20.7 0.6 copy-done.11
  21.3 0.6 copy-done.34
  21.9 0.6 copy-done.36
  22.5 0.0 collective-permute-start.3
  22.5 1.6 %collective-permute-start.4 = (f32[16,128]{1,0:T(8,128)}, f32[16,128]{1,0:T(8,128)}, u32[]{:S(2)}, u32[]{:S(2)}) collective-permute-start(f32[16,128]{1,0:T(8,128)} %get-tuple-element.32.a_ref), channel_id=1, source_target_pairs={{0,8},{1,9},{2,10},{3,11},{4,12},{5,13},{6,14},{7,15},{8,0},{9,1},... | collective-permute-start | bytes 24584 | tf_op jit(solution)/shard_map/ppermute | solution.py:492
  24.1 0.3 collective-permute-start.5
  24.4 2.2 %collective-permute-start.8 = (f32[32,1280]{1,0:T(8,128)}, f32[32,1280]{1,0:T(8,128)}, u32[]{:S(2)}, u32[]{:S(2)}) collective-permute-start(f32[32,1280]{1,0:T(8,128)} %get-tuple-element.40), channel_id=1, source_target_pairs={{0,1},{1,2},{2,3},{3,4},{4,5},{5,6},{6,7},{7,8},{8,9},{9,10},{10,1... | collective-permute-start | bytes 491528 | tf_op jit(solution)/shard_map/ppermute | solution.py:496
  26.5 7.6 %collective-permute-start.9 = (f32[32,1280]{1,0:T(8,128)}, f32[32,1280]{1,0:T(8,128)}, u32[]{:S(2)}, u32[]{:S(2)}) collective-permute-start(f32[32,1280]{1,0:T(8,128)} %get-tuple-element.41), channel_id=1, source_target_pairs={{1,0},{2,1},{3,2},{4,3},{5,4},{6,5},{7,6},{8,7},{9,8},{10,9},{11,1... | collective-permute-start | bytes 491528 | tf_op jit(solution)/shard_map/ppermute | solution.py:496
  34.1 0.8 copy.28.before_ref
  34.9 0.8 copy-done.12
  35.7 6.6 %near.4.hold_ref.before_ref = f32[32,4096]{1,0:T(8,128)} custom-call(f32[8,4096]{1,0:T(8,128)S(1)} %get-tuple-element.27.coords_ref, f32[32,4096]{1,0:T(8,128)S(1)} %get-tuple-element.28.masked_ref, f32[32,4096]{1,0:T(8,128)} %copy.28.before_ref, f32[32,256]{1,0:T(8,128)S(1)} %copy-done.12), custom_call_target="tpu_custom_call", output_to_operand_aliasing={{}: (2, {})} | custom-call | tf_op jit(solution)/shard_map/near/pallas_call | solution.py:538
  42.3 0.0 collective-permute-done.3.b_ref
  42.3 1.9 %collective-permute-start.12 = (f32[32,256]{1,0:T(8,128)S(1)}, f32[32,256]{1,0:T(8,128)S(1)}, u32[]{:S(2)}, u32[]{:S(2)}) collective-permute-start(f32[32,256]{1,0:T(8,128)S(1)} %copy-done.37), channel_id=1, source_target_pairs={{0,4},{1,5},{2,6},{3,7},{4,8},{5,9},{6,10},{7,11},{8,12},{9,13},{1... | collective-permute-start | bytes 98312 | tf_op jit(solution)/shard_map/ppermute | solution.py:496
  44.2 0.0 collective-permute-done.4.c_ref
  44.3 5.8 %collective-permute-start.13 = (f32[32,256]{1,0:T(8,128)S(1)}, f32[32,256]{1,0:T(8,128)S(1)}, u32[]{:S(2)}, u32[]{:S(2)}) collective-permute-start(f32[32,256]{1,0:T(8,128)S(1)} %copy-done.35), channel_id=1, source_target_pairs={{4,0},{5,1},{6,2},{7,3},{8,4},{9,5},{10,6},{11,7},{12,8},{13,9},{1... | collective-permute-start | bytes 98312 | tf_op jit(solution)/shard_map/ppermute | solution.py:496
  50.0 0.0 collective-permute-done.5.d_ref
  50.1 0.0 copy-start
  50.1 1.0 %copy-done = f32[32,4096]{1,0:T(8,128)S(1)} copy-done((f32[32,4096]{1,0:T(8,128)S(1)}, f32[32,4096]{1,0:T(8,128)}, u32[]{:S(2)}) %copy-start) | copy-done | bytes 524312
  51.1 1.7 %gather.3 = (f32[32,256]{1,0:T(8,128)S(1)}, f32[32,128]{1,0:T(8,128)}, f32[16,128]{1,0:T(8,128)S(1)}, f32[32,256]{1,0:T(8,128)S(1)}, f32[32,256]{1,0:T(8,128)S(1)}) custom-call(s32[1]{0:T(128)} %bitcast.3.member_ref, f32[16,128]{1,0:T(8,128)} %get-tuple-element.32.a_ref, f32[16,128]{1,0:T(8,128)} %collective-permute-done.3.b_ref, ...), custom_call_target="tpu_custom_call" | custom-call | tf_op jit(solution)/shard_map/gather/pallas_call | solution.py:523
  52.8 5.6 %near.5.before_ref = f32[32,4096]{1,0:T(8,128)} custom-call(f32[8,4096]{1,0:T(8,128)S(1)} %get-tuple-element.27.coords_ref, f32[32,4096]{1,0:T(8,128)S(1)} %get-tuple-element.28.masked_ref, f32[32,4096]{1,0:T(8,128)} %near.4.hold_ref.before_ref, f32[32,256]{1,0:T(8,128)S(1)} %get-tuple-element.33.hold_ref.quad5_ref), custom_call_target="tpu_custom_call", output_to_operand_aliasing={{}: (2, {})} | custom-call | tf_op jit(solution)/shard_map/near/pallas_call | solution.py:538
  58.4 0.0 collective-permute-done.6
  58.5 1.0 %collective-permute-start.7 = (f32[2,16,128]{2,1,0:T(8,128)S(1)}, f32[2,16,128]{2,1,0:T(8,128)S(1)}, u32[]{:S(2)}, u32[]{:S(2)}) collective-permute-start(f32[2,16,128]{2,1,0:T(8,128)S(1)} %pad_maximum_fusion.2.hold_ref), channel_id=1, source_target_pairs={{0,32},{1,33},{2,34},{3,35},{4,36},{5,37},{6,38},{7,39},{8,40},{9,... | collective-permute-start | bytes 49160 | tf_op jit(solution)/shard_map/ppermute | solution.py:492
  59.5 5.6 %near.6.before_ref = f32[32,4096]{1,0:T(8,128)} custom-call(f32[8,4096]{1,0:T(8,128)S(1)} %get-tuple-element.27.coords_ref, f32[32,4096]{1,0:T(8,128)S(1)} %get-tuple-element.28.masked_ref, f32[32,4096]{1,0:T(8,128)} %near.5.before_ref, f32[2,16,128]{2,1,0:T(8,128)S(1)} %pad_maximum_fusion.2.hold_ref), custom_call_target="tpu_custom_call", output_to_operand_aliasing={{}: (2, {})} | custom-call | tf_op jit(solution)/shard_map/near/pallas_call | solution.py:538
  65.1 3.9 %collective-permute-start.10 = (f32[4,16,128]{2,1,0:T(8,128)S(1)}, f32[4,16,128]{2,1,0:T(8,128)S(1)}, u32[]{:S(2)}, u32[]{:S(2)}) collective-permute-start(f32[4,16,128]{2,1,0:T(8,128)S(1)} %pad_maximum_fusion.1.hold_ref), channel_id=1, source_target_pairs={{0,64},{1,65},{2,66},{3,67},{4,68},{5,69},{6,70},{7,71},{8,72},{9,... | collective-permute-start | bytes 98312 | tf_op jit(solution)/shard_map/ppermute | solution.py:492
  69.0 0.0 copy-start.20
  69.0 0.0 copy-start.21
  69.0 0.0 copy-start.22
  69.0 0.0 copy-start.23
  69.1 0.0 copy-start.26
  69.1 0.0 copy-start.27
  69.1 4.6 %near.7.near_ref = f32[32,4096]{1,0:T(8,128)} custom-call(f32[8,4096]{1,0:T(8,128)S(1)} %get-tuple-element.27.coords_ref, f32[32,4096]{1,0:T(8,128)S(1)} %get-tuple-element.28.masked_ref, f32[32,4096]{1,0:T(8,128)} %near.6.before_ref, f32[4,16,128]{2,1,0:T(8,128)S(1)} %pad_maximum_fusion.1.hold_ref), custom_call_target="tpu_custom_call", output_to_operand_aliasing={{}: (2, {})} | custom-call | tf_op jit(solution)/shard_map/near/pallas_call | solution.py:538
  73.7 0.0 collective-permute-done.10
  73.7 0.0 copy-start.14
  73.7 0.1 collective-permute-start.11
  73.8 8.1 %collective-permute-done.11 = f32[8,16,128]{2,1,0:T(8,128)S(1)} collective-permute-done((f32[8,16,128]{2,1,0:T(8,128)S(1)}, f32[8,16,128]{2,1,0:T(8,128)S(1)}, u32[]{:S(2)}, u32[]{:S(2)}) %collective-permute-start.11) | collective-permute-done | bytes 65568 | tf_op jit(solution)/shard_map/ppermute | solution.py:492
  81.9 5.4 %collective-permute-start.14 = (f32[32,256]{1,0:T(8,128)S(1)}, f32[32,256]{1,0:T(8,128)S(1)}, u32[]{:S(2)}, u32[]{:S(2)}) collective-permute-start(f32[32,256]{1,0:T(8,128)S(1)} %get-tuple-element.47), channel_id=1, source_target_pairs={{0,16},{1,17},{2,18},{3,19},{4,20},{5,21},{6,22},{7,23},{8,24},{9,... | collective-permute-start | bytes 98312 | tf_op jit(solution)/shard_map/ppermute | solution.py:496
  87.4 0.0 copy-start.18
  87.4 3.1 %collective-permute-start.15 = (f32[32,256]{1,0:T(8,128)S(1)}, f32[32,256]{1,0:T(8,128)S(1)}, u32[]{:S(2)}, u32[]{:S(2)}) collective-permute-start(f32[32,256]{1,0:T(8,128)S(1)} %get-tuple-element.48), channel_id=1, source_target_pairs={{16,0},{17,1},{18,2},{19,3},{20,4},{21,5},{22,6},{23,7},{24,8},{25... | collective-permute-start | bytes 98312 | tf_op jit(solution)/shard_map/ppermute | solution.py:496
  90.5 0.0 collective-permute-done.9.right_ref
  90.7 0.0 copy-start.4
  90.7 0.0 copy-start.5
  90.7 4.9 %rim.1.base_ref = f32[32,4096]{1,0:T(8,128)} custom-call(f32[8,4096]{1,0:T(8,128)S(1)} %get-tuple-element.27.coords_ref, f32[32,4096]{1,0:T(8,128)S(1)} %get-tuple-element.28.masked_ref, f32[32,4096]{1,0:T(8,128)} %near.7.near_ref, f32[32,4096]{1,0:T(8,128)S(1)} %get-tuple-element.35.coef_ref, ...), custom_call_target="tpu_custom_call", output_to_operand_aliasing={{}: (2, {})} | custom-call | tf_op jit(solution)/shard_map/rim/pallas_call | solution.py:577
  95.6 0.0 collective-permute-done.12.left3_ref
  95.6 0.0 collective-permute-done.13.right3_ref
  95.6 0.0 collective-permute-done.14.left5_ref
  95.7 0.0 collective-permute-done.15.right5_ref
  95.7 4.2 %tail.1 = f32[32,4096]{1,0:T(8,128)} custom-call(s32[1]{0:T(128)} %bitcast.index_ref, f32[32,4096]{1,0:T(8,128)} %rim.1.base_ref, f32[1,4096]{1,0:T(1,128)S(1)} %copy-done.32, bf16[64,4096]{1,0:T(8,128)(2,1)S(1)} %get-tuple-element.43.high_ref, bf16[64,4096]{1,0:T(8,128)(2,1)S(1)} %get-tuple-element.44.low_ref, ...), custom_call_target="tpu_custom_call", output_to_operand_aliasing={{}: (1, {})} | custom-call | tf_op jit(solution)/shard_map/tail/pallas_call | solution.py:589
  (63 shorter events, 0.1 us)
Async XLA Ops:
  0.0 0.7 copy-start.33
  0.7 1.0 %copy-start.3 = (f32[32,4096]{1,0:T(8,128)S(1)}, f32[32,4096]{1,0:T(8,128)}, u32[]{:S(2)}) copy-start(f32[32,4096]{1,0:T(8,128)} %vectors_ref.1) | copy-start | bytes 1572868
  1.7 0.8 copy-start.28
  2.6 8.3 %copy-start.1 = (bf16[512,64]{1,0:T(8,128)(2,1)S(1)}, bf16[512,64]{1,0:T(8,128)(2,1)}, u32[]{:S(2)}) copy-start(bf16[512,64]{1,0:T(8,128)(2,1)} %constant.55.clone.octh_ref) | copy-start | bytes 196612
  2.6 8.3 %copy-start.2 = (bf16[512,64]{1,0:T(8,128)(2,1)S(1)}, bf16[512,64]{1,0:T(8,128)(2,1)}, u32[]{:S(2)}) copy-start(bf16[512,64]{1,0:T(8,128)(2,1)} %constant.56.clone.octl_ref) | copy-start | bytes 196612
  5.5 0.6 copy-start.31
  6.1 12.6 %collective-permute-start = (f32[16,128]{1,0:T(8,128)}, f32[16,128]{1,0:T(8,128)}, u32[]{:S(2)}, u32[]{:S(2)}) collective-permute-start(f32[16,128]{1,0:T(8,128)} %get-tuple-element.29.a_ref), channel_id=1, source_target_pairs={{0,1},{1,0},{2,3},{3,2},{4,5},{5,4},{6,7},{7,6},{8,9},{9,8},{10,11... | collective-permute-start | bytes 24584 | tf_op jit(solution)/shard_map/ppermute | solution.py:492
  7.6 11.1 %collective-permute-start.1 = (f32[16,128]{1,0:T(8,128)}, f32[16,128]{1,0:T(8,128)}, u32[]{:S(2)}, u32[]{:S(2)}) collective-permute-start(f32[16,128]{1,0:T(8,128)} %get-tuple-element.29.a_ref), channel_id=1, source_target_pairs={{0,2},{1,3},{2,0},{3,1},{4,6},{5,7},{6,4},{7,5},{8,10},{9,11},{10,... | collective-permute-start | bytes 24584 | tf_op jit(solution)/shard_map/ppermute | solution.py:492
  10.4 8.4 %collective-permute-start.2 = (f32[16,128]{1,0:T(8,128)}, f32[16,128]{1,0:T(8,128)}, u32[]{:S(2)}, u32[]{:S(2)}) collective-permute-start(f32[16,128]{1,0:T(8,128)} %get-tuple-element.29.a_ref), channel_id=1, source_target_pairs={{0,3},{1,2},{2,1},{3,0},{4,7},{5,6},{6,5},{7,4},{8,11},{9,10},{10,... | collective-permute-start | bytes 24584 | tf_op jit(solution)/shard_map/ppermute | solution.py:492
  10.8 0.8 copy-start.6
  11.6 0.8 copy-start.9
  12.4 6.4 %copy-start.7 = (bf16[128,64]{1,0:T(8,128)(2,1)S(1)}, bf16[128,64]{1,0:T(8,128)(2,1)}, u32[]{:S(2)}) copy-start(bf16[128,64]{1,0:T(8,128)(2,1)} %constant.57.clone.lifth_ref) | copy-start | bytes 49156
  17.5 0.6 copy-start.24
  18.2 0.6 copy-start.29
  20.7 0.6 copy-start.11
  21.3 0.6 copy-start.34
  21.9 0.6 copy-start.36
  22.5 19.8 %collective-permute-start.3 = (f32[16,128]{1,0:T(8,128)}, f32[16,128]{1,0:T(8,128)}, u32[]{:S(2)}, u32[]{:S(2)}) collective-permute-start(f32[16,128]{1,0:T(8,128)} %get-tuple-element.32.a_ref), channel_id=1, source_target_pairs={{0,4},{1,5},{2,6},{3,7},{4,0},{5,1},{6,2},{7,3},{8,12},{9,13},{10,... | collective-permute-start | bytes 24584 | tf_op jit(solution)/shard_map/ppermute | solution.py:492
  22.5 21.8 %collective-permute-start.4 = (f32[16,128]{1,0:T(8,128)}, f32[16,128]{1,0:T(8,128)}, u32[]{:S(2)}, u32[]{:S(2)}) collective-permute-start(f32[16,128]{1,0:T(8,128)} %get-tuple-element.32.a_ref), channel_id=1, source_target_pairs={{0,8},{1,9},{2,10},{3,11},{4,12},{5,13},{6,14},{7,15},{8,0},{9,1},... | collective-permute-start | bytes 24584 | tf_op jit(solution)/shard_map/ppermute | solution.py:492
  24.1 26.0 %collective-permute-start.5 = (f32[16,128]{1,0:T(8,128)}, f32[16,128]{1,0:T(8,128)}, u32[]{:S(2)}, u32[]{:S(2)}) collective-permute-start(f32[16,128]{1,0:T(8,128)} %get-tuple-element.32.a_ref), channel_id=1, source_target_pairs={{0,12},{1,13},{2,14},{3,15},{4,8},{5,9},{6,10},{7,11},{8,4},{9,5},... | collective-permute-start | bytes 24584 | tf_op jit(solution)/shard_map/ppermute | solution.py:492
  24.4 63.0 %collective-permute-start.8 = (f32[32,1280]{1,0:T(8,128)}, f32[32,1280]{1,0:T(8,128)}, u32[]{:S(2)}, u32[]{:S(2)}) collective-permute-start(f32[32,1280]{1,0:T(8,128)} %get-tuple-element.40), channel_id=1, source_target_pairs={{0,1},{1,2},{2,3},{3,4},{4,5},{5,6},{6,7},{7,8},{8,9},{9,10},{10,1... | collective-permute-start | bytes 491528 | tf_op jit(solution)/shard_map/ppermute | solution.py:496
  26.5 64.0 %collective-permute-start.9 = (f32[32,1280]{1,0:T(8,128)}, f32[32,1280]{1,0:T(8,128)}, u32[]{:S(2)}, u32[]{:S(2)}) collective-permute-start(f32[32,1280]{1,0:T(8,128)} %get-tuple-element.41), channel_id=1, source_target_pairs={{1,0},{2,1},{3,2},{4,3},{5,4},{6,5},{7,6},{8,7},{9,8},{10,9},{11,1... | collective-permute-start | bytes 491528 | tf_op jit(solution)/shard_map/ppermute | solution.py:496
  34.9 0.8 copy-start.12
  35.7 6.6 %copy-start.37 = (f32[32,256]{1,0:T(8,128)S(1)}, f32[32,256]{1,0:T(8,128)}, u32[]{:S(2)}) copy-start(f32[32,256]{1,0:T(8,128)} %copy-done.36) | copy-start | bytes 98308
  35.7 8.6 %copy-start.35 = (f32[32,256]{1,0:T(8,128)S(1)}, f32[32,256]{1,0:T(8,128)}, u32[]{:S(2)}) copy-start(f32[32,256]{1,0:T(8,128)} %copy-done.34) | copy-start | bytes 98308
  35.7 14.3 %copy-start.8 = (bf16[128,64]{1,0:T(8,128)(2,1)S(1)}, bf16[128,64]{1,0:T(8,128)(2,1)}, u32[]{:S(2)}) copy-start(bf16[128,64]{1,0:T(8,128)(2,1)} %constant.57.clone.lifth_ref) | copy-start | bytes 49156
  35.7 14.3 %copy-start.10 = (bf16[128,64]{1,0:T(8,128)(2,1)S(1)}, bf16[128,64]{1,0:T(8,128)(2,1)}, u32[]{:S(2)}) copy-start(bf16[128,64]{1,0:T(8,128)(2,1)} %constant.58.clone.liftl_ref) | copy-start | bytes 49156
  42.3 53.3 %collective-permute-start.12 = (f32[32,256]{1,0:T(8,128)S(1)}, f32[32,256]{1,0:T(8,128)S(1)}, u32[]{:S(2)}, u32[]{:S(2)}) collective-permute-start(f32[32,256]{1,0:T(8,128)S(1)} %copy-done.37), channel_id=1, source_target_pairs={{0,4},{1,5},{2,6},{3,7},{4,8},{5,9},{6,10},{7,11},{8,12},{9,13},{1... | collective-permute-start | bytes 98312 | tf_op jit(solution)/shard_map/ppermute | solution.py:496
  44.3 51.4 %collective-permute-start.13 = (f32[32,256]{1,0:T(8,128)S(1)}, f32[32,256]{1,0:T(8,128)S(1)}, u32[]{:S(2)}, u32[]{:S(2)}) collective-permute-start(f32[32,256]{1,0:T(8,128)S(1)} %copy-done.35), channel_id=1, source_target_pairs={{4,0},{5,1},{6,2},{7,3},{8,4},{9,5},{10,6},{11,7},{12,8},{13,9},{1... | collective-permute-start | bytes 98312 | tf_op jit(solution)/shard_map/ppermute | solution.py:496
  50.1 1.0 %copy-start = (f32[32,4096]{1,0:T(8,128)S(1)}, f32[32,4096]{1,0:T(8,128)}, u32[]{:S(2)}) copy-start(f32[32,4096]{1,0:T(8,128)} %near.4.hold_ref.before_ref) | copy-start | bytes 1572868
  52.8 5.6 %collective-permute-start.6 = (f32[16,128]{1,0:T(8,128)S(1)}, f32[16,128]{1,0:T(8,128)S(1)}, u32[]{:S(2)}, u32[]{:S(2)}) collective-permute-start(f32[16,128]{1,0:T(8,128)S(1)} %get-tuple-element.34), channel_id=1, source_target_pairs={{0,16},{1,17},{2,18},{3,19},{4,20},{5,21},{6,22},{7,23},{8,24},{9,... | collective-permute-start | bytes 24584 | tf_op jit(solution)/shard_map/ppermute | solution.py:492
  58.5 6.7 %collective-permute-start.7 = (f32[2,16,128]{2,1,0:T(8,128)S(1)}, f32[2,16,128]{2,1,0:T(8,128)S(1)}, u32[]{:S(2)}, u32[]{:S(2)}) collective-permute-start(f32[2,16,128]{2,1,0:T(8,128)S(1)} %pad_maximum_fusion.2.hold_ref), channel_id=1, source_target_pairs={{0,32},{1,33},{2,34},{3,35},{4,36},{5,37},{6,38},{7,39},{8,40},{9,... | collective-permute-start | bytes 49160 | tf_op jit(solution)/shard_map/ppermute | solution.py:492
  65.1 8.5 %collective-permute-start.10 = (f32[4,16,128]{2,1,0:T(8,128)S(1)}, f32[4,16,128]{2,1,0:T(8,128)S(1)}, u32[]{:S(2)}, u32[]{:S(2)}) collective-permute-start(f32[4,16,128]{2,1,0:T(8,128)S(1)} %pad_maximum_fusion.1.hold_ref), channel_id=1, source_target_pairs={{0,64},{1,65},{2,66},{3,67},{4,68},{5,69},{6,70},{7,71},{8,72},{9,... | collective-permute-start | bytes 98312 | tf_op jit(solution)/shard_map/ppermute | solution.py:492
  69.0 21.6 %copy-start.16 = (bf16[256,256]{1,0:T(8,128)(2,1)S(1)}, bf16[256,256]{1,0:T(8,128)(2,1)}, u32[]{:S(2)}) copy-start(bf16[256,256]{1,0:T(8,128)(2,1)} %constant.63.clone.k3h_ref) | copy-start | bytes 393220
  69.0 21.6 %copy-start.17 = (bf16[256,256]{1,0:T(8,128)(2,1)S(1)}, bf16[256,256]{1,0:T(8,128)(2,1)}, u32[]{:S(2)}) copy-start(bf16[256,256]{1,0:T(8,128)(2,1)} %constant.64.clone.k3l_ref) | copy-start | bytes 393220
  69.0 21.6 %copy-start.19 = (bf16[256,128]{1,0:T(8,128)(2,1)S(1)}, bf16[256,128]{1,0:T(8,128)(2,1)}, u32[]{:S(2)}) copy-start(bf16[256,128]{1,0:T(8,128)(2,1)} %constant.66.clone.m0l_ref) | copy-start | bytes 196612
  69.0 21.6 %copy-start.20 = (bf16[256,128]{1,0:T(8,128)(2,1)S(1)}, bf16[256,128]{1,0:T(8,128)(2,1)}, u32[]{:S(2)}) copy-start(bf16[256,128]{1,0:T(8,128)(2,1)} %constant.67.clone.m1h_ref) | copy-start | bytes 196612
  69.0 21.6 %copy-start.21 = (bf16[256,128]{1,0:T(8,128)(2,1)S(1)}, bf16[256,128]{1,0:T(8,128)(2,1)}, u32[]{:S(2)}) copy-start(bf16[256,128]{1,0:T(8,128)(2,1)} %constant.68.clone.m1l_ref) | copy-start | bytes 196612
  69.0 21.6 %copy-start.22 = (bf16[256,128]{1,0:T(8,128)(2,1)S(1)}, bf16[256,128]{1,0:T(8,128)(2,1)}, u32[]{:S(2)}) copy-start(bf16[256,128]{1,0:T(8,128)(2,1)} %constant.69.clone.m2h_ref) | copy-start | bytes 196612
  69.0 21.6 %copy-start.23 = (bf16[256,128]{1,0:T(8,128)(2,1)S(1)}, bf16[256,128]{1,0:T(8,128)(2,1)}, u32[]{:S(2)}) copy-start(bf16[256,128]{1,0:T(8,128)(2,1)} %constant.70.clone.m2l_ref) | copy-start | bytes 196612
  69.1 21.6 %copy-start.25 = (f32[128,128]{1,0:T(8,128)S(1)}, f32[128,128]{1,0:T(8,128)}, u32[]{:S(2)}) copy-start(f32[128,128]{1,0:T(8,128)} %copy-done.24) | copy-start | bytes 196612
  69.1 21.6 %copy-start.26 = (bf16[64,128]{1,0:T(8,128)(2,1)S(1)}, bf16[64,128]{1,0:T(8,128)(2,1)}, u32[]{:S(2)}) copy-start(bf16[64,128]{1,0:T(8,128)(2,1)} %constant.59.clone.sinkh_ref) | copy-start | bytes 49156
  69.1 21.6 %copy-start.27 = (bf16[64,128]{1,0:T(8,128)(2,1)S(1)}, bf16[64,128]{1,0:T(8,128)(2,1)}, u32[]{:S(2)}) copy-start(bf16[64,128]{1,0:T(8,128)(2,1)} %constant.60.clone.sinkl_ref) | copy-start | bytes 49156
  69.1 21.6 %copy-start.30 = (f32[64,128]{1,0:T(8,128)S(1)}, f32[64,128]{1,0:T(8,128)}, u32[]{:S(2)}) copy-start(f32[64,128]{1,0:T(8,128)} %copy-done.29) | copy-start | bytes 98308
  73.7 17.0 %copy-start.15 = (bf16[256,256]{1,0:T(8,128)(2,1)S(1)}, bf16[256,256]{1,0:T(8,128)(2,1)}, u32[]{:S(2)}) copy-start(bf16[256,256]{1,0:T(8,128)(2,1)} %constant.62.clone.k2l_ref) | copy-start | bytes 393220
  73.7 17.0 %copy-start.14 = (bf16[256,256]{1,0:T(8,128)(2,1)S(1)}, bf16[256,256]{1,0:T(8,128)(2,1)}, u32[]{:S(2)}) copy-start(bf16[256,256]{1,0:T(8,128)(2,1)} %constant.61.clone.k2h_ref) | copy-start | bytes 393220
  73.7 8.3 %collective-permute-start.11 = (f32[8,16,128]{2,1,0:T(8,128)S(1)}, f32[8,16,128]{2,1,0:T(8,128)S(1)}, u32[]{:S(2)}, u32[]{:S(2)}) collective-permute-start(f32[8,16,128]{2,1,0:T(8,128)S(1)} %pad_maximum_fusion.hold_ref), channel_id=1, source_target_pairs={{0,128},{1,129},{2,130},{3,131},{4,132},{5,133},{6,134},{7,135},{8... | collective-permute-start | bytes 196616 | tf_op jit(solution)/shard_map/ppermute | solution.py:492
  81.9 13.7 %collective-permute-start.14 = (f32[32,256]{1,0:T(8,128)S(1)}, f32[32,256]{1,0:T(8,128)S(1)}, u32[]{:S(2)}, u32[]{:S(2)}) collective-permute-start(f32[32,256]{1,0:T(8,128)S(1)} %get-tuple-element.47), channel_id=1, source_target_pairs={{0,16},{1,17},{2,18},{3,19},{4,20},{5,21},{6,22},{7,23},{8,24},{9,... | collective-permute-start | bytes 98312 | tf_op jit(solution)/shard_map/ppermute | solution.py:496
  87.4 3.3 %copy-start.18 = (bf16[256,128]{1,0:T(8,128)(2,1)S(1)}, bf16[256,128]{1,0:T(8,128)(2,1)}, u32[]{:S(2)}) copy-start(bf16[256,128]{1,0:T(8,128)(2,1)} %constant.65.clone.m0h_ref) | copy-start | bytes 196612
  87.4 8.3 %collective-permute-start.15 = (f32[32,256]{1,0:T(8,128)S(1)}, f32[32,256]{1,0:T(8,128)S(1)}, u32[]{:S(2)}, u32[]{:S(2)}) collective-permute-start(f32[32,256]{1,0:T(8,128)S(1)} %get-tuple-element.48), channel_id=1, source_target_pairs={{16,0},{17,1},{18,2},{19,3},{20,4},{21,5},{22,6},{23,7},{24,8},{25... | collective-permute-start | bytes 98312 | tf_op jit(solution)/shard_map/ppermute | solution.py:496
  90.7 5.0 %copy-start.4 = (bf16[7,256,128]{2,1,0:T(8,128)(2,1)S(1)}, bf16[7,256,128]{2,1,0:T(8,128)(2,1)}, u32[]{:S(2)}) copy-start(bf16[7,256,128]{2,1,0:T(8,128)(2,1)} %constant.71.clone.mh_ref) | copy-start | bytes 1376260
  90.7 5.0 %copy-start.5 = (bf16[7,256,128]{2,1,0:T(8,128)(2,1)S(1)}, bf16[7,256,128]{2,1,0:T(8,128)(2,1)}, u32[]{:S(2)}) copy-start(bf16[7,256,128]{2,1,0:T(8,128)(2,1)} %constant.72.clone.ml_ref) | copy-start | bytes 1376260
  90.7 5.0 %copy-start.13 = (f32[32,256]{1,0:T(8,128)S(1)}, f32[32,256]{1,0:T(8,128)}, u32[]{:S(2)}) copy-start(f32[32,256]{1,0:T(8,128)} %copy-done.11) | copy-start | bytes 98308
  90.7 5.0 %copy-start.32 = (f32[1,4096]{1,0:T(1,128)S(1)}, f32[1,4096]{1,0:T(1,128)}, u32[]{:S(2)}) copy-start(f32[1,4096]{1,0:T(1,128)} %copy-done.31) | copy-start | bytes 49156

commit v2 on v1

v2 whole, which is shorter than its diff:
```python
import functools
import math

import jax
import jax.numpy as jnp
import ml_dtypes
import numpy as np
from jax import lax
from jax.experimental import pallas as pl
from jax.experimental.pallas import tpu as pltpu
from jax.sharding import PartitionSpec as P

ORDER = 4
VECS = 32
CUBES = 8
LAYERS = 16
SLOTS = 4096
TOP = 10
ROOT_THREE = math.sqrt(3.0)
AXES = ("leaf", "sub")
F32 = jnp.float32
BF16 = jnp.bfloat16
NN = (((1,), (0,)), ((), ()))
NT = (((1,), (1,)), ((), ()))
NODES = np.cos((2.0 * np.arange(ORDER) + 1.0) * np.pi / (2.0 * ORDER))
LENGTHS = [512.0, 64.0, 8.0, 1.0]
STRETCH = ROOT_THREE / math.log(2.0)
VMEM_LIMIT = 16 * 1024 * 1024


def lagrange_table(values):
    columns = []
    for anchor in range(ORDER):
        product = values * 0.0 + 1.0
        for against in range(ORDER):
            if against != anchor:
                product = product * (values - NODES[against]) / (NODES[anchor] - NODES[against])
        columns.append(product)
    return np.stack(columns, -1)


def grid_nodes():
    z, y, x = np.meshgrid(np.arange(ORDER), np.arange(ORDER), np.arange(ORDER), indexing="ij")
    return np.stack([NODES[x.ravel()], NODES[y.ravel()], NODES[z.ravel()]], -1)


def kernel_table(targets, sources):
    gaps = targets[:, None, :] - sources[None, :, :]
    distance = np.sqrt(np.sum(gaps * gaps, -1))
    total = distance * 0.0
    for length in LENGTHS:
        scaled = distance * (ROOT_THREE / length)
        total = total + (1.0 + scaled) * np.exp(-scaled) / (32.0 * math.sqrt(length))
    return total


def layer_nodes(layer):
    scaled = grid_nodes() * 0.25
    leaves = []
    for row in range(2):
        for column in range(2):
            centre = [(column + 0.5) * 0.5, (row + 0.5) * 0.5, (layer + 0.5) * 0.5]
            leaves.append(scaled + np.array(centre))
    return np.concatenate(leaves)


def pair_coupling(level):
    span = float(1 << level)
    nodes = grid_nodes() * np.array([0.5, 0.5, 0.5 * span])

    def block(offset):
        return kernel_table(nodes, nodes + np.array([0.0, 0.0, offset * span])).T

    zero = np.zeros((64, 64))
    before = np.block([[block(-2), block(-3)], [zero, block(-2)]])
    after = np.block([[block(2), zero], [block(3), block(2)]])
    return np.concatenate([before, after], 0)


def transfer_tables():
    halves = [lagrange_table(side + 0.5 * NODES) for side in (-0.5, 0.5)]
    eye = np.eye(ORDER)
    octants = [
        np.kron(np.kron(halves[z], halves[y]), halves[x])
        for z in range(2)
        for y in range(2)
        for x in range(2)
    ]
    along = [np.kron(np.kron(half, eye), eye) for half in halves]
    return np.concatenate(octants, 0), np.concatenate(along, 0)


def hi_lo(table):
    high = table.astype(ml_dtypes.bfloat16)
    low = (table - high.astype(np.float64)).astype(ml_dtypes.bfloat16)
    return np.stack([high, low])


def split(x):
    high = x.astype(BF16)
    return high, (x - high.astype(F32)).astype(BF16)


def mxu(a, b, dims=NN):
    return lax.dot_general(a, b, dims, preferred_element_type=F32)


def dot3(x, high, low, dims=NN):
    rows = x.shape[0]
    x_high, x_low = split(x)
    both = mxu(jnp.concatenate([x_high, x_low], 0), high, dims)
    return both[:rows] + both[rows:] + mxu(x_high, low, dims)


def poly4(u):
    gaps = [u - float(node) for node in NODES]
    polys = []
    for anchor in range(ORDER):
        scale = 1.0
        product = None
        for against in range(ORDER):
            if against != anchor:
                scale = scale / float(NODES[anchor] - NODES[against])
                product = gaps[against] if product is None else product * gaps[against]
        polys.append(product * scale)
    return polys


def basis64(u):
    count = u.shape[1]
    polys = poly4(u)
    row = lax.broadcasted_iota(jnp.int32, (16, count), 0)

    def picked(dim, key):
        rows = [jnp.broadcast_to(poly[dim : dim + 1], (16, count)) for poly in polys]
        low = jnp.where(key == 0, rows[0], rows[1])
        high = jnp.where(key == 2, rows[2], rows[3])
        return jnp.where(key < 2, low, high)

    plane = picked(0, row % 4) * picked(1, row // 4)
    return jnp.concatenate([plane * poly[2:3] for poly in polys], 0)


def stack_rows(x, width):
    return jnp.concatenate(
        [x[:, i * width : (i + 1) * width] for i in range(x.shape[1] // width)], 0
    )


def pair_rows(boxes):
    count = boxes.shape[0] // VECS
    parts = [boxes[i * VECS : (i + 1) * VECS] for i in range(count)]
    return jnp.concatenate(
        [jnp.concatenate(parts[i : i + 2], 1) for i in range(0, count, 2)], 0
    )


def unpair_rows(pairs):
    count = pairs.shape[0] // VECS
    parts = []
    for i in range(count):
        block = pairs[i * VECS : (i + 1) * VECS]
        parts += [block[:, :64], block[:, 64:]]
    return jnp.concatenate(parts, 0)


def pack_box(box):
    return jnp.concatenate([box[:16], box[16:]], 1)


def unpack_box(packed):
    return jnp.concatenate([packed[:, :64], packed[:, 64:]], 0)


def features(coords, origin):
    row = lax.broadcasted_iota(jnp.int32, coords.shape, 0)
    q = (coords - jnp.where(row == 2, origin, 0.0)) * STRETCH
    norm = jnp.sum(q * q, axis=0, keepdims=True)
    left = jnp.where(row == 3, norm, jnp.where(row == 4, 1.0, q))
    right = jnp.where(row == 3, 1.0, jnp.where(row == 4, norm, -2.0 * q))
    return left, right


def three_parts(x):
    first = x.astype(BF16).astype(F32)
    rest = x - first
    second = rest.astype(BF16).astype(F32)
    return first, second, rest - second


def left_side(left):
    f1, f2, f3 = three_parts(left)
    return jnp.concatenate([f1, f1, f2, f2, f1, f3], 0)


def right_side(right):
    g1, g2, g3 = three_parts(right)
    return jnp.concatenate([g1, g2, g1, g2, g3, g1], 0).astype(BF16)


def matern(squared):
    squared = jnp.maximum(squared, 1e-20)
    w = squared * lax.rsqrt(squared)
    total = None
    for length in LENGTHS:
        weight = 1.0 / (32.0 * math.sqrt(length))
        slope = weight * math.log(2.0) / length
        term = (weight + slope * w) * jnp.exp2(w * (-1.0 / length))
        total = term if total is None else total + term
    return total


def fill_weights(turned, sources, high_ref, low_ref, top=0, begin=0):
    rows, columns = turned.shape[0], sources.shape[1]
    step = 128
    for row in range(0, rows, step):
        values = matern(mxu(turned[row : row + step], sources))
        high, low = split(values)
        at = slice(top + row, top + row + step), slice(begin, begin + columns)
        high_ref[at] = high
        low_ref[at] = low


def turned_side(left):
    return jnp.transpose(left_side(left)).astype(BF16)


def head_kernel(slab_ref, counts_hbm, points_hbm, vectors_hbm, coords_ref, masked_ref, occ_ref,
                box_ref, high_ref, low_ref, counts_ref, points_ref, vectors_ref, sems):
    first = slab_ref[0].astype(F32)
    lane = lax.broadcasted_iota(jnp.int32, (1, 512), 1)
    row = lax.broadcasted_iota(jnp.int32, (8, 512), 0)
    copies = [
        pltpu.make_async_copy(counts_hbm, counts_ref, sems.at[0]),
        pltpu.make_async_copy(points_hbm, points_ref, sems.at[1]),
    ]
    half = SLOTS // 2
    for part in range(2):
        at = slice(part * half, part * half + half)
        copies.append(
            pltpu.make_async_copy(vectors_hbm.at[:, at], vectors_ref.at[:, at], sems.at[2 + part])
        )
    for copy in copies:
        copy.start()

    def cube(s, total):
        at = pl.ds(pl.multiple_of(s * 512, 512), 512)
        filled = jnp.zeros((1, 512), jnp.int32)
        for c in range(8):
            filled = jnp.where(lane // 64 == c, counts_ref[s, c], filled)
        occupied = (lane % 64 < filled).astype(F32)
        occ_ref[:, at] = occupied
        masked = vectors_ref[:, at] * occupied
        masked_ref[:, at] = masked
        points = points_ref[:, at]
        points = jnp.concatenate([points, jnp.zeros((5, 512), F32)], 0)
        shift = jnp.where(row == 2, first, jnp.where(row < 2, 0.5, 0.0))
        coords = points - shift
        coords_ref[:, at] = coords
        u = (coords - jnp.where(row == 2, 4.0, 0.0)) * jnp.where(row == 2, 0.25, 2.0)
        high, low = split(basis64(u))
        high_ref[:, at] = high
        low_ref[:, at] = low
        return total + dot3(masked, high, low, NT)

    for copy in copies[:3]:
        copy.wait()
    total = lax.fori_loop(0, CUBES // 2, cube, jnp.zeros((VECS, 64), F32))
    copies[3].wait()
    total = lax.fori_loop(CUBES // 2, CUBES, cube, total)
    box_ref[...] = pack_box(total)


def spread_basis(high, low):
    lane = lax.broadcasted_iota(jnp.int32, (1, 256), 1)
    highs, lows = [], []
    for leaf in range(4):
        mask = (lane // 64 == leaf).astype(F32).astype(BF16)
        highs.append(high * mask)
        lows.append(low * mask)
    return jnp.concatenate(highs, 0), jnp.concatenate(lows, 0)


def leaf_kernel(index_ref, coords_ref, masked_ref, octants_ref, sink_ref, coef_ref, high_ref,
                low_ref, pairs_ref, facing_ref, away_ref):
    lane = lax.broadcasted_iota(jnp.int32, (8, 256), 1)
    row = lax.broadcasted_iota(jnp.int32, (8, 256), 0)
    centre_x = jnp.where(lane // 64 % 2 == 0, -0.25, 0.25)
    centre_y = jnp.where(lane // 128 == 0, -0.25, 0.25)

    def layer(z, carry):
        at = pl.ds(pl.multiple_of(z * 256, 256), 256)
        centre_z = z.astype(F32) * 0.5 + 0.25
        centre = jnp.where(row == 0, centre_x, jnp.where(row == 1, centre_y, centre_z))
        u = (coords_ref[:, at] - centre) * 4.0
        high, low = split(basis64(u))
        high_ref[:, at] = high
        low_ref[:, at] = low
        wide_high, wide_low = spread_basis(high, low)
        coef_ref[:, at] = dot3(masked_ref[:, at], wide_high, wide_low, NT)
        return carry

    lax.fori_loop(0, LAYERS, layer, 0)
    boxes = dot3(stack_rows(coef_ref[...], 512), octants_ref[0], octants_ref[1], NT)
    p0 = pair_rows(boxes)
    p1 = pair_rows(dot3(p0, sink_ref[0], sink_ref[1], NT))
    p2 = pair_rows(dot3(p1, sink_ref[0], sink_ref[1], NT))
    pairs_ref[...] = jnp.concatenate([p0, p1, p2], 0)

    def bundle(ref, near, far, low_pair, mid_pair):
        ref[:, 0:256] = masked_ref[:, near : near + 256]
        ref[:, 256:768] = coef_ref[:, far : far + 512]
        ref[:, 768:896] = low_pair
        ref[:, 896:1024] = mid_pair
        ref[:, 1024:1152] = p2
        ref[:, 1152:1280] = jnp.zeros((VECS, 128), F32)
        ref[0:8, 1152:1280] = coords_ref[:, near : near + 128]
        ref[8:16, 1152:1280] = coords_ref[:, near + 128 : near + 256]

    is_even = index_ref[0] % 2 == 0

    @pl.when(is_even)
    def _():
        bundle(facing_ref, SLOTS - 256, SLOTS - 512, p0[96:], p1[32:])
        bundle(away_ref, 0, 0, p0[:32], p1[:32])

    @pl.when(jnp.logical_not(is_even))
    def _():
        bundle(away_ref, SLOTS - 256, SLOTS - 512, p0[96:], p1[32:])
        bundle(facing_ref, 0, 0, p0[:32], p1[:32])


def near_kernel(begin, end, coords_ref, masked_ref, hold_ref, near_ref, own_high, own_low,
                next_high, next_low, turned_ref):
    del hold_ref
    near_ref[...] = jnp.zeros_like(near_ref)

    def out(z):
        return pl.ds(pl.multiple_of((z - begin) * 256, 256), 256)

    def lanes(z):
        return pl.ds(pl.multiple_of(z * 256, 256), 256)

    def top_of(z):
        return jnp.asarray(z, F32) * 0.5 + 0.5

    def fill_own(z):
        left, right = features(coords_ref[:, lanes(z)], top_of(z))
        turned = turned_side(left)
        turned_ref[...] = turned
        sources = right_side(right)
        fill_weights(turned[:128], sources, own_high, own_low)
        fill_weights(turned[128:], sources[:, 128:], own_high, own_low, 128, 128)

    def fill_next(z):
        _, right = features(coords_ref[:, lanes(z + 1)], top_of(z))
        fill_weights(turned_ref[...], right_side(right), next_high, next_low)

    def add_own(z):
        x = masked_ref[:, lanes(z)]
        both = dot3(x[:, :128], own_high[:128], own_low[:128])
        first = dot3(x[:, 128:], own_high[:128, 128:], own_low[:128, 128:], NT)
        second = dot3(x[:, 128:], own_high[128:, 128:], own_low[128:, 128:])
        near_ref[:, out(z)] += both + jnp.concatenate([first, second], 1)

    def add_next(z):
        near_ref[:, out(z)] += dot3(masked_ref[:, lanes(z + 1)], next_high[...], next_low[...], NT)
        near_ref[:, out(z + 1)] += dot3(masked_ref[:, lanes(z)], next_high[...], next_low[...])

    def layer(z, carry):
        fill_next(z)
        add_own(z)
        fill_own(z + 1)
        add_next(z)
        return carry

    fill_own(begin)
    lax.fori_loop(begin, end - 1, layer, 0)
    if end < LAYERS:
        fill_next(end - 1)
    add_own(end - 1)
    if end < LAYERS:
        add_next(end - 1)


def four_to_one(slots, sink_ref):
    left = jnp.concatenate([slots[0], slots[1]], 1)
    right = jnp.concatenate([slots[2], slots[3]], 1)
    lifted = dot3(jnp.concatenate([left, right], 0), sink_ref[0], sink_ref[1], NT)
    pair = pair_rows(lifted)
    box = pack_box(dot3(pair, sink_ref[0], sink_ref[1], NT))
    return left, right, pair, box


def lower_gather_kernel(index_ref, own_ref, far_ref, sink_ref, hold_ref, quad_ref, close_ref,
                        wide_ref, slots):
    del hold_ref
    index = index_ref[0]
    for step, box in enumerate((own_ref[0], own_ref[1], far_ref[0], far_ref[1])):
        slots[pl.ds(index % 4 ^ step, 1)] = unpack_box(box)[None]
    left, right, pair, box = four_to_one(slots, sink_ref)
    quad_ref[...] = jnp.concatenate([left, right], 1)
    is_even = index // 4 % 2 == 0
    facing = jnp.where(is_even, right, left)
    away = jnp.where(is_even, left, right)
    close_ref[...] = jnp.concatenate([box, facing, pair, away, pair], 0)
    wide_ref[...] = jnp.concatenate([box, away, pair], 0)


def upper_gather_kernel(index_ref, own_ref, one_ref, two_ref, three_ref, sink_ref, hold_ref,
                        quad_ref, box_ref, inside_ref, close_ref, wide_ref, slots, edges):
    del hold_ref
    index = index_ref[0]
    member = index // 4 % 4
    for step, ref in enumerate((own_ref, one_ref, two_ref, three_ref)):
        slots[pl.ds(member ^ step, 1)] = unpack_box(ref[:16])[None]
        edges[pl.ds(member ^ step, 1)] = ref[80:144][None] if step == 1 else ref[16:80][None]
    left, right, pair, box = four_to_one(slots, sink_ref)
    quad_ref[...] = jnp.concatenate([left, right], 1)
    box_ref[...] = box
    beside, across = one_ref[16:80], three_ref[16:80]
    is_odd = member % 2 == 1
    inside_ref[:64] = jnp.where(is_odd, beside, across)
    inside_ref[64:] = jnp.where(is_odd, across, beside)
    is_even = index // 16 % 2 == 0
    first, last = edges[0], edges[3]
    facing = jnp.where(is_even, right, left)
    away = jnp.where(is_even, left, right)
    close_ref[...] = jnp.concatenate([box, facing, pair, jnp.where(is_even, last, first)], 0)
    wide_ref[...] = jnp.concatenate([away, pair, jnp.where(is_even, first, last)], 0)


def rim_kernel(parts, index_ref, coords_ref, masked_ref, coef_ref, basish_ref, basisl_ref,
               pairs_ref, facing_ref, away_ref, layers_ref, coupling_ref, sink_ref, octants_ref,
               quad3_ref, quad5_ref, inside_ref, close_ref, wide_ref, *refs):
    near_refs = refs[: len(parts)]
    _, base_ref, local_ref, path_ref, high_ref, low_ref, left_ref, right_ref = refs[len(parts) :]
    index = index_ref[0]
    base_ref[...] = jnp.zeros_like(base_ref)
    for (begin, end), ref in zip(parts, near_refs):
        base_ref[:, 256 * begin : 256 * end + 256] += ref[...]
    is_even = index % 2 == 0
    left_ref[...] = jnp.where(is_even, away_ref[...], facing_ref[...])
    right_ref[...] = jnp.where(is_even, facing_ref[...], away_ref[...])
    row = lax.broadcasted_iota(jnp.int32, (8, 256), 0)

    def rim_coords(ref, shift):
        coords = jnp.concatenate([ref[0:8, 1152:1280], ref[8:16, 1152:1280]], 1)
        return coords + jnp.where(row == 2, shift, 0.0)

    low_rim = rim_coords(left_ref, -float(CUBES))
    left, _ = features(low_rim, 0.0)
    _, right = features(coords_ref[:, :256], 0.0)
    fill_weights(turned_side(left), right_side(right), high_ref, low_ref)
    base_ref[:, :256] += dot3(left_ref[:, :256], high_ref[...], low_ref[...], NN)
    high_rim = rim_coords(right_ref, float(CUBES))
    left, _ = features(coords_ref[:, SLOTS - 256 :], float(CUBES))
    _, right = features(high_rim, float(CUBES))
    fill_weights(turned_side(left), right_side(right), high_ref, low_ref)
    base_ref[:, SLOTS - 256 :] += dot3(right_ref[:, :256], high_ref[...], low_ref[...], NT)

    coefs = [coef_ref[:, 512 * s : 512 * s + 512] for s in range(CUBES)]
    before = jnp.concatenate([left_ref[:, 256:768]] + coefs[:-1], 0)
    after = jnp.concatenate(coefs[1:] + [right_ref[:, 256:768]], 0)
    k2 = (layers_ref[0], layers_ref[1])
    k3 = (layers_ref[2], layers_ref[3])
    even = dot3(before[:, :256], *k2) + dot3(after[:, :256], *k2, NT) + dot3(after[:, 256:], *k3, NT)
    odd = dot3(before[:, :256], *k3) + dot3(before[:, 256:], *k2) + dot3(after[:, 256:], *k2, NT)

    def coupled(pairs, level):
        at = slice(768 + 128 * level, 896 + 128 * level)
        lower, upper = left_ref[:, at], right_ref[:, at]
        sides = jnp.concatenate(
            [
                jnp.concatenate([lower, pairs[:-VECS]], 0) if pairs.shape[0] > VECS else lower,
                jnp.concatenate([pairs[VECS:], upper], 0) if pairs.shape[0] > VECS else upper,
            ],
            1,
        )
        return dot3(sides, coupling_ref[2 * level], coupling_ref[2 * level + 1])

    sink = (sink_ref[0], sink_ref[1])
    local = coupled(pairs_ref[6 * VECS :], 2)
    local = coupled(pairs_ref[4 * VECS : 6 * VECS], 1) + dot3(unpair_rows(local), *sink)
    local = coupled(pairs_ref[: 4 * VECS], 0) + dot3(unpair_rows(local), *sink)
    inherited = dot3(unpair_rows(local), octants_ref[0], octants_ref[1])
    even = even + inherited[:, :256]
    odd = odd + inherited[:, 256:]
    for s in range(CUBES):
        for part, values in ((0, even), (1, odd)):
            at = slice(512 * s + 256 * part, 512 * s + 256 * part + 256)
            high, low = spread_basis(basish_ref[:, at], basisl_ref[:, at])
            base_ref[:, at] += dot3(values[VECS * s : VECS * s + VECS], high, low)

    member = index // 4 % 4
    is_even = index // 16 % 2 == 0
    beside, outer = close_ref[...], wide_ref[...]
    left = jnp.where(member == 0, jnp.where(is_even, outer[64:], beside[80:]), inside_ref[:64])
    right = jnp.where(member == 3, jnp.where(is_even, beside[80:], outer[64:]), inside_ref[64:])
    edges = {
        3: (left, right),
        5: (
            jnp.where(is_even, outer[:64], beside[16:80]),
            jnp.where(is_even, beside[16:80], outer[:64]),
        ),
    }

    def is_low(level):
        return index // (1 << (level - 3)) % 2 == 0

    def half(both, level):
        return jnp.where(is_low(level), both[:, :64], both[:, 64:])

    sides = {}
    for level, quad_ref in ((3, quad3_ref), (5, quad5_ref)):
        left, right = edges[level]
        low = is_low(level + 1)
        sides[level] = jnp.concatenate(
            [
                jnp.where(low, left[:VECS], quad_ref[:, :128]),
                jnp.where(low, quad_ref[:, 128:], right[:VECS]),
            ],
            1,
        )
        sides[level + 1] = jnp.concatenate([left[VECS:], right[VECS:]], 1)
    local = path = None
    for level in (6, 5, 4, 3):
        far = dot3(sides[level], coupling_ref[2 * level], coupling_ref[2 * level + 1])
        step = sink[0].astype(F32) + sink[1].astype(F32)
        if local is not None:
            far = far + dot3(local, *sink)
            step = dot3(path, *sink)
        local = half(far, level)
        path = half(step, level)
    local_ref[...] = local
    path_ref[...] = path


def tail_kernel(begin, index_ref, base_ref, near_ref, occ_ref, high_ref, low_ref, boxes_ref,
                far_ref, local_ref, path_ref, coupling_ref, sink_ref, out_ref):
    index = index_ref[0]
    top = index // 16
    count = boxes_ref.shape[0]

    def box7(number):
        inside = ((number >= 0) & (number < 16)).astype(F32)
        place = jnp.clip(number, 0, 15) ^ top
        at = pl.ds(place % count, 1)
        packed = jnp.where(place < count, boxes_ref[at][0], far_ref[at][0])
        return unpack_box(packed) * inside

    sink = (sink_ref[0], sink_ref[1])

    def lift(pairs):
        return pair_rows(dot3(pairs, *sink, NT))

    def level7(pair):
        return jnp.concatenate([box7(2 * pair), box7(2 * pair + 1)], 1)

    sides = {}
    pair7 = top // 2
    sides[7] = jnp.concatenate([level7(pair7 - 1), level7(pair7 + 1)], 1)
    pair8 = top // 4
    pairs = [level7(2 * (pair8 + side) + half) for side in (-1, 1) for half in (0, 1)]
    pair9 = 1 - top // 8
    pairs += [level7(4 * pair9 + quarter) for quarter in range(4)]
    lifted = lift(jnp.concatenate(pairs, 0))
    sides[8] = jnp.concatenate([lifted[:VECS], lifted[VECS : 2 * VECS]], 1)
    other = lift(lifted[2 * VECS :])
    is_upper = (pair9 == 0).astype(F32)
    sides[9] = jnp.concatenate([other * is_upper, other * (1.0 - is_upper)], 1)
    local = None
    for level in (9, 8, 7):
        far = dot3(sides[level], coupling_ref[2 * level - 14], coupling_ref[2 * level - 13])
        if local is not None:
            far = far + dot3(local, *sink)
        is_low = index // (1 << (level - 3)) % 2 == 0
        local = jnp.where(is_low, far[:, :64], far[:, 64:])
    local = local_ref[...] + dot3(local, *split(path_ref[...]))
    split_at = 256 * begin
    far = dot3(local, high_ref[...], low_ref[...])
    out_ref[...] = (base_ref[...] + far) * occ_ref[...]
    out_ref[:, split_at:] += near_ref[...] * occ_ref[:, split_at:]


VMEM = pl.BlockSpec(memory_space=pltpu.VMEM)
SMEM = pl.BlockSpec(memory_space=pltpu.SMEM)
HBM = pl.BlockSpec(memory_space=pltpu.HBM)
ANY = pl.BlockSpec(memory_space=pl.ANY)


def call(body, in_specs, outs, scratch=(), aliases=None, name=None):
    return pl.pallas_call(
        body,
        out_shape=[jax.ShapeDtypeStruct(shape, dtype) for shape, dtype in outs],
        in_specs=in_specs,
        out_specs=[VMEM] * len(outs),
        scratch_shapes=list(scratch),
        input_output_aliases=aliases or {},
        compiler_params=pltpu.CompilerParams(vmem_limit_bytes=VMEM_LIMIT),
        name=name,
    )


def local(points, vectors, counts):
    devices = lax.axis_size(AXES)
    index = lax.axis_index(AXES).astype(jnp.int32)

    def crossed(value, mask):
        return lax.ppermute(value, AXES, [(i, i ^ mask) for i in range(devices)])

    def swapped(value, size):
        pairs = []
        for i in range(size, devices - size):
            pairs.append((i, i + size if i // size % 2 else i - size))
        return lax.ppermute(value, AXES, pairs)

    def after(value, *others):
        return lax.optimization_barrier((value,) + others)[0]

    octants, along = transfer_tables()
    octants = jnp.asarray(hi_lo(octants.T))
    sink = jnp.asarray(hi_lo(along.T))
    layers = jnp.asarray(
        np.concatenate([hi_lo(kernel_table(layer_nodes(0), layer_nodes(z))) for z in (2, 3)])
    )
    couplings = [hi_lo(pair_coupling(level)) for level in range(TOP)]
    low_couplings = jnp.asarray(np.concatenate(couplings[:7]))
    high_couplings = jnp.asarray(np.concatenate(couplings[7:]))

    coords, masked, occupied, box3, far_high, far_low = call(
        head_kernel,
        [SMEM, HBM, HBM, HBM],
        [
            ((8, SLOTS), F32),
            ((VECS, SLOTS), F32),
            ((1, SLOTS), F32),
            ((16, 128), F32),
            ((64, SLOTS), BF16),
            ((64, SLOTS), BF16),
        ],
        [
            pltpu.SMEM((CUBES, 8), jnp.int32),
            pltpu.VMEM((3, SLOTS), F32),
            pltpu.VMEM((VECS, SLOTS), F32),
            pltpu.SemaphoreType.DMA((4,)),
        ],
        name="head",
    )((index * CUBES)[None], counts, points, vectors)

    number = index[None]

    def near_part(part, hold):
        own = pltpu.VMEM((256, 256), BF16)
        begin, end = part
        width = 256 * (min(end + 1, LAYERS) - begin)
        return call(
            functools.partial(near_kernel, begin, end),
            [VMEM, VMEM, ANY],
            [((VECS, width), F32)],
            [own] * 4 + [pltpu.VMEM((256, 48), BF16)],
            name="near",
        )(coords, masked, hold)[0]

    parts = [(0, 4), (4, 6), (6, 10), (10, 13)]
    last = (13, 16)
    arrived = crossed(box3, 1)
    coef, leaf_high, leaf_low, pairs, facing, away = call(
        leaf_kernel,
        [SMEM] + [VMEM] * 4,
        [
            ((VECS, SLOTS), F32),
            ((64, SLOTS), BF16),
            ((64, SLOTS), BF16),
            ((7 * VECS, 128), F32),
            ((VECS, 1280), F32),
            ((VECS, 1280), F32),
        ],
        name="leaf",
    )(number, coords, masked, octants, sink)
    boxes3 = jnp.stack([box3, after(arrived, pairs)])
    arrived = crossed(boxes3, 2)
    near = [near_part(parts[0], boxes3)]
    slots = pltpu.VMEM((4, VECS, 64), F32)
    quad3, close3, wide3 = call(
        lower_gather_kernel,
        [SMEM] + [VMEM] * 3 + [ANY],
        [((VECS, 256), F32), ((144, 128), F32), ((80, 128), F32)],
        [slots],
        name="gather3",
    )(number, boxes3, arrived, sink, near[-1])
    others = [crossed(close3, 4), crossed(wide3, 8), crossed(wide3, 12)]
    near.append(near_part(parts[1], wide3))
    quad5, box7, inside, close5, wide5 = call(
        upper_gather_kernel,
        [SMEM] + [VMEM] * 5 + [ANY],
        [
            ((VECS, 256), F32),
            ((16, 128), F32),
            ((128, 128), F32),
            ((144, 128), F32),
            ((128, 128), F32),
        ],
        [slots, pltpu.VMEM((4, 64, 128), F32)],
        name="gather5",
    )(number, wide3, *others, sink, near[-1])
    beside5 = crossed(close5, 16)
    facing = crossed(after(facing, box7), 1)
    near.append(near_part(parts[2], box7))
    boxes = jnp.stack([box7, after(beside5, near[-1])[:16]])
    arrived = crossed(boxes, 32)
    away = swapped(after(away, boxes), 1)
    outer5 = swapped(after(wide5, boxes), 16)
    near.append(near_part(parts[3], boxes))
    boxes = jnp.concatenate([boxes, after(arrived, near[-1])], 0)
    arrived = crossed(boxes, 64)
    halo = pltpu.VMEM((VECS, 1280), F32)
    base, far_local, path = call(
        functools.partial(rim_kernel, parts),
        [SMEM] + [VMEM] * (17 + len(parts)) + [ANY],
        [((VECS, SLOTS), F32), ((VECS, 64), F32), ((64, 64), F32)],
        [pltpu.VMEM((256, 256), BF16)] * 2 + [halo] * 2,
        name="rim",
    )(
        number, coords, masked, coef, leaf_high, leaf_low, pairs, facing, away, layers,
        low_couplings, sink, octants, quad3, quad5, inside, beside5, outer5, *near, boxes,
    )
    boxes = jnp.concatenate([boxes, after(arrived, base)], 0)
    arrived = crossed(boxes, 128)
    final = near_part(last, boxes)
    return call(
        functools.partial(tail_kernel, last[0]),
        [SMEM] + [VMEM] * 11,
        [((VECS, SLOTS), F32)],
        name="tail",
    )(
        number, base, final, occupied, far_high, far_low, boxes, after(arrived, final), far_local,
        path, high_couplings, sink,
    )[0]


def solution(mesh):
    in_specs = (P(None, AXES), P(None, AXES), P(AXES, None))
    return jax.shard_map(
        local, mesh=mesh, in_specs=in_specs, out_specs=P(None, AXES), check_vma=False
    )
```

time: 101 us -> 62.9 us (0.62)
  the two profiles are of different devices: /device:TPU:224 before, /device:TPU:64 now
where the time goes in v2:
time: 62.9 us; the launch traced here: 62.7 us
  Pallas kernels  26.1 us (41%)
  starting transfers between devices  21.2 us (34%)
  waiting for transfers between devices  12.6 us (20%)
  local copies, waits for them, and re-layouts  2.59 us (4%)
    ppermute x10, starting transfers between devices, crossed(): return lax.ppermute(value, AXES, [(i, i ^ mask) for i in range(devices)])  16.1 us
    pallas_call x5, Pallas kernels, near_part(): call(functools.partial(near_kernel, begin, end), [VMEM, VMEM, ANY], [((VE...  11.9 us
    ppermute x2, waiting for transfers between devices, swapped(): return lax.ppermute(value, AXES, pairs)  7.67 us
    ppermute x2, starting transfers between devices, swapped(): return lax.ppermute(value, AXES, pairs)  5.16 us
    ppermute x10, waiting for transfers between devices, crossed(): return lax.ppermute(value, AXES, [(i, i ^ mask) for i in range(devices)])  4.9 us
    pallas_call x1, Pallas kernels, local(): call(leaf_kernel, [SMEM] + [VMEM] * 4, [((VECS, SLOTS), F32), ((64, SLOTS...  4.46 us
    pallas_call x1, Pallas kernels, local(): call(functools.partial(rim_kernel, parts), [SMEM] + [VMEM] * (17 + len(pa...  3.76 us
    unnamed x16, local copies, waits for them, and re-layouts  2.59 us
  transfers between devices with their start and end apart: 12, of which 4 were waited for; matrix products, arithmetic and copies ran while one was open for 0% of the time, Pallas kernels for 32%

profile of v2, /device:TPU:64, one launch (start us, length us, event | category | flops | bytes accessed | tf_op | source)
XLA Modules:
  0.0 62.7 jit_solution(12982342869693352302)
XLA Ops:
  0.0 0.0 copy-start.7
  0.0 0.7 %copy-done.7 = s32[8,8]{1,0:T(8,128)S(1)} copy-done((s32[8,8]{1,0:T(8,128)S(1)}, s32[8,8]{1,0:T(8,128)}, u32[]{:S(2)}) %copy-start.7) | copy-done | bytes 280
  0.7 0.0 copy-start.2
  0.7 1.0 %copy-done.2 = f32[32,4096]{1,0:T(8,128)S(1)} copy-done((f32[32,4096]{1,0:T(8,128)S(1)}, f32[32,4096]{1,0:T(8,128)}, u32[]{:S(2)}) %copy-start.2) | copy-done | bytes 524312
  1.7 0.0 copy-start.6
  1.7 0.8 %copy-done.6 = f32[3,4096]{1,0:T(4,128)S(1)} copy-done((f32[3,4096]{1,0:T(4,128)S(1)}, f32[3,4096]{1,0:T(4,128)}, u32[]{:S(2)}) %copy-start.6) | copy-done | bytes 49176
  2.6 0.0 copy-start.1
  2.6 0.0 copy-start.4
  2.6 2.4 %head.1 = (f32[8,4096]{1,0:T(8,128)S(1)}, f32[32,4096]{1,0:T(8,128)S(1)}, f32[1,4096]{1,0:T(1,128)S(1)}, f32[16,128]{1,0:T(8,128)S(1)}, bf16[64,4096]{1,0:T(8,128)(2,1)S(1)}, /*index=5*/bf16[64,4096]{1,0:T(8,128)(2,1)S(1)}) custom-call(s32[1]{0:T(128)} %bitcast.1.slab_ref, s32[8,8]{1,0:T(8,128)S(1)} %copy-done.7, f32[3,4096]{1,0:T(4,128)S(1)} %copy-done.6, ...), custom_call_target="tpu_custom_call" | custom-call | tf_op jit(solution)/shard_map/head/pallas_call | solution.py:631
  4.9 1.6 %collective-permute-start = (f32[16,128]{1,0:T(8,128)S(1)}, f32[16,128]{1,0:T(8,128)S(1)}, u32[]{:S(2)}, u32[]{:S(2)}) collective-permute-start(f32[16,128]{1,0:T(8,128)S(1)} %get-tuple-element.43), channel_id=1, source_target_pairs={{0,1},{1,0},{2,3},{3,2},{4,5},{5,4},{6,7},{7,6},{8,9},{9,8},{10,11... | collective-permute-start | bytes 24584 | tf_op jit(solution)/shard_map/ppermute | solution.py:610
  6.5 0.0 copy-done.1
  6.5 0.0 copy-done.4
  6.5 4.5 %leaf.1 = (f32[32,4096]{1,0:T(8,128)S(1)}, bf16[64,4096]{1,0:T(8,128)(2,1)S(1)}, bf16[64,4096]{1,0:T(8,128)(2,1)S(1)}, f32[224,128]{1,0:T(8,128)S(1)}, f32[32,1280]{1,0:T(8,128)S(1)}, /*index=5*/f32[32,1280]{1,0:T(8,128)S(1)}) custom-call(s32[1]{0:T(128)} %bitcast.index_ref, f32[8,4096]{1,0:T(8,128)S(1)} %get-tuple-element.36.coords_ref, ...), custom_call_target="tpu_custom_call" | custom-call | tf_op jit(solution)/shard_map/leaf/pallas_call | solution.py:668
  11.0 0.0 collective-permute-done
  11.1 2.8 %collective-permute-start.1 = (f32[2,16,128]{2,1,0:T(8,128)S(1)}, f32[2,16,128]{2,1,0:T(8,128)S(1)}, u32[]{:S(2)}, u32[]{:S(2)}) collective-permute-start(f32[2,16,128]{2,1,0:T(8,128)S(1)} %pad_maximum_fusion.2.hold_ref.own_ref), channel_id=1, source_target_pairs={{0,2},{1,3},{2,0},{3,1},{4,6},{5,7},{6,4},{7,5},{8,10},{9,11},{10,... | collective-permute-start | bytes 49160 | tf_op jit(solution)/shard_map/ppermute | solution.py:610
  13.9 3.1 %near.5.hold_ref.refs_0_ = f32[32,1280]{1,0:T(8,128)S(1)} custom-call(f32[8,4096]{1,0:T(8,128)S(1)} %get-tuple-element.36.coords_ref, f32[32,4096]{1,0:T(8,128)S(1)} %get-tuple-element.37.masked_ref, f32[2,16,128]{2,1,0:T(8,128)S(1)} %pad_maximum_fusion.2.hold_ref.own_ref), custom_call_target="tpu_custom_call" | custom-call | tf_op jit(solution)/shard_map/near/pallas_call | solution.py:657
  17.0 0.0 collective-permute-done.1.far_ref
  17.0 0.6 gather3.1
  17.6 0.0 collective-permute-start.2
  17.6 1.6 %collective-permute-start.3 = (f32[80,128]{1,0:T(8,128)S(1)}, f32[80,128]{1,0:T(8,128)S(1)}, u32[]{:S(2)}, u32[]{:S(2)}) collective-permute-start(f32[80,128]{1,0:T(8,128)S(1)} %get-tuple-element.45.hold_ref.own_ref), channel_id=1, source_target_pairs={{0,8},{1,9},{2,10},{3,11},{4,12},{5,13},{6,14},{7,15},{8,0},{9,1},... | collective-permute-start | bytes 122888 | tf_op jit(solution)/shard_map/ppermute | solution.py:610
  19.2 0.3 collective-permute-start.4
  19.4 1.4 %near.6.hold_ref.refs_1_ = f32[32,768]{1,0:T(8,128)S(1)} custom-call(f32[8,4096]{1,0:T(8,128)S(1)} %get-tuple-element.36.coords_ref, f32[32,4096]{1,0:T(8,128)S(1)} %get-tuple-element.37.masked_ref, f32[80,128]{1,0:T(8,128)S(1)} %get-tuple-element.45.hold_ref.own_ref), custom_call_target="tpu_custom_call" | custom-call | tf_op jit(solution)/shard_map/near/pallas_call | solution.py:657
  20.8 0.8 %collective-permute-done.3.two_ref = f32[80,128]{1,0:T(8,128)S(1)} collective-permute-done((f32[80,128]{1,0:T(8,128)S(1)}, f32[80,128]{1,0:T(8,128)S(1)}, u32[]{:S(2)}, u32[]{:S(2)}) %collective-permute-start.3) | collective-permute-done | bytes 40992 | tf_op jit(solution)/shard_map/ppermute | solution.py:610
  21.6 1.1 %collective-permute-done.4.three_ref = f32[80,128]{1,0:T(8,128)S(1)} collective-permute-done((f32[80,128]{1,0:T(8,128)S(1)}, f32[80,128]{1,0:T(8,128)S(1)}, u32[]{:S(2)}, u32[]{:S(2)}) %collective-permute-start.4) | collective-permute-done | bytes 40992 | tf_op jit(solution)/shard_map/ppermute | solution.py:610
  22.7 0.0 collective-permute-done.2.one_ref
  22.7 0.5 gather5.1
  23.3 0.0 copy-start
  23.3 2.9 %collective-permute-start.6 = (f32[144,128]{1,0:T(8,128)S(1)}, f32[144,128]{1,0:T(8,128)S(1)}, u32[]{:S(2)}, u32[]{:S(2)}) collective-permute-start(f32[144,128]{1,0:T(8,128)S(1)} %get-tuple-element.50), channel_id=1, source_target_pairs={{0,16},{1,17},{2,18},{3,19},{4,20},{5,21},{6,22},{7,23},{8,24},{9,... | collective-permute-start | bytes 221192 | tf_op jit(solution)/shard_map/ppermute | solution.py:610
  26.2 3.1 %near.7.refs_2_ = f32[32,1280]{1,0:T(8,128)S(1)} custom-call(f32[8,4096]{1,0:T(8,128)S(1)} %get-tuple-element.36.coords_ref, f32[32,4096]{1,0:T(8,128)S(1)} %get-tuple-element.37.masked_ref, f32[16,128]{1,0:T(8,128)S(1)} %get-tuple-element.47.hold_ref), custom_call_target="tpu_custom_call" | custom-call | tf_op jit(solution)/shard_map/near/pallas_call | solution.py:657
  29.3 0.0 copy-start.3
  29.3 0.3 collective-permute-start.5
  29.7 0.0 collective-permute-done.6.close_ref
  29.7 3.2 %collective-permute-start.7 = (f32[32,1280]{1,0:T(8,128)S(1)}, f32[32,1280]{1,0:T(8,128)S(1)}, u32[]{:S(2)}, u32[]{:S(2)}) collective-permute-start(f32[32,1280]{1,0:T(8,128)S(1)} %get-tuple-element.52), channel_id=1, source_target_pairs={{1,2},{2,1},{3,4},{4,3},{5,6},{6,5},{7,8},{8,7},{9,10},{10,9},{11,... | collective-permute-start | bytes 491528 | tf_op jit(solution)/shard_map/ppermute | solution.py:616
  32.9 2.0 %collective-permute-start.9 = (f32[2,16,128]{2,1,0:T(8,128)S(1)}, f32[2,16,128]{2,1,0:T(8,128)S(1)}, u32[]{:S(2)}, u32[]{:S(2)}) collective-permute-start(f32[2,16,128]{2,1,0:T(8,128)S(1)} %pad_maximum_fusion.3.hold_ref), channel_id=1, source_target_pairs={{0,32},{1,33},{2,34},{3,35},{4,36},{5,37},{6,38},{7,39},{8,40},{9,... | collective-permute-start | bytes 49160 | tf_op jit(solution)/shard_map/ppermute | solution.py:610
  34.9 2.4 %near.8.refs_3_ = f32[32,1024]{1,0:T(8,128)S(1)} custom-call(f32[8,4096]{1,0:T(8,128)S(1)} %get-tuple-element.36.coords_ref, f32[32,4096]{1,0:T(8,128)S(1)} %get-tuple-element.37.masked_ref, f32[2,16,128]{2,1,0:T(8,128)S(1)} %pad_maximum_fusion.3.hold_ref), custom_call_target="tpu_custom_call" | custom-call | tf_op jit(solution)/shard_map/near/pallas_call | solution.py:657
  37.3 1.9 %collective-permute-start.8 = (f32[128,128]{1,0:T(8,128)S(1)}, f32[128,128]{1,0:T(8,128)S(1)}, u32[]{:S(2)}, u32[]{:S(2)}) collective-permute-start(f32[128,128]{1,0:T(8,128)S(1)} %get-tuple-element.57), channel_id=1, source_target_pairs={{16,32},{17,33},{18,34},{19,35},{20,36},{21,37},{22,38},{23,39},{2... | collective-permute-start | bytes 196616 | tf_op jit(solution)/shard_map/ppermute | solution.py:616
  39.3 0.0 collective-permute-done.9
  39.3 0.3 collective-permute-start.10
  39.6 7.7 %collective-permute-done.8.wide_ref = f32[128,128]{1,0:T(8,128)S(1)} collective-permute-done((f32[128,128]{1,0:T(8,128)S(1)}, f32[128,128]{1,0:T(8,128)S(1)}, u32[]{:S(2)}, u32[]{:S(2)}) %collective-permute-start.8) | collective-permute-done | bytes 65568 | tf_op jit(solution)/shard_map/ppermute | solution.py:616
  47.2 0.0 collective-permute-done.5.facing_ref
  47.3 0.0 collective-permute-done.7.away_ref
  47.3 0.0 copy-done
  47.3 0.0 copy-done.3
  47.3 3.8 %rim.1 = (f32[32,4096]{1,0:T(8,128)S(1)}, f32[32,64]{1,0:T(8,128)S(1)}, f32[64,64]{1,0:T(8,128)S(1)}) custom-call(s32[1]{0:T(128)} %bitcast.index_ref, f32[8,4096]{1,0:T(8,128)S(1)} %get-tuple-element.36.coords_ref, f32[32,4096]{1,0:T(8,128)S(1)} %get-tuple-element.37.masked_ref, f32[32,4096]{1,0:T(8,128)S(1)} %get-tuple-element.38.coef_ref, ...), custom_call_target="tpu_custom_call" | custom-call | tf_op jit(solution)/shard_map/rim/pallas_call | solution.py:718
  51.0 0.0 collective-permute-done.10
  51.1 0.0 copy-start.5
  51.1 4.2 %collective-permute-start.11 = (f32[8,16,128]{2,1,0:T(8,128)S(1)}, f32[8,16,128]{2,1,0:T(8,128)S(1)}, u32[]{:S(2)}, u32[]{:S(2)}) collective-permute-start(f32[8,16,128]{2,1,0:T(8,128)S(1)} %pad_maximum_fusion.hold_ref.boxes_ref), channel_id=1, source_target_pairs={{0,128},{1,129},{2,130},{3,131},{4,132},{5,133},{6,134},{7,135},{8... | collective-permute-start | bytes 196616 | tf_op jit(solution)/shard_map/ppermute | solution.py:610
  55.3 1.9 %near.9.near_ref = f32[32,768]{1,0:T(8,128)S(1)} custom-call(f32[8,4096]{1,0:T(8,128)S(1)} %get-tuple-element.36.coords_ref, f32[32,4096]{1,0:T(8,128)S(1)} %get-tuple-element.37.masked_ref, f32[8,16,128]{2,1,0:T(8,128)S(1)} %pad_maximum_fusion.hold_ref.boxes_ref), custom_call_target="tpu_custom_call" | custom-call | tf_op jit(solution)/shard_map/near/pallas_call | solution.py:657
  57.2 2.9 %collective-permute-done.11.far_ref = f32[8,16,128]{2,1,0:T(8,128)S(1)} collective-permute-done((f32[8,16,128]{2,1,0:T(8,128)S(1)}, f32[8,16,128]{2,1,0:T(8,128)S(1)}, u32[]{:S(2)}, u32[]{:S(2)}) %collective-permute-start.11) | collective-permute-done | bytes 65568 | tf_op jit(solution)/shard_map/ppermute | solution.py:610
  60.1 0.0 copy-done.5
  60.1 2.6 %tail.1 = f32[32,4096]{1,0:T(8,128)} custom-call(s32[1]{0:T(128)} %bitcast.index_ref, f32[32,4096]{1,0:T(8,128)S(1)} %get-tuple-element.59.base_ref, f32[32,768]{1,0:T(8,128)S(1)} %near.9.near_ref, f32[1,4096]{1,0:T(1,128)S(1)} %get-tuple-element.61.occ_ref, bf16[64,4096]{1,0:T(8,128)(2,1)S(1)} %get-tuple-element.62.high_ref, ...), custom_call_target="tpu_custom_call" | custom-call | tf_op jit(solution)/shard_map/tail/pallas_call | solution.py:731
  (5 shorter events, 0.0 us)
Async XLA Ops:
  0.0 0.7 %copy-start.7 = (s32[8,8]{1,0:T(8,128)S(1)}, s32[8,8]{1,0:T(8,128)}, u32[]{:S(2)}) copy-start(s32[8,8]{1,0:T(8,128)} %counts_hbm.1) | copy-start | bytes 772
  0.7 1.0 %copy-start.2 = (f32[32,4096]{1,0:T(8,128)S(1)}, f32[32,4096]{1,0:T(8,128)}, u32[]{:S(2)}) copy-start(f32[32,4096]{1,0:T(8,128)} %vectors_hbm.1) | copy-start | bytes 1572868
  1.7 0.8 %copy-start.6 = (f32[3,4096]{1,0:T(4,128)S(1)}, f32[3,4096]{1,0:T(4,128)}, u32[]{:S(2)}) copy-start(f32[3,4096]{1,0:T(4,128)} %points_hbm.1) | copy-start | bytes 147460
  2.6 3.9 %copy-start.1 = (bf16[2,64,128]{2,1,0:T(8,128)(2,1)S(1)}, bf16[2,64,128]{2,1,0:T(8,128)(2,1)}, u32[]{:S(2)}) copy-start(bf16[2,64,128]{2,1,0:T(8,128)(2,1)} %constant.24.clone.sink_ref) | copy-start | bytes 98308
  2.6 4.0 %copy-start.4 = (bf16[2,64,512]{2,1,0:T(8,128)(2,1)S(1)}, bf16[2,64,512]{2,1,0:T(8,128)(2,1)}, u32[]{:S(2)}) copy-start(bf16[2,64,512]{2,1,0:T(8,128)(2,1)} %constant.23.clone.octants_ref) | copy-start | bytes 393220
  4.9 6.1 %collective-permute-start = (f32[16,128]{1,0:T(8,128)S(1)}, f32[16,128]{1,0:T(8,128)S(1)}, u32[]{:S(2)}, u32[]{:S(2)}) collective-permute-start(f32[16,128]{1,0:T(8,128)S(1)} %get-tuple-element.43), channel_id=1, source_target_pairs={{0,1},{1,0},{2,3},{3,2},{4,5},{5,4},{6,7},{7,6},{8,9},{9,8},{10,11... | collective-permute-start | bytes 24584 | tf_op jit(solution)/shard_map/ppermute | solution.py:610
  11.1 6.0 %collective-permute-start.1 = (f32[2,16,128]{2,1,0:T(8,128)S(1)}, f32[2,16,128]{2,1,0:T(8,128)S(1)}, u32[]{:S(2)}, u32[]{:S(2)}) collective-permute-start(f32[2,16,128]{2,1,0:T(8,128)S(1)} %pad_maximum_fusion.2.hold_ref.own_ref), channel_id=1, source_target_pairs={{0,2},{1,3},{2,0},{3,1},{4,6},{5,7},{6,4},{7,5},{8,10},{9,11},{10,... | collective-permute-start | bytes 49160 | tf_op jit(solution)/shard_map/ppermute | solution.py:610
  17.6 5.2 %collective-permute-start.2 = (f32[144,128]{1,0:T(8,128)S(1)}, f32[144,128]{1,0:T(8,128)S(1)}, u32[]{:S(2)}, u32[]{:S(2)}) collective-permute-start(f32[144,128]{1,0:T(8,128)S(1)} %get-tuple-element.46), channel_id=1, source_target_pairs={{0,4},{1,5},{2,6},{3,7},{4,0},{5,1},{6,2},{7,3},{8,12},{9,13},{10,... | collective-permute-start | bytes 221192 | tf_op jit(solution)/shard_map/ppermute | solution.py:610
  17.6 4.0 %collective-permute-start.3 = (f32[80,128]{1,0:T(8,128)S(1)}, f32[80,128]{1,0:T(8,128)S(1)}, u32[]{:S(2)}, u32[]{:S(2)}) collective-permute-start(f32[80,128]{1,0:T(8,128)S(1)} %get-tuple-element.45.hold_ref.own_ref), channel_id=1, source_target_pairs={{0,8},{1,9},{2,10},{3,11},{4,12},{5,13},{6,14},{7,15},{8,0},{9,1},... | collective-permute-start | bytes 122888 | tf_op jit(solution)/shard_map/ppermute | solution.py:610
  19.2 3.5 %collective-permute-start.4 = (f32[80,128]{1,0:T(8,128)S(1)}, f32[80,128]{1,0:T(8,128)S(1)}, u32[]{:S(2)}, u32[]{:S(2)}) collective-permute-start(f32[80,128]{1,0:T(8,128)S(1)} %get-tuple-element.45.hold_ref.own_ref), channel_id=1, source_target_pairs={{0,12},{1,13},{2,14},{3,15},{4,8},{5,9},{6,10},{7,11},{8,4},{9,5},... | collective-permute-start | bytes 122888 | tf_op jit(solution)/shard_map/ppermute | solution.py:610
  23.3 24.0 %copy-start = (bf16[14,256,128]{2,1,0:T(8,128)(2,1)S(1)}, bf16[14,256,128]{2,1,0:T(8,128)(2,1)}, u32[]{:S(2)}) copy-start(bf16[14,256,128]{2,1,0:T(8,128)(2,1)} %constant.26.clone.coupling_ref) | copy-start | bytes 2752516
  23.3 6.4 %collective-permute-start.6 = (f32[144,128]{1,0:T(8,128)S(1)}, f32[144,128]{1,0:T(8,128)S(1)}, u32[]{:S(2)}, u32[]{:S(2)}) collective-permute-start(f32[144,128]{1,0:T(8,128)S(1)} %get-tuple-element.50), channel_id=1, source_target_pairs={{0,16},{1,17},{2,18},{3,19},{4,20},{5,21},{6,22},{7,23},{8,24},{9,... | collective-permute-start | bytes 221192 | tf_op jit(solution)/shard_map/ppermute | solution.py:610
  29.3 18.0 %copy-start.3 = (bf16[4,256,256]{2,1,0:T(8,128)(2,1)S(1)}, bf16[4,256,256]{2,1,0:T(8,128)(2,1)}, u32[]{:S(2)}) copy-start(bf16[4,256,256]{2,1,0:T(8,128)(2,1)} %constant.25.clone.layers_ref) | copy-start | bytes 1572868
  29.3 17.9 %collective-permute-start.5 = (f32[32,1280]{1,0:T(8,128)S(1)}, f32[32,1280]{1,0:T(8,128)S(1)}, u32[]{:S(2)}, u32[]{:S(2)}) collective-permute-start(f32[32,1280]{1,0:T(8,128)S(1)} %get-tuple-element.48), channel_id=1, source_target_pairs={{0,1},{1,0},{2,3},{3,2},{4,5},{5,4},{6,7},{7,6},{8,9},{9,8},{10,11... | collective-permute-start | bytes 491528 | tf_op jit(solution)/shard_map/ppermute | solution.py:610
  29.7 17.6 %collective-permute-start.7 = (f32[32,1280]{1,0:T(8,128)S(1)}, f32[32,1280]{1,0:T(8,128)S(1)}, u32[]{:S(2)}, u32[]{:S(2)}) collective-permute-start(f32[32,1280]{1,0:T(8,128)S(1)} %get-tuple-element.52), channel_id=1, source_target_pairs={{1,2},{2,1},{3,4},{4,3},{5,6},{6,5},{7,8},{8,7},{9,10},{10,9},{11,... | collective-permute-start | bytes 491528 | tf_op jit(solution)/shard_map/ppermute | solution.py:616
  32.9 6.4 %collective-permute-start.9 = (f32[2,16,128]{2,1,0:T(8,128)S(1)}, f32[2,16,128]{2,1,0:T(8,128)S(1)}, u32[]{:S(2)}, u32[]{:S(2)}) collective-permute-start(f32[2,16,128]{2,1,0:T(8,128)S(1)} %pad_maximum_fusion.3.hold_ref), channel_id=1, source_target_pairs={{0,32},{1,33},{2,34},{3,35},{4,36},{5,37},{6,38},{7,39},{8,40},{9,... | collective-permute-start | bytes 49160 | tf_op jit(solution)/shard_map/ppermute | solution.py:610
  37.3 9.9 %collective-permute-start.8 = (f32[128,128]{1,0:T(8,128)S(1)}, f32[128,128]{1,0:T(8,128)S(1)}, u32[]{:S(2)}, u32[]{:S(2)}) collective-permute-start(f32[128,128]{1,0:T(8,128)S(1)} %get-tuple-element.57), channel_id=1, source_target_pairs={{16,32},{17,33},{18,34},{19,35},{20,36},{21,37},{22,38},{23,39},{2... | collective-permute-start | bytes 196616 | tf_op jit(solution)/shard_map/ppermute | solution.py:616
  39.3 11.7 %collective-permute-start.10 = (f32[4,16,128]{2,1,0:T(8,128)S(1)}, f32[4,16,128]{2,1,0:T(8,128)S(1)}, u32[]{:S(2)}, u32[]{:S(2)}) collective-permute-start(f32[4,16,128]{2,1,0:T(8,128)S(1)} %pad_maximum_fusion.1.refs_4_), channel_id=1, source_target_pairs={{0,64},{1,65},{2,66},{3,67},{4,68},{5,69},{6,70},{7,71},{8,72},{9,... | collective-permute-start | bytes 98312 | tf_op jit(solution)/shard_map/ppermute | solution.py:610
  51.1 9.1 %copy-start.5 = (bf16[6,256,128]{2,1,0:T(8,128)(2,1)S(1)}, bf16[6,256,128]{2,1,0:T(8,128)(2,1)}, u32[]{:S(2)}) copy-start(bf16[6,256,128]{2,1,0:T(8,128)(2,1)} %constant.27.clone.coupling_ref) | copy-start | bytes 1179652
  51.1 9.1 %collective-permute-start.11 = (f32[8,16,128]{2,1,0:T(8,128)S(1)}, f32[8,16,128]{2,1,0:T(8,128)S(1)}, u32[]{:S(2)}, u32[]{:S(2)}) collective-permute-start(f32[8,16,128]{2,1,0:T(8,128)S(1)} %pad_maximum_fusion.hold_ref.boxes_ref), channel_id=1, source_target_pairs={{0,128},{1,129},{2,130},{3,131},{4,132},{5,133},{6,134},{7,135},{8... | collective-permute-start | bytes 196616 | tf_op jit(solution)/shard_map/ppermute | solution.py:610

commit v3 on v2

--- a/solution.py
+++ b/solution.py
@@ -265,9 +265,9 @@
 
     for copy in copies[:3]:
         copy.wait()
-    total = lax.fori_loop(0, CUBES // 2, cube, jnp.zeros((VECS, 64), F32))
+    total = lax.fori_loop(0, CUBES // 2, cube, jnp.zeros((VECS, 64), F32), unroll=2)
     copies[3].wait()
-    total = lax.fori_loop(CUBES // 2, CUBES, cube, total)
+    total = lax.fori_loop(CUBES // 2, CUBES, cube, total, unroll=2)
     box_ref[...] = pack_box(total)
 
 
@@ -281,8 +281,9 @@
     return jnp.concatenate(highs, 0), jnp.concatenate(lows, 0)
 
 
-def leaf_kernel(index_ref, coords_ref, masked_ref, octants_ref, sink_ref, coef_ref, high_ref,
-                low_ref, pairs_ref, facing_ref, away_ref):
+def leaf_kernel(index_ref, coords_ref, masked_ref, octants_ref, sink_ref, hold_ref, coef_ref,
+                high_ref, low_ref, pairs_ref, facing_ref, away_ref):
+    del hold_ref
     lane = lax.broadcasted_iota(jnp.int32, (8, 256), 1)
     row = lax.broadcasted_iota(jnp.int32, (8, 256), 0)
     centre_x = jnp.where(lane // 64 % 2 == 0, -0.25, 0.25)
@@ -300,7 +301,7 @@
         coef_ref[:, at] = dot3(masked_ref[:, at], wide_high, wide_low, NT)
         return carry
 
-    lax.fori_loop(0, LAYERS, layer, 0)
+    lax.fori_loop(0, LAYERS, layer, 0, unroll=4)
     boxes = dot3(stack_rows(coef_ref[...], 512), octants_ref[0], octants_ref[1], NT)
     p0 = pair_rows(boxes)
     p1 = pair_rows(dot3(p0, sink_ref[0], sink_ref[1], NT))
@@ -330,9 +331,8 @@
         bundle(facing_ref, 0, 0, p0[:32], p1[:32])
 
 
-def near_kernel(begin, end, coords_ref, masked_ref, hold_ref, near_ref, own_high, own_low,
-                next_high, next_low, turned_ref):
-    del hold_ref
+def near_kernel(begin, end, coords_ref, masked_ref, *refs):
+    near_ref, own_high, own_low, next_high, next_low, turned_ref = refs[-6:]
     near_ref[...] = jnp.zeros_like(near_ref)
 
     def out(z):
@@ -438,7 +438,7 @@
     index = index_ref[0]
     base_ref[...] = jnp.zeros_like(base_ref)
     for (begin, end), ref in zip(parts, near_refs):
-        base_ref[:, 256 * begin : 256 * end + 256] += ref[...]
+        base_ref[:, 256 * begin : min(256 * end + 256, SLOTS)] += ref[...]
     is_even = index % 2 == 0
     left_ref[...] = jnp.where(is_even, away_ref[...], facing_ref[...])
     right_ref[...] = jnp.where(is_even, facing_ref[...], away_ref[...])
@@ -536,7 +536,7 @@
     path_ref[...] = path
 
 
-def tail_kernel(begin, index_ref, base_ref, near_ref, occ_ref, high_ref, low_ref, boxes_ref,
+def tail_kernel(index_ref, base_ref, occ_ref, high_ref, low_ref, boxes_ref,
                 far_ref, local_ref, path_ref, coupling_ref, sink_ref, out_ref):
     index = index_ref[0]
     top = index // 16
@@ -577,10 +577,8 @@
         is_low = index // (1 << (level - 3)) % 2 == 0
         local = jnp.where(is_low, far[:, :64], far[:, 64:])
     local = local_ref[...] + dot3(local, *split(path_ref[...]))
-    split_at = 256 * begin
     far = dot3(local, high_ref[...], low_ref[...])
     out_ref[...] = (base_ref[...] + far) * occ_ref[...]
-    out_ref[:, split_at:] += near_ref[...] * occ_ref[:, split_at:]
 
 
 VMEM = pl.BlockSpec(memory_space=pltpu.VMEM)
@@ -650,24 +648,26 @@
 
     number = index[None]
 
-    def near_part(part, hold):
+    def near_part(part, *holds):
         own = pltpu.VMEM((256, 256), BF16)
         begin, end = part
         width = 256 * (min(end + 1, LAYERS) - begin)
         return call(
             functools.partial(near_kernel, begin, end),
-            [VMEM, VMEM, ANY],
+            [VMEM, VMEM] + [ANY] * len(holds),
             [((VECS, width), F32)],
             [own] * 4 + [pltpu.VMEM((256, 48), BF16)],
             name="near",
-        )(coords, masked, hold)[0]
-
-    parts = [(0, 4), (4, 6), (6, 10), (10, 13)]
-    last = (13, 16)
+        )(coords, masked, *holds)[0]
+
+    parts = [(0, 3), (3, 6), (6, 10), (10, 13), (13, 16)]
     arrived = crossed(box3, 1)
+    near = [near_part(parts[0], box3)]
+    boxes3 = jnp.stack([box3, after(arrived, near[0])])
+    arrived = crossed(boxes3, 2)
     coef, leaf_high, leaf_low, pairs, facing, away = call(
         leaf_kernel,
-        [SMEM] + [VMEM] * 4,
+        [SMEM] + [VMEM] * 4 + [ANY],
         [
             ((VECS, SLOTS), F32),
             ((64, SLOTS), BF16),
@@ -677,10 +677,7 @@
             ((VECS, 1280), F32),
         ],
         name="leaf",
-    )(number, coords, masked, octants, sink)
-    boxes3 = jnp.stack([box3, after(arrived, pairs)])
-    arrived = crossed(boxes3, 2)
-    near = [near_part(parts[0], boxes3)]
+    )(number, coords, masked, octants, sink, boxes3)
     slots = pltpu.VMEM((4, VECS, 64), F32)
     quad3, close3, wide3 = call(
         lower_gather_kernel,
@@ -688,7 +685,7 @@
         [((VECS, 256), F32), ((144, 128), F32), ((80, 128), F32)],
         [slots],
         name="gather3",
-    )(number, boxes3, arrived, sink, near[-1])
+    )(number, boxes3, arrived, sink, pairs)
     others = [crossed(close3, 4), crossed(wide3, 8), crossed(wide3, 12)]
     near.append(near_part(parts[1], wide3))
     quad5, box7, inside, close5, wide5 = call(
@@ -705,15 +702,18 @@
         name="gather5",
     )(number, wide3, *others, sink, near[-1])
     beside5 = crossed(close5, 16)
-    facing = crossed(after(facing, box7), 1)
     near.append(near_part(parts[2], box7))
     boxes = jnp.stack([box7, after(beside5, near[-1])[:16]])
     arrived = crossed(boxes, 32)
+    facing = crossed(after(facing, boxes), 1)
     away = swapped(after(away, boxes), 1)
-    outer5 = swapped(after(wide5, boxes), 16)
     near.append(near_part(parts[3], boxes))
     boxes = jnp.concatenate([boxes, after(arrived, near[-1])], 0)
     arrived = crossed(boxes, 64)
+    outer5 = swapped(after(wide5, boxes), 16)
+    near.append(near_part(parts[4], boxes, facing, away))
+    boxes = jnp.concatenate([boxes, after(arrived, near[-1])], 0)
+    arrived = crossed(boxes, 128)
     halo = pltpu.VMEM((VECS, 1280), F32)
     base, far_local, path = call(
         functools.partial(rim_kernel, parts),
@@ -725,17 +725,14 @@
         number, coords, masked, coef, leaf_high, leaf_low, pairs, facing, away, layers,
         low_couplings, sink, octants, quad3, quad5, inside, beside5, outer5, *near, boxes,
     )
-    boxes = jnp.concatenate([boxes, after(arrived, base)], 0)
-    arrived = crossed(boxes, 128)
-    final = near_part(last, boxes)
     return call(
-        functools.partial(tail_kernel, last[0]),
-        [SMEM] + [VMEM] * 11,
+        tail_kernel,
+        [SMEM] + [VMEM] * 10,
         [((VECS, SLOTS), F32)],
         name="tail",
     )(
-        number, base, final, occupied, far_high, far_low, boxes, after(arrived, final), far_local,
-        path, high_couplings, sink,
+        number, base, occupied, far_high, far_low, boxes, after(arrived, base), far_local, path,
+        high_couplings, sink,
     )[0]
 
 

time: 62.9 us -> 57 us (0.906)
  the two profiles are of different devices: /device:TPU:64 before, /device:TPU:33 now
where the time goes in v3:
time: 57 us; the launch traced here: 56.7 us
  starting transfers between devices  28.7 us (50%)
  Pallas kernels  24.1 us (42%)
  local copies, waits for them, and re-layouts  2.59 us (5%)
  waiting for transfers between devices  1.01 us (2%)
    ppermute x10, starting transfers between devices, crossed(): return lax.ppermute(value, AXES, [(i, i ^ mask) for i in range(devices)])  17.3 us
    pallas_call x5, Pallas kernels, near_part(): call(functools.partial(near_kernel, begin, end), [VMEM, VMEM] + [ANY] * l...  12.2 us
    ppermute x2, starting transfers between devices, swapped(): return lax.ppermute(value, AXES, pairs)  11.4 us
    pallas_call x1, Pallas kernels, local(): call(functools.partial(rim_kernel, parts), [SMEM] + [VMEM] * (17 + len(pa...  3.76 us
    pallas_call x1, Pallas kernels, local(): call(leaf_kernel, [SMEM] + [VMEM] * 4 + [ANY], [((VECS, SLOTS), F32), ((6...  2.66 us
    unnamed x16, local copies, waits for them, and re-layouts  2.59 us
    pallas_call x1, Pallas kernels, local(): call(tail_kernel, [SMEM] + [VMEM] * 10, [((VECS, SLOTS), F32)], name='tail')  2.55 us
    pallas_call x1, Pallas kernels, local(): call(head_kernel, [SMEM, HBM, HBM, HBM], [((8, SLOTS), F32), ((VECS, SLOT...  1.79 us
  transfers between devices with their start and end apart: 12, of which 3 were waited for; matrix products, arithmetic and copies ran while one was open for 0% of the time, Pallas kernels for 33%

profile of v3, /device:TPU:33, one launch (start us, length us, event | category | flops | bytes accessed | tf_op | source)
XLA Modules:
  0.0 56.7 jit_solution(14369456070459249257)
XLA Ops:
  0.0 0.0 copy-start.7
  0.0 0.7 %copy-done.7 = s32[8,8]{1,0:T(8,128)S(1)} copy-done((s32[8,8]{1,0:T(8,128)S(1)}, s32[8,8]{1,0:T(8,128)}, u32[]{:S(2)}) %copy-start.7) | copy-done | bytes 280
  0.7 0.0 copy-start.2
  0.7 1.0 %copy-done.2 = f32[32,4096]{1,0:T(8,128)S(1)} copy-done((f32[32,4096]{1,0:T(8,128)S(1)}, f32[32,4096]{1,0:T(8,128)}, u32[]{:S(2)}) %copy-start.2) | copy-done | bytes 524312
  1.7 0.0 copy-start.6
  1.7 0.8 %copy-done.6 = f32[3,4096]{1,0:T(4,128)S(1)} copy-done((f32[3,4096]{1,0:T(4,128)S(1)}, f32[3,4096]{1,0:T(4,128)}, u32[]{:S(2)}) %copy-start.6) | copy-done | bytes 49176
  2.6 1.8 %head.1 = (f32[8,4096]{1,0:T(8,128)S(1)}, f32[32,4096]{1,0:T(8,128)S(1)}, f32[1,4096]{1,0:T(1,128)S(1)}, f32[16,128]{1,0:T(8,128)S(1)}, bf16[64,4096]{1,0:T(8,128)(2,1)S(1)}, /*index=5*/bf16[64,4096]{1,0:T(8,128)(2,1)S(1)}) custom-call(s32[1]{0:T(128)} %bitcast.1.slab_ref, s32[8,8]{1,0:T(8,128)S(1)} %copy-done.7, f32[3,4096]{1,0:T(4,128)S(1)} %copy-done.6, ...), custom_call_target="tpu_custom_call" | custom-call | tf_op jit(solution)/shard_map/head/pallas_call | solution.py:629
  4.4 1.3 %collective-permute-start = (f32[16,128]{1,0:T(8,128)S(1)}, f32[16,128]{1,0:T(8,128)S(1)}, u32[]{:S(2)}, u32[]{:S(2)}) collective-permute-start(f32[16,128]{1,0:T(8,128)S(1)} %get-tuple-element.38.refs_0_), channel_id=1, source_target_pairs={{0,1},{1,0},{2,3},{3,2},{4,5},{5,4},{6,7},{7,6},{8,9},{9,8},{10,11... | collective-permute-start | bytes 24584 | tf_op jit(solution)/shard_map/ppermute | solution.py:608
  5.7 0.0 copy-start.3
  5.7 2.4 %near.5.refs_0_ = f32[32,1024]{1,0:T(8,128)S(1)} custom-call(f32[8,4096]{1,0:T(8,128)S(1)} %get-tuple-element.36.coords_ref, f32[32,4096]{1,0:T(8,128)S(1)} %get-tuple-element.37.masked_ref, f32[16,128]{1,0:T(8,128)S(1)} %get-tuple-element.38.refs_0_), custom_call_target="tpu_custom_call" | custom-call | tf_op jit(solution)/shard_map/near/pallas_call | solution.py:655
  8.1 0.0 copy-start.1
  8.1 0.0 collective-permute-done
  8.1 2.5 %collective-permute-start.1 = (f32[2,16,128]{2,1,0:T(8,128)S(1)}, f32[2,16,128]{2,1,0:T(8,128)S(1)}, u32[]{:S(2)}, u32[]{:S(2)}) collective-permute-start(f32[2,16,128]{2,1,0:T(8,128)S(1)} %pad_maximum_fusion.2.hold_ref.own_ref), channel_id=1, source_target_pairs={{0,2},{1,3},{2,0},{3,1},{4,6},{5,7},{6,4},{7,5},{8,10},{9,11},{10,... | collective-permute-start | bytes 49160 | tf_op jit(solution)/shard_map/ppermute | solution.py:608
  10.7 0.0 copy-done.3
  10.7 0.0 copy-done.1
  10.7 2.7 %leaf.1 = (f32[32,4096]{1,0:T(8,128)S(1)}, bf16[64,4096]{1,0:T(8,128)(2,1)S(1)}, bf16[64,4096]{1,0:T(8,128)(2,1)S(1)}, f32[224,128]{1,0:T(8,128)S(1)}, f32[32,1280]{1,0:T(8,128)S(1)}, /*index=5*/f32[32,1280]{1,0:T(8,128)S(1)}) custom-call(s32[1]{0:T(128)} %bitcast.index_ref, f32[8,4096]{1,0:T(8,128)S(1)} %get-tuple-element.36.coords_ref, ...), custom_call_target="tpu_custom_call" | custom-call | tf_op jit(solution)/shard_map/leaf/pallas_call | solution.py:668
  13.3 0.0 collective-permute-done.1.far_ref
  13.4 0.6 gather3.1
  13.9 1.2 %collective-permute-start.2 = (f32[144,128]{1,0:T(8,128)S(1)}, f32[144,128]{1,0:T(8,128)S(1)}, u32[]{:S(2)}, u32[]{:S(2)}) collective-permute-start(f32[144,128]{1,0:T(8,128)S(1)} %get-tuple-element.46), channel_id=1, source_target_pairs={{0,4},{1,5},{2,6},{3,7},{4,0},{5,1},{6,2},{7,3},{8,12},{9,13},{10,... | collective-permute-start | bytes 221192 | tf_op jit(solution)/shard_map/ppermute | solution.py:608
  15.2 1.2 %collective-permute-start.4 = (f32[80,128]{1,0:T(8,128)S(1)}, f32[80,128]{1,0:T(8,128)S(1)}, u32[]{:S(2)}, u32[]{:S(2)}) collective-permute-start(f32[80,128]{1,0:T(8,128)S(1)} %get-tuple-element.45.refs_0_.own_ref), channel_id=1, source_target_pairs={{0,12},{1,13},{2,14},{3,15},{4,8},{5,9},{6,10},{7,11},{8,4},{9,5},... | collective-permute-start | bytes 122888 | tf_op jit(solution)/shard_map/ppermute | solution.py:608
  16.4 0.2 collective-permute-start.3
  16.5 2.4 %near.6.hold_ref.refs_1_ = f32[32,1024]{1,0:T(8,128)S(1)} custom-call(f32[8,4096]{1,0:T(8,128)S(1)} %get-tuple-element.36.coords_ref, f32[32,4096]{1,0:T(8,128)S(1)} %get-tuple-element.37.masked_ref, f32[80,128]{1,0:T(8,128)S(1)} %get-tuple-element.45.refs_0_.own_ref), custom_call_target="tpu_custom_call" | custom-call | tf_op jit(solution)/shard_map/near/pallas_call | solution.py:655
  19.0 0.0 collective-permute-done.4.three_ref
  19.0 0.2 collective-permute-done.3.two_ref
  19.2 0.0 collective-permute-done.2.one_ref
  19.2 0.5 gather5.1
  19.8 2.8 %collective-permute-start.5 = (f32[144,128]{1,0:T(8,128)S(1)}, f32[144,128]{1,0:T(8,128)S(1)}, u32[]{:S(2)}, u32[]{:S(2)}) collective-permute-start(f32[144,128]{1,0:T(8,128)S(1)} %get-tuple-element.48), channel_id=1, source_target_pairs={{0,16},{1,17},{2,18},{3,19},{4,20},{5,21},{6,22},{7,23},{8,24},{9,... | collective-permute-start | bytes 221192 | tf_op jit(solution)/shard_map/ppermute | solution.py:608
  22.5 3.1 %near.7.refs_2_ = f32[32,1280]{1,0:T(8,128)S(1)} custom-call(f32[8,4096]{1,0:T(8,128)S(1)} %get-tuple-element.36.coords_ref, f32[32,4096]{1,0:T(8,128)S(1)} %get-tuple-element.37.masked_ref, f32[16,128]{1,0:T(8,128)S(1)} %get-tuple-element.47.refs_0_), custom_call_target="tpu_custom_call" | custom-call | tf_op jit(solution)/shard_map/near/pallas_call | solution.py:655
  25.7 0.0 collective-permute-done.5.close_ref
  25.7 0.0 copy-start
  25.7 0.7 %collective-permute-start.6 = (f32[32,1280]{1,0:T(8,128)S(1)}, f32[32,1280]{1,0:T(8,128)S(1)}, u32[]{:S(2)}, u32[]{:S(2)}) collective-permute-start(f32[32,1280]{1,0:T(8,128)S(1)} %get-tuple-element.50), channel_id=1, source_target_pairs={{0,1},{1,0},{2,3},{3,2},{4,5},{5,4},{6,7},{7,6},{8,9},{9,8},{10,11... | collective-permute-start | bytes 491528 | tf_op jit(solution)/shard_map/ppermute | solution.py:608
  26.4 5.8 %collective-permute-start.7 = (f32[32,1280]{1,0:T(8,128)S(1)}, f32[32,1280]{1,0:T(8,128)S(1)}, u32[]{:S(2)}, u32[]{:S(2)}) collective-permute-start(f32[32,1280]{1,0:T(8,128)S(1)} %get-tuple-element.52), channel_id=1, source_target_pairs={{1,2},{2,1},{3,4},{4,3},{5,6},{6,5},{7,8},{8,7},{9,10},{10,9},{11,... | collective-permute-start | bytes 491528 | tf_op jit(solution)/shard_map/ppermute | solution.py:614
  32.2 0.1 collective-permute-start.8
  32.3 2.4 %near.8.refs_3_ = f32[32,1024]{1,0:T(8,128)S(1)} custom-call(f32[8,4096]{1,0:T(8,128)S(1)} %get-tuple-element.36.coords_ref, f32[32,4096]{1,0:T(8,128)S(1)} %get-tuple-element.37.masked_ref, f32[2,16,128]{2,1,0:T(8,128)S(1)} %pad_maximum_fusion.3.refs_0_), custom_call_target="tpu_custom_call" | custom-call | tf_op jit(solution)/shard_map/near/pallas_call | solution.py:655
  34.7 0.2 collective-permute-done.8
  34.9 3.0 %collective-permute-start.10 = (f32[4,16,128]{2,1,0:T(8,128)S(1)}, f32[4,16,128]{2,1,0:T(8,128)S(1)}, u32[]{:S(2)}, u32[]{:S(2)}) collective-permute-start(f32[4,16,128]{2,1,0:T(8,128)S(1)} %pad_maximum_fusion.1.refs_0_), channel_id=1, source_target_pairs={{0,64},{1,65},{2,66},{3,67},{4,68},{5,69},{6,70},{7,71},{8,72},{9,... | collective-permute-start | bytes 98312 | tf_op jit(solution)/shard_map/ppermute | solution.py:608
  37.9 0.0 copy-start.4
  37.9 5.7 %collective-permute-start.9 = (f32[128,128]{1,0:T(8,128)S(1)}, f32[128,128]{1,0:T(8,128)S(1)}, u32[]{:S(2)}, u32[]{:S(2)}) collective-permute-start(f32[128,128]{1,0:T(8,128)S(1)} %get-tuple-element.58), channel_id=1, source_target_pairs={{16,32},{17,33},{18,34},{19,35},{20,36},{21,37},{22,38},{23,39},{2... | collective-permute-start | bytes 196616 | tf_op jit(solution)/shard_map/ppermute | solution.py:614
  43.5 0.0 collective-permute-done.6.refs_1_.facing_ref
  43.6 0.0 collective-permute-done.7.refs_2_.away_ref
  43.6 1.9 %near.9.refs_4_ = f32[32,768]{1,0:T(8,128)S(1)} custom-call(f32[8,4096]{1,0:T(8,128)S(1)} %get-tuple-element.36.coords_ref, f32[32,4096]{1,0:T(8,128)S(1)} %get-tuple-element.37.masked_ref, f32[4,16,128]{2,1,0:T(8,128)S(1)} %pad_maximum_fusion.1.refs_0_, f32[32,1280]{1,0:T(8,128)S(1)} %collective-permute-done.6.refs_1_.facing_ref, ...), custom_call_target="tpu_custom_call" | custom-call | tf_op jit(solution)/shard_map/near/pallas_call | solution.py:655
  45.5 0.0 collective-permute-done.10
  45.5 4.3 %collective-permute-start.11 = (f32[8,16,128]{2,1,0:T(8,128)S(1)}, f32[8,16,128]{2,1,0:T(8,128)S(1)}, u32[]{:S(2)}, u32[]{:S(2)}) collective-permute-start(f32[8,16,128]{2,1,0:T(8,128)S(1)} %pad_maximum_fusion.refs_5_.boxes_ref), channel_id=1, source_target_pairs={{0,128},{1,129},{2,130},{3,131},{4,132},{5,133},{6,134},{7,135},{8... | collective-permute-start | bytes 196616 | tf_op jit(solution)/shard_map/ppermute | solution.py:608
  49.8 0.0 collective-permute-done.9.wide_ref
  49.8 0.0 copy-done
  49.8 0.0 copy-done.4
  49.8 0.0 copy-start.5
  49.8 3.8 %rim.1 = (f32[32,4096]{1,0:T(8,128)S(1)}, f32[32,64]{1,0:T(8,128)S(1)}, f32[64,64]{1,0:T(8,128)S(1)}) custom-call(s32[1]{0:T(128)} %bitcast.index_ref, f32[8,4096]{1,0:T(8,128)S(1)} %get-tuple-element.36.coords_ref, f32[32,4096]{1,0:T(8,128)S(1)} %get-tuple-element.37.masked_ref, f32[32,4096]{1,0:T(8,128)S(1)} %get-tuple-element.40.coef_ref, ...), custom_call_target="tpu_custom_call" | custom-call | tf_op jit(solution)/shard_map/rim/pallas_call | solution.py:718
  53.6 0.5 collective-permute-done.11.far_ref
  54.1 0.0 copy-done.5
  54.1 2.5 %tail.1 = f32[32,4096]{1,0:T(8,128)} custom-call(s32[1]{0:T(128)} %bitcast.index_ref, f32[32,4096]{1,0:T(8,128)S(1)} %get-tuple-element.60.base_ref, f32[1,4096]{1,0:T(1,128)S(1)} %get-tuple-element.61.occ_ref, bf16[64,4096]{1,0:T(8,128)(2,1)S(1)} %get-tuple-element.62.high_ref, bf16[64,4096]{1,0:T(8,128)(2,1)S(1)} %get-tuple-element.63.low_ref, ...), custom_call_target="tpu_custom_call" | custom-call | tf_op jit(solution)/shard_map/tail/pallas_call | solution.py:728
  (5 shorter events, 0.0 us)
Async XLA Ops:
  0.0 0.7 %copy-start.7 = (s32[8,8]{1,0:T(8,128)S(1)}, s32[8,8]{1,0:T(8,128)}, u32[]{:S(2)}) copy-start(s32[8,8]{1,0:T(8,128)} %counts_hbm.1) | copy-start | bytes 772
  0.7 1.0 %copy-start.2 = (f32[32,4096]{1,0:T(8,128)S(1)}, f32[32,4096]{1,0:T(8,128)}, u32[]{:S(2)}) copy-start(f32[32,4096]{1,0:T(8,128)} %vectors_hbm.1) | copy-start | bytes 1572868
  1.7 0.8 %copy-start.6 = (f32[3,4096]{1,0:T(4,128)S(1)}, f32[3,4096]{1,0:T(4,128)}, u32[]{:S(2)}) copy-start(f32[3,4096]{1,0:T(4,128)} %points_hbm.1) | copy-start | bytes 147460
  4.4 3.7 %collective-permute-start = (f32[16,128]{1,0:T(8,128)S(1)}, f32[16,128]{1,0:T(8,128)S(1)}, u32[]{:S(2)}, u32[]{:S(2)}) collective-permute-start(f32[16,128]{1,0:T(8,128)S(1)} %get-tuple-element.38.refs_0_), channel_id=1, source_target_pairs={{0,1},{1,0},{2,3},{3,2},{4,5},{5,4},{6,7},{7,6},{8,9},{9,8},{10,11... | collective-permute-start | bytes 24584 | tf_op jit(solution)/shard_map/ppermute | solution.py:608
  5.7 5.0 %copy-start.3 = (bf16[2,64,512]{2,1,0:T(8,128)(2,1)S(1)}, bf16[2,64,512]{2,1,0:T(8,128)(2,1)}, u32[]{:S(2)}) copy-start(bf16[2,64,512]{2,1,0:T(8,128)(2,1)} %constant.23.clone.octants_ref) | copy-start | bytes 393220
  8.1 2.6 %copy-start.1 = (bf16[2,64,128]{2,1,0:T(8,128)(2,1)S(1)}, bf16[2,64,128]{2,1,0:T(8,128)(2,1)}, u32[]{:S(2)}) copy-start(bf16[2,64,128]{2,1,0:T(8,128)(2,1)} %constant.24.clone.sink_ref) | copy-start | bytes 98308
  8.1 5.2 %collective-permute-start.1 = (f32[2,16,128]{2,1,0:T(8,128)S(1)}, f32[2,16,128]{2,1,0:T(8,128)S(1)}, u32[]{:S(2)}, u32[]{:S(2)}) collective-permute-start(f32[2,16,128]{2,1,0:T(8,128)S(1)} %pad_maximum_fusion.2.hold_ref.own_ref), channel_id=1, source_target_pairs={{0,2},{1,3},{2,0},{3,1},{4,6},{5,7},{6,4},{7,5},{8,10},{9,11},{10,... | collective-permute-start | bytes 49160 | tf_op jit(solution)/shard_map/ppermute | solution.py:608
  13.9 5.3 %collective-permute-start.2 = (f32[144,128]{1,0:T(8,128)S(1)}, f32[144,128]{1,0:T(8,128)S(1)}, u32[]{:S(2)}, u32[]{:S(2)}) collective-permute-start(f32[144,128]{1,0:T(8,128)S(1)} %get-tuple-element.46), channel_id=1, source_target_pairs={{0,4},{1,5},{2,6},{3,7},{4,0},{5,1},{6,2},{7,3},{8,12},{9,13},{10,... | collective-permute-start | bytes 221192 | tf_op jit(solution)/shard_map/ppermute | solution.py:608
  15.2 3.8 %collective-permute-start.4 = (f32[80,128]{1,0:T(8,128)S(1)}, f32[80,128]{1,0:T(8,128)S(1)}, u32[]{:S(2)}, u32[]{:S(2)}) collective-permute-start(f32[80,128]{1,0:T(8,128)S(1)} %get-tuple-element.45.refs_0_.own_ref), channel_id=1, source_target_pairs={{0,12},{1,13},{2,14},{3,15},{4,8},{5,9},{6,10},{7,11},{8,4},{9,5},... | collective-permute-start | bytes 122888 | tf_op jit(solution)/shard_map/ppermute | solution.py:608
  16.4 2.9 %collective-permute-start.3 = (f32[80,128]{1,0:T(8,128)S(1)}, f32[80,128]{1,0:T(8,128)S(1)}, u32[]{:S(2)}, u32[]{:S(2)}) collective-permute-start(f32[80,128]{1,0:T(8,128)S(1)} %get-tuple-element.45.refs_0_.own_ref), channel_id=1, source_target_pairs={{0,8},{1,9},{2,10},{3,11},{4,12},{5,13},{6,14},{7,15},{8,0},{9,1},... | collective-permute-start | bytes 122888 | tf_op jit(solution)/shard_map/ppermute | solution.py:608
  19.8 5.9 %collective-permute-start.5 = (f32[144,128]{1,0:T(8,128)S(1)}, f32[144,128]{1,0:T(8,128)S(1)}, u32[]{:S(2)}, u32[]{:S(2)}) collective-permute-start(f32[144,128]{1,0:T(8,128)S(1)} %get-tuple-element.48), channel_id=1, source_target_pairs={{0,16},{1,17},{2,18},{3,19},{4,20},{5,21},{6,22},{7,23},{8,24},{9,... | collective-permute-start | bytes 221192 | tf_op jit(solution)/shard_map/ppermute | solution.py:608
  25.7 24.1 %copy-start = (bf16[14,256,128]{2,1,0:T(8,128)(2,1)S(1)}, bf16[14,256,128]{2,1,0:T(8,128)(2,1)}, u32[]{:S(2)}) copy-start(bf16[14,256,128]{2,1,0:T(8,128)(2,1)} %constant.26.clone.coupling_ref) | copy-start | bytes 2752516
  25.7 17.8 %collective-permute-start.6 = (f32[32,1280]{1,0:T(8,128)S(1)}, f32[32,1280]{1,0:T(8,128)S(1)}, u32[]{:S(2)}, u32[]{:S(2)}) collective-permute-start(f32[32,1280]{1,0:T(8,128)S(1)} %get-tuple-element.50), channel_id=1, source_target_pairs={{0,1},{1,0},{2,3},{3,2},{4,5},{5,4},{6,7},{7,6},{8,9},{9,8},{10,11... | collective-permute-start | bytes 491528 | tf_op jit(solution)/shard_map/ppermute | solution.py:608
  26.4 17.1 %collective-permute-start.7 = (f32[32,1280]{1,0:T(8,128)S(1)}, f32[32,1280]{1,0:T(8,128)S(1)}, u32[]{:S(2)}, u32[]{:S(2)}) collective-permute-start(f32[32,1280]{1,0:T(8,128)S(1)} %get-tuple-element.52), channel_id=1, source_target_pairs={{1,2},{2,1},{3,4},{4,3},{5,6},{6,5},{7,8},{8,7},{9,10},{10,9},{11,... | collective-permute-start | bytes 491528 | tf_op jit(solution)/shard_map/ppermute | solution.py:614
  32.2 2.7 %collective-permute-start.8 = (f32[2,16,128]{2,1,0:T(8,128)S(1)}, f32[2,16,128]{2,1,0:T(8,128)S(1)}, u32[]{:S(2)}, u32[]{:S(2)}) collective-permute-start(f32[2,16,128]{2,1,0:T(8,128)S(1)} %pad_maximum_fusion.3.refs_0_), channel_id=1, source_target_pairs={{0,32},{1,33},{2,34},{3,35},{4,36},{5,37},{6,38},{7,39},{8,40},{9,... | collective-permute-start | bytes 49160 | tf_op jit(solution)/shard_map/ppermute | solution.py:608
  34.9 10.6 %collective-permute-start.10 = (f32[4,16,128]{2,1,0:T(8,128)S(1)}, f32[4,16,128]{2,1,0:T(8,128)S(1)}, u32[]{:S(2)}, u32[]{:S(2)}) collective-permute-start(f32[4,16,128]{2,1,0:T(8,128)S(1)} %pad_maximum_fusion.1.refs_0_), channel_id=1, source_target_pairs={{0,64},{1,65},{2,66},{3,67},{4,68},{5,69},{6,70},{7,71},{8,72},{9,... | collective-permute-start | bytes 98312 | tf_op jit(solution)/shard_map/ppermute | solution.py:608
  37.9 11.9 %copy-start.4 = (bf16[4,256,256]{2,1,0:T(8,128)(2,1)S(1)}, bf16[4,256,256]{2,1,0:T(8,128)(2,1)}, u32[]{:S(2)}) copy-start(bf16[4,256,256]{2,1,0:T(8,128)(2,1)} %constant.25.clone.layers_ref) | copy-start | bytes 1572868
  37.9 11.9 %collective-permute-start.9 = (f32[128,128]{1,0:T(8,128)S(1)}, f32[128,128]{1,0:T(8,128)S(1)}, u32[]{:S(2)}, u32[]{:S(2)}) collective-permute-start(f32[128,128]{1,0:T(8,128)S(1)} %get-tuple-element.58), channel_id=1, source_target_pairs={{16,32},{17,33},{18,34},{19,35},{20,36},{21,37},{22,38},{23,39},{2... | collective-permute-start | bytes 196616 | tf_op jit(solution)/shard_map/ppermute | solution.py:614
  45.5 8.6 %collective-permute-start.11 = (f32[8,16,128]{2,1,0:T(8,128)S(1)}, f32[8,16,128]{2,1,0:T(8,128)S(1)}, u32[]{:S(2)}, u32[]{:S(2)}) collective-permute-start(f32[8,16,128]{2,1,0:T(8,128)S(1)} %pad_maximum_fusion.refs_5_.boxes_ref), channel_id=1, source_target_pairs={{0,128},{1,129},{2,130},{3,131},{4,132},{5,133},{6,134},{7,135},{8... | collective-permute-start | bytes 196616 | tf_op jit(solution)/shard_map/ppermute | solution.py:608
  49.8 4.3 %copy-start.5 = (bf16[6,256,128]{2,1,0:T(8,128)(2,1)S(1)}, bf16[6,256,128]{2,1,0:T(8,128)(2,1)}, u32[]{:S(2)}) copy-start(bf16[6,256,128]{2,1,0:T(8,128)(2,1)} %constant.27.clone.coupling_ref) | copy-start | bytes 1179652

commit v4 on v3

--- a/solution.py
+++ b/solution.py
@@ -660,7 +660,7 @@
             name="near",
         )(coords, masked, *holds)[0]
 
-    parts = [(0, 3), (3, 6), (6, 10), (10, 13), (13, 16)]
+    parts = [(0, 4), (4, 7), (7, 11), (11, 14), (14, 16)]
     arrived = crossed(box3, 1)
     near = [near_part(parts[0], box3)]
     boxes3 = jnp.stack([box3, after(arrived, near[0])])

time: 57 us -> 56.7 us (level)
  no operation moved by 1% of the time
where the time goes in v4:
time: 56.7 us; the launch traced here: 56.4 us
  starting transfers between devices  28.7 us (51%)
  Pallas kernels  24 us (42%)
  local copies, waits for them, and re-layouts  2.59 us (5%)
  waiting for transfers between devices  0.77 us (1%)
    ppermute x10, starting transfers between devices, crossed(): return lax.ppermute(value, AXES, [(i, i ^ mask) for i in range(devices)])  16.7 us
    pallas_call x5, Pallas kernels, near_part(): call(functools.partial(near_kernel, begin, end), [VMEM, VMEM] + [ANY] * l...  12.2 us
    ppermute x2, starting transfers between devices, swapped(): return lax.ppermute(value, AXES, pairs)  12 us
    pallas_call x1, Pallas kernels, local(): call(functools.partial(rim_kernel, parts), [SMEM] + [VMEM] * (17 + len(pa...  3.77 us
    pallas_call x1, Pallas kernels, local(): call(leaf_kernel, [SMEM] + [VMEM] * 4 + [ANY], [((VECS, SLOTS), F32), ((6...  2.66 us
    unnamed x16, local copies, waits for them, and re-layouts  2.59 us
    pallas_call x1, Pallas kernels, local(): call(tail_kernel, [SMEM] + [VMEM] * 10, [((VECS, SLOTS), F32)], name='tail')  2.54 us
    pallas_call x1, Pallas kernels, local(): call(head_kernel, [SMEM, HBM, HBM, HBM], [((8, SLOTS), F32), ((VECS, SLOT...  1.79 us
  transfers between devices with their start and end apart: 12, of which 3 were waited for; matrix products, arithmetic and copies ran while one was open for 0% of the time, Pallas kernels for 33%

profile of v4, /device:TPU:33, one launch (start us, length us, event | category | flops | bytes accessed | tf_op | source)
XLA Modules:
  0.0 56.4 jit_solution(3502511124826485317)
XLA Ops:
  0.0 0.0 copy-start.7
  0.0 0.7 %copy-done.7 = s32[8,8]{1,0:T(8,128)S(1)} copy-done((s32[8,8]{1,0:T(8,128)S(1)}, s32[8,8]{1,0:T(8,128)}, u32[]{:S(2)}) %copy-start.7) | copy-done | bytes 280
  0.7 0.0 copy-start.2
  0.7 1.0 %copy-done.2 = f32[32,4096]{1,0:T(8,128)S(1)} copy-done((f32[32,4096]{1,0:T(8,128)S(1)}, f32[32,4096]{1,0:T(8,128)}, u32[]{:S(2)}) %copy-start.2) | copy-done | bytes 524312
  1.7 0.0 copy-start.6
  1.7 0.8 %copy-done.6 = f32[3,4096]{1,0:T(4,128)S(1)} copy-done((f32[3,4096]{1,0:T(4,128)S(1)}, f32[3,4096]{1,0:T(4,128)}, u32[]{:S(2)}) %copy-start.6) | copy-done | bytes 49176
  2.6 1.8 %head.1 = (f32[8,4096]{1,0:T(8,128)S(1)}, f32[32,4096]{1,0:T(8,128)S(1)}, f32[1,4096]{1,0:T(1,128)S(1)}, f32[16,128]{1,0:T(8,128)S(1)}, bf16[64,4096]{1,0:T(8,128)(2,1)S(1)}, /*index=5*/bf16[64,4096]{1,0:T(8,128)(2,1)S(1)}) custom-call(s32[1]{0:T(128)} %bitcast.1.slab_ref, s32[8,8]{1,0:T(8,128)S(1)} %copy-done.7, f32[3,4096]{1,0:T(4,128)S(1)} %copy-done.6, ...), custom_call_target="tpu_custom_call" | custom-call | tf_op jit(solution)/shard_map/head/pallas_call | solution.py:629
  4.4 1.3 %collective-permute-start = (f32[16,128]{1,0:T(8,128)S(1)}, f32[16,128]{1,0:T(8,128)S(1)}, u32[]{:S(2)}, u32[]{:S(2)}) collective-permute-start(f32[16,128]{1,0:T(8,128)S(1)} %get-tuple-element.38.refs_0_), channel_id=1, source_target_pairs={{0,1},{1,0},{2,3},{3,2},{4,5},{5,4},{6,7},{7,6},{8,9},{9,8},{10,11... | collective-permute-start | bytes 24584 | tf_op jit(solution)/shard_map/ppermute | solution.py:608
  5.7 0.0 copy-start.3
  5.7 3.1 %near.5.refs_0_ = f32[32,1280]{1,0:T(8,128)S(1)} custom-call(f32[8,4096]{1,0:T(8,128)S(1)} %get-tuple-element.36.coords_ref, f32[32,4096]{1,0:T(8,128)S(1)} %get-tuple-element.37.masked_ref, f32[16,128]{1,0:T(8,128)S(1)} %get-tuple-element.38.refs_0_), custom_call_target="tpu_custom_call" | custom-call | tf_op jit(solution)/shard_map/near/pallas_call | solution.py:655
  8.8 0.0 copy-start.1
  8.8 0.0 collective-permute-done
  8.8 2.5 %collective-permute-start.1 = (f32[2,16,128]{2,1,0:T(8,128)S(1)}, f32[2,16,128]{2,1,0:T(8,128)S(1)}, u32[]{:S(2)}, u32[]{:S(2)}) collective-permute-start(f32[2,16,128]{2,1,0:T(8,128)S(1)} %pad_maximum_fusion.2.hold_ref.own_ref), channel_id=1, source_target_pairs={{0,2},{1,3},{2,0},{3,1},{4,6},{5,7},{6,4},{7,5},{8,10},{9,11},{10,... | collective-permute-start | bytes 49160 | tf_op jit(solution)/shard_map/ppermute | solution.py:608
  11.4 0.0 copy-done.3
  11.4 0.0 copy-done.1
  11.4 2.7 %leaf.1 = (f32[32,4096]{1,0:T(8,128)S(1)}, bf16[64,4096]{1,0:T(8,128)(2,1)S(1)}, bf16[64,4096]{1,0:T(8,128)(2,1)S(1)}, f32[224,128]{1,0:T(8,128)S(1)}, f32[32,1280]{1,0:T(8,128)S(1)}, /*index=5*/f32[32,1280]{1,0:T(8,128)S(1)}) custom-call(s32[1]{0:T(128)} %bitcast.index_ref, f32[8,4096]{1,0:T(8,128)S(1)} %get-tuple-element.36.coords_ref, ...), custom_call_target="tpu_custom_call" | custom-call | tf_op jit(solution)/shard_map/leaf/pallas_call | solution.py:668
  14.0 0.0 collective-permute-done.1.far_ref
  14.1 0.6 gather3.1
  14.6 1.3 %collective-permute-start.2 = (f32[144,128]{1,0:T(8,128)S(1)}, f32[144,128]{1,0:T(8,128)S(1)}, u32[]{:S(2)}, u32[]{:S(2)}) collective-permute-start(f32[144,128]{1,0:T(8,128)S(1)} %get-tuple-element.46), channel_id=1, source_target_pairs={{0,4},{1,5},{2,6},{3,7},{4,0},{5,1},{6,2},{7,3},{8,12},{9,13},{10,... | collective-permute-start | bytes 221192 | tf_op jit(solution)/shard_map/ppermute | solution.py:608
  15.9 1.2 %collective-permute-start.4 = (f32[80,128]{1,0:T(8,128)S(1)}, f32[80,128]{1,0:T(8,128)S(1)}, u32[]{:S(2)}, u32[]{:S(2)}) collective-permute-start(f32[80,128]{1,0:T(8,128)S(1)} %get-tuple-element.45.refs_0_.own_ref), channel_id=1, source_target_pairs={{0,12},{1,13},{2,14},{3,15},{4,8},{5,9},{6,10},{7,11},{8,4},{9,5},... | collective-permute-start | bytes 122888 | tf_op jit(solution)/shard_map/ppermute | solution.py:608
  17.1 0.2 collective-permute-start.3
  17.3 2.4 %near.6.hold_ref.refs_1_ = f32[32,1024]{1,0:T(8,128)S(1)} custom-call(f32[8,4096]{1,0:T(8,128)S(1)} %get-tuple-element.36.coords_ref, f32[32,4096]{1,0:T(8,128)S(1)} %get-tuple-element.37.masked_ref, f32[80,128]{1,0:T(8,128)S(1)} %get-tuple-element.45.refs_0_.own_ref), custom_call_target="tpu_custom_call" | custom-call | tf_op jit(solution)/shard_map/near/pallas_call | solution.py:655
  19.7 0.0 collective-permute-done.4.three_ref
  19.7 0.2 collective-permute-done.3.two_ref
  19.9 0.0 collective-permute-done.2.one_ref
  19.9 0.5 gather5.1
  20.5 2.8 %collective-permute-start.5 = (f32[144,128]{1,0:T(8,128)S(1)}, f32[144,128]{1,0:T(8,128)S(1)}, u32[]{:S(2)}, u32[]{:S(2)}) collective-permute-start(f32[144,128]{1,0:T(8,128)S(1)} %get-tuple-element.48), channel_id=1, source_target_pairs={{0,16},{1,17},{2,18},{3,19},{4,20},{5,21},{6,22},{7,23},{8,24},{9,... | collective-permute-start | bytes 221192 | tf_op jit(solution)/shard_map/ppermute | solution.py:608
  23.2 3.1 %near.7.refs_2_ = f32[32,1280]{1,0:T(8,128)S(1)} custom-call(f32[8,4096]{1,0:T(8,128)S(1)} %get-tuple-element.36.coords_ref, f32[32,4096]{1,0:T(8,128)S(1)} %get-tuple-element.37.masked_ref, f32[16,128]{1,0:T(8,128)S(1)} %get-tuple-element.47.refs_0_), custom_call_target="tpu_custom_call" | custom-call | tf_op jit(solution)/shard_map/near/pallas_call | solution.py:655
  26.4 0.0 collective-permute-done.5.close_ref
  26.4 0.0 copy-start
  26.4 0.1 collective-permute-start.6
  26.6 6.4 %collective-permute-start.7 = (f32[32,1280]{1,0:T(8,128)S(1)}, f32[32,1280]{1,0:T(8,128)S(1)}, u32[]{:S(2)}, u32[]{:S(2)}) collective-permute-start(f32[32,1280]{1,0:T(8,128)S(1)} %get-tuple-element.52), channel_id=1, source_target_pairs={{1,2},{2,1},{3,4},{4,3},{5,6},{6,5},{7,8},{8,7},{9,10},{10,9},{11,... | collective-permute-start | bytes 491528 | tf_op jit(solution)/shard_map/ppermute | solution.py:614
  32.9 0.1 collective-permute-start.8
  33.0 2.4 %near.8.refs_3_ = f32[32,1024]{1,0:T(8,128)S(1)} custom-call(f32[8,4096]{1,0:T(8,128)S(1)} %get-tuple-element.36.coords_ref, f32[32,4096]{1,0:T(8,128)S(1)} %get-tuple-element.37.masked_ref, f32[2,16,128]{2,1,0:T(8,128)S(1)} %pad_maximum_fusion.3.refs_0_), custom_call_target="tpu_custom_call" | custom-call | tf_op jit(solution)/shard_map/near/pallas_call | solution.py:655
  35.4 0.2 collective-permute-done.8
  35.6 3.0 %collective-permute-start.10 = (f32[4,16,128]{2,1,0:T(8,128)S(1)}, f32[4,16,128]{2,1,0:T(8,128)S(1)}, u32[]{:S(2)}, u32[]{:S(2)}) collective-permute-start(f32[4,16,128]{2,1,0:T(8,128)S(1)} %pad_maximum_fusion.1.refs_0_), channel_id=1, source_target_pairs={{0,64},{1,65},{2,66},{3,67},{4,68},{5,69},{6,70},{7,71},{8,72},{9,... | collective-permute-start | bytes 98312 | tf_op jit(solution)/shard_map/ppermute | solution.py:608
  38.6 0.0 copy-start.4
  38.6 5.7 %collective-permute-start.9 = (f32[128,128]{1,0:T(8,128)S(1)}, f32[128,128]{1,0:T(8,128)S(1)}, u32[]{:S(2)}, u32[]{:S(2)}) collective-permute-start(f32[128,128]{1,0:T(8,128)S(1)} %get-tuple-element.58), channel_id=1, source_target_pairs={{16,32},{17,33},{18,34},{19,35},{20,36},{21,37},{22,38},{23,39},{2... | collective-permute-start | bytes 196616 | tf_op jit(solution)/shard_map/ppermute | solution.py:614
  44.3 0.0 collective-permute-done.6.refs_1_.facing_ref
  44.3 0.0 collective-permute-done.7.refs_2_.away_ref
  44.3 1.1 %near.9.refs_4_ = f32[32,512]{1,0:T(8,128)S(1)} custom-call(f32[8,4096]{1,0:T(8,128)S(1)} %get-tuple-element.36.coords_ref, f32[32,4096]{1,0:T(8,128)S(1)} %get-tuple-element.37.masked_ref, f32[4,16,128]{2,1,0:T(8,128)S(1)} %pad_maximum_fusion.1.refs_0_, f32[32,1280]{1,0:T(8,128)S(1)} %collective-permute-done.6.refs_1_.facing_ref, ...), custom_call_target="tpu_custom_call" | custom-call | tf_op jit(solution)/shard_map/near/pallas_call | solution.py:655
  45.4 0.0 collective-permute-done.10
  45.4 4.3 %collective-permute-start.11 = (f32[8,16,128]{2,1,0:T(8,128)S(1)}, f32[8,16,128]{2,1,0:T(8,128)S(1)}, u32[]{:S(2)}, u32[]{:S(2)}) collective-permute-start(f32[8,16,128]{2,1,0:T(8,128)S(1)} %pad_maximum_fusion.refs_5_.boxes_ref), channel_id=1, source_target_pairs={{0,128},{1,129},{2,130},{3,131},{4,132},{5,133},{6,134},{7,135},{8... | collective-permute-start | bytes 196616 | tf_op jit(solution)/shard_map/ppermute | solution.py:608
  49.7 0.0 collective-permute-done.9.wide_ref
  49.7 0.0 copy-done
  49.7 0.0 copy-done.4
  49.7 0.0 copy-start.5
  49.7 3.8 %rim.1 = (f32[32,4096]{1,0:T(8,128)S(1)}, f32[32,64]{1,0:T(8,128)S(1)}, f32[64,64]{1,0:T(8,128)S(1)}) custom-call(s32[1]{0:T(128)} %bitcast.index_ref, f32[8,4096]{1,0:T(8,128)S(1)} %get-tuple-element.36.coords_ref, f32[32,4096]{1,0:T(8,128)S(1)} %get-tuple-element.37.masked_ref, f32[32,4096]{1,0:T(8,128)S(1)} %get-tuple-element.40.coef_ref, ...), custom_call_target="tpu_custom_call" | custom-call | tf_op jit(solution)/shard_map/rim/pallas_call | solution.py:718
  53.5 0.3 collective-permute-done.11.far_ref
  53.8 0.0 copy-done.5
  53.8 2.5 %tail.1 = f32[32,4096]{1,0:T(8,128)} custom-call(s32[1]{0:T(128)} %bitcast.index_ref, f32[32,4096]{1,0:T(8,128)S(1)} %get-tuple-element.60.base_ref, f32[1,4096]{1,0:T(1,128)S(1)} %get-tuple-element.61.occ_ref, bf16[64,4096]{1,0:T(8,128)(2,1)S(1)} %get-tuple-element.62.high_ref, bf16[64,4096]{1,0:T(8,128)(2,1)S(1)} %get-tuple-element.63.low_ref, ...), custom_call_target="tpu_custom_call" | custom-call | tf_op jit(solution)/shard_map/tail/pallas_call | solution.py:728
  (5 shorter events, 0.1 us)
Async XLA Ops:
  0.0 0.7 %copy-start.7 = (s32[8,8]{1,0:T(8,128)S(1)}, s32[8,8]{1,0:T(8,128)}, u32[]{:S(2)}) copy-start(s32[8,8]{1,0:T(8,128)} %counts_hbm.1) | copy-start | bytes 772
  0.7 1.0 %copy-start.2 = (f32[32,4096]{1,0:T(8,128)S(1)}, f32[32,4096]{1,0:T(8,128)}, u32[]{:S(2)}) copy-start(f32[32,4096]{1,0:T(8,128)} %vectors_hbm.1) | copy-start | bytes 1572868
  1.7 0.8 %copy-start.6 = (f32[3,4096]{1,0:T(4,128)S(1)}, f32[3,4096]{1,0:T(4,128)}, u32[]{:S(2)}) copy-start(f32[3,4096]{1,0:T(4,128)} %points_hbm.1) | copy-start | bytes 147460
  4.4 4.4 %collective-permute-start = (f32[16,128]{1,0:T(8,128)S(1)}, f32[16,128]{1,0:T(8,128)S(1)}, u32[]{:S(2)}, u32[]{:S(2)}) collective-permute-start(f32[16,128]{1,0:T(8,128)S(1)} %get-tuple-element.38.refs_0_), channel_id=1, source_target_pairs={{0,1},{1,0},{2,3},{3,2},{4,5},{5,4},{6,7},{7,6},{8,9},{9,8},{10,11... | collective-permute-start | bytes 24584 | tf_op jit(solution)/shard_map/ppermute | solution.py:608
  5.7 5.7 %copy-start.3 = (bf16[2,64,512]{2,1,0:T(8,128)(2,1)S(1)}, bf16[2,64,512]{2,1,0:T(8,128)(2,1)}, u32[]{:S(2)}) copy-start(bf16[2,64,512]{2,1,0:T(8,128)(2,1)} %constant.23.clone.octants_ref) | copy-start | bytes 393220
  8.8 2.6 %copy-start.1 = (bf16[2,64,128]{2,1,0:T(8,128)(2,1)S(1)}, bf16[2,64,128]{2,1,0:T(8,128)(2,1)}, u32[]{:S(2)}) copy-start(bf16[2,64,128]{2,1,0:T(8,128)(2,1)} %constant.24.clone.sink_ref) | copy-start | bytes 98308
  8.8 5.2 %collective-permute-start.1 = (f32[2,16,128]{2,1,0:T(8,128)S(1)}, f32[2,16,128]{2,1,0:T(8,128)S(1)}, u32[]{:S(2)}, u32[]{:S(2)}) collective-permute-start(f32[2,16,128]{2,1,0:T(8,128)S(1)} %pad_maximum_fusion.2.hold_ref.own_ref), channel_id=1, source_target_pairs={{0,2},{1,3},{2,0},{3,1},{4,6},{5,7},{6,4},{7,5},{8,10},{9,11},{10,... | collective-permute-start | bytes 49160 | tf_op jit(solution)/shard_map/ppermute | solution.py:608
  14.6 5.3 %collective-permute-start.2 = (f32[144,128]{1,0:T(8,128)S(1)}, f32[144,128]{1,0:T(8,128)S(1)}, u32[]{:S(2)}, u32[]{:S(2)}) collective-permute-start(f32[144,128]{1,0:T(8,128)S(1)} %get-tuple-element.46), channel_id=1, source_target_pairs={{0,4},{1,5},{2,6},{3,7},{4,0},{5,1},{6,2},{7,3},{8,12},{9,13},{10,... | collective-permute-start | bytes 221192 | tf_op jit(solution)/shard_map/ppermute | solution.py:608
  15.9 3.8 %collective-permute-start.4 = (f32[80,128]{1,0:T(8,128)S(1)}, f32[80,128]{1,0:T(8,128)S(1)}, u32[]{:S(2)}, u32[]{:S(2)}) collective-permute-start(f32[80,128]{1,0:T(8,128)S(1)} %get-tuple-element.45.refs_0_.own_ref), channel_id=1, source_target_pairs={{0,12},{1,13},{2,14},{3,15},{4,8},{5,9},{6,10},{7,11},{8,4},{9,5},... | collective-permute-start | bytes 122888 | tf_op jit(solution)/shard_map/ppermute | solution.py:608
  17.1 2.9 %collective-permute-start.3 = (f32[80,128]{1,0:T(8,128)S(1)}, f32[80,128]{1,0:T(8,128)S(1)}, u32[]{:S(2)}, u32[]{:S(2)}) collective-permute-start(f32[80,128]{1,0:T(8,128)S(1)} %get-tuple-element.45.refs_0_.own_ref), channel_id=1, source_target_pairs={{0,8},{1,9},{2,10},{3,11},{4,12},{5,13},{6,14},{7,15},{8,0},{9,1},... | collective-permute-start | bytes 122888 | tf_op jit(solution)/shard_map/ppermute | solution.py:608
  20.5 5.9 %collective-permute-start.5 = (f32[144,128]{1,0:T(8,128)S(1)}, f32[144,128]{1,0:T(8,128)S(1)}, u32[]{:S(2)}, u32[]{:S(2)}) collective-permute-start(f32[144,128]{1,0:T(8,128)S(1)} %get-tuple-element.48), channel_id=1, source_target_pairs={{0,16},{1,17},{2,18},{3,19},{4,20},{5,21},{6,22},{7,23},{8,24},{9,... | collective-permute-start | bytes 221192 | tf_op jit(solution)/shard_map/ppermute | solution.py:608
  26.4 23.3 %copy-start = (bf16[14,256,128]{2,1,0:T(8,128)(2,1)S(1)}, bf16[14,256,128]{2,1,0:T(8,128)(2,1)}, u32[]{:S(2)}) copy-start(bf16[14,256,128]{2,1,0:T(8,128)(2,1)} %constant.26.clone.coupling_ref) | copy-start | bytes 2752516
  26.4 17.8 %collective-permute-start.6 = (f32[32,1280]{1,0:T(8,128)S(1)}, f32[32,1280]{1,0:T(8,128)S(1)}, u32[]{:S(2)}, u32[]{:S(2)}) collective-permute-start(f32[32,1280]{1,0:T(8,128)S(1)} %get-tuple-element.50), channel_id=1, source_target_pairs={{0,1},{1,0},{2,3},{3,2},{4,5},{5,4},{6,7},{7,6},{8,9},{9,8},{10,11... | collective-permute-start | bytes 491528 | tf_op jit(solution)/shard_map/ppermute | solution.py:608
  26.6 17.7 %collective-permute-start.7 = (f32[32,1280]{1,0:T(8,128)S(1)}, f32[32,1280]{1,0:T(8,128)S(1)}, u32[]{:S(2)}, u32[]{:S(2)}) collective-permute-start(f32[32,1280]{1,0:T(8,128)S(1)} %get-tuple-element.52), channel_id=1, source_target_pairs={{1,2},{2,1},{3,4},{4,3},{5,6},{6,5},{7,8},{8,7},{9,10},{10,9},{11,... | collective-permute-start | bytes 491528 | tf_op jit(solution)/shard_map/ppermute | solution.py:614
  32.9 2.7 %collective-permute-start.8 = (f32[2,16,128]{2,1,0:T(8,128)S(1)}, f32[2,16,128]{2,1,0:T(8,128)S(1)}, u32[]{:S(2)}, u32[]{:S(2)}) collective-permute-start(f32[2,16,128]{2,1,0:T(8,128)S(1)} %pad_maximum_fusion.3.refs_0_), channel_id=1, source_target_pairs={{0,32},{1,33},{2,34},{3,35},{4,36},{5,37},{6,38},{7,39},{8,40},{9,... | collective-permute-start | bytes 49160 | tf_op jit(solution)/shard_map/ppermute | solution.py:608
  35.6 9.8 %collective-permute-start.10 = (f32[4,16,128]{2,1,0:T(8,128)S(1)}, f32[4,16,128]{2,1,0:T(8,128)S(1)}, u32[]{:S(2)}, u32[]{:S(2)}) collective-permute-start(f32[4,16,128]{2,1,0:T(8,128)S(1)} %pad_maximum_fusion.1.refs_0_), channel_id=1, source_target_pairs={{0,64},{1,65},{2,66},{3,67},{4,68},{5,69},{6,70},{7,71},{8,72},{9,... | collective-permute-start | bytes 98312 | tf_op jit(solution)/shard_map/ppermute | solution.py:608
  38.6 11.1 %copy-start.4 = (bf16[4,256,256]{2,1,0:T(8,128)(2,1)S(1)}, bf16[4,256,256]{2,1,0:T(8,128)(2,1)}, u32[]{:S(2)}) copy-start(bf16[4,256,256]{2,1,0:T(8,128)(2,1)} %constant.25.clone.layers_ref) | copy-start | bytes 1572868
  38.6 11.1 %collective-permute-start.9 = (f32[128,128]{1,0:T(8,128)S(1)}, f32[128,128]{1,0:T(8,128)S(1)}, u32[]{:S(2)}, u32[]{:S(2)}) collective-permute-start(f32[128,128]{1,0:T(8,128)S(1)} %get-tuple-element.58), channel_id=1, source_target_pairs={{16,32},{17,33},{18,34},{19,35},{20,36},{21,37},{22,38},{23,39},{2... | collective-permute-start | bytes 196616 | tf_op jit(solution)/shard_map/ppermute | solution.py:614
  45.4 8.4 %collective-permute-start.11 = (f32[8,16,128]{2,1,0:T(8,128)S(1)}, f32[8,16,128]{2,1,0:T(8,128)S(1)}, u32[]{:S(2)}, u32[]{:S(2)}) collective-permute-start(f32[8,16,128]{2,1,0:T(8,128)S(1)} %pad_maximum_fusion.refs_5_.boxes_ref), channel_id=1, source_target_pairs={{0,128},{1,129},{2,130},{3,131},{4,132},{5,133},{6,134},{7,135},{8... | collective-permute-start | bytes 196616 | tf_op jit(solution)/shard_map/ppermute | solution.py:608
  49.7 4.1 %copy-start.5 = (bf16[6,256,128]{2,1,0:T(8,128)(2,1)S(1)}, bf16[6,256,128]{2,1,0:T(8,128)(2,1)}, u32[]{:S(2)}) copy-start(bf16[6,256,128]{2,1,0:T(8,128)(2,1)} %constant.27.clone.coupling_ref) | copy-start | bytes 1179652
